TPU v7x, 256 devices: a whole 4x4x8 slice. The times are simulated.
256 devices in a mesh: tile: 64 (over y, z, core), var: 4 (over x).
Axes of the slice: x: 4, y: 4, z: 8, core: 2. Of those that a mesh axis runs over, the one named last changes fastest.
Arguments:
- mesh_latents: bfloat16 [256, 262144], P('var', 'tile'), may hold values from -6 to 6
- edge_idx: int32 [3, 64, 8192], P(None, None, 'tile'), may hold values from 0 to 262143, as said below
- edge_weight: float32 [3, 64, 8192], P(None, None, 'tile'), may hold values from 0.2 to 1
- conv1_weight: bfloat16 [9, 512, 256], P(None, 'var'), may hold values from -0.125 to 0.125
- conv1_bias: float32 [512], P('var'), may hold values from -3 to 3
- conv2_weight: bfloat16 [9, 24, 512], P(None, None, 'var'), may hold values from -0.09375 to 0.09375
- conv2_bias: float32 [24], P('var'), may hold values from -3 to 3
Outputs:
- archive: float32 [24, 64, 8192], P('var', 'tile')
Inputs may be any that keep to these rules, and one draw needn't show every extreme that they name: `edge_idx`: A grid cell in longitude column j has all three mesh nodes within 64 nodes, counted cyclically over 262144, of partition (j // 128), the nodes (j // 128) * 4096 to (j // 128 + 1) * 4096 - 1; the reach 64 is met on both sides.
All inputs are finite; a program needn't handle non-finite values.
Results may differ from a plain program's by a relative error of at most 0.0033.
Values may be sent and summed in bfloat16 or wider, within the bound.
No kernel may reach another device: no remote copies, remote signals or barrier semaphores. Data moves between devices by JAX's collectives and lax.ppermute only.
A program may use at most 320 MiB of HBM per device.

v0:
```python
import jax
import jax.numpy as jnp
from jax import lax
from jax.sharding import PartitionSpec as P


def extended(value, sides, width):
    for axis, dim in sides:
        size, length = (lax.axis_size(axis), value.shape[dim])
        up = [(i, (i + 1) % size) for i in range(size)]
        down = [(j, i) for i, j in up]
        last = lax.slice_in_dim(value, length - width, length, axis=dim)
        leading = lax.slice_in_dim(value, 0, width, axis=dim)
        before = lax.ppermute(last, axis, up)
        after = lax.ppermute(leading, axis, down)
        value = jnp.concatenate([before, value, after], axis=dim)
    return value


def sweep(padded, weight, out_cols):
    lat_rows = padded.shape[1] - 2
    summed = None
    for row_off in range(3):
        for col_off in range(3):
            term_part = jnp.einsum(
                "oc,clw->olw",
                weight[3 * row_off + col_off],
                padded[:, row_off : row_off + lat_rows, col_off : col_off + out_cols],
                preferred_element_type=jnp.float32,
            )
            summed = term_part if summed is None else summed + term_part
    return summed


def body(mesh_latents, edge_idx, edge_weight, conv1_weight, conv1_bias, conv2_weight, conv2_bias):
    tile_at = lax.axis_index("tile")
    tile_count = lax.axis_size("tile")
    mesh_dev = mesh_latents.shape[1]
    lat_rows = edge_idx.shape[1]
    lon_dev = edge_idx.shape[2]
    stride = mesh_dev // lon_dev
    margin = 2 * stride
    near_index = (edge_idx - tile_at * mesh_dev + margin) % (mesh_dev * tile_count)
    span = 8
    blocks = lon_dev // span
    window = span * stride + 2 * margin
    block_idx = near_index.reshape(3, lat_rows, blocks, span).transpose(2, 0, 1, 3)
    block_wts = edge_weight.reshape(3, lat_rows, blocks, span).transpose(2, 0, 1, 3)
    starts = jnp.arange(blocks, dtype=jnp.int32) * (span * stride)
    extra = 1
    out_cols = lon_dev + 2 * extra - 2
    source = extended(
        lax.all_gather(mesh_latents, "var", axis=0, tiled=True), (("tile", 1),), margin
    )
    channels = source.shape[0]
    nodes = jnp.arange(window, dtype=jnp.int32)[:, None]

    def one_block(packed):
        start, idx_block, wts_block = packed
        part_src = lax.dynamic_slice_in_dim(source, start, window, 1).astype(jnp.float32)
        table = jnp.zeros((window, lat_rows * span), jnp.float32)
        for k in range(3):
            rel = (idx_block[k] - start).reshape(1, lat_rows * span)
            table = table + jnp.where(nodes == rel, wts_block[k].reshape(1, lat_rows * span), 0.0)
        return jnp.dot(
            part_src, table, precision=lax.Precision.HIGHEST, preferred_element_type=jnp.float32
        )

    result = lax.map(one_block, (starts, block_idx, block_wts))
    result = result.reshape(blocks, channels, lat_rows, span).transpose(1, 2, 0, 3)
    bordered = extended(
        result.reshape(channels, lat_rows, lon_dev).astype(jnp.bfloat16), (("tile", 2),), extra
    )
    padded = jnp.pad(bordered, ((0, 0), (1, 1), (0, 0)))
    pre_act = sweep(padded, conv1_weight, out_cols)
    hidden = jax.nn.silu(pre_act + conv1_bias[:, None, None]).astype(jnp.bfloat16)
    hidden = extended(hidden, (("tile", 2),), 1)
    hid_pad = jnp.pad(hidden, ((0, 0), (1, 1), (0, 0)))
    fields = lax.psum_scatter(
        sweep(hid_pad, conv2_weight, lon_dev), "var", scatter_dimension=0, tiled=True
    )
    fields = fields + conv2_bias[:, None, None]
    return lax.all_to_all(fields, "tile", split_axis=1, concat_axis=2, tiled=True)


def solution(mesh):
    return jax.shard_map(
        body,
        mesh=mesh,
        in_specs=(
            P("var", "tile"),
            P(None, None, "tile"),
            P(None, None, "tile"),
            P(None, "var", None),
            P("var"),
            P(None, None, "var"),
            P("var"),
        ),
        out_specs=P("var", "tile", None),
        check_vma=False,
    )
```

profile of v0, /device:TPU:1, one launch (start us, length us, event | category | flops | bytes accessed | tf_op | source)
XLA Modules:
  0.0 295.2 jit_solution(1656604217625428345)
XLA Ops:
  8.4 37.9 %all-gather.2.cloned.1.call-done = bf16[256,4096]{1,0:T(8,128)(2,1)} async-done(((bf16[64,4096]{1,0:T(8,128)(2,1)}), bf16[256,4096]{1,0:T(8,128)(2,1)}) %all-gather.2.cloned.1.call-update) | async-done | bytes 2097168 | tf_op jit(solution)/shard_map/all_gather | solution.py:53
  51.2 2.6 collective-permute-done
  53.8 4.5 %concatenate.21 = bf16[256,4224]{1,0:T(8,128)(2,1)S(1)} concatenate(bf16[256,64]{1,0:T(8,128)(2,1)S(1)} %collective-permute-done, bf16[256,4096]{1,0:T(8,128)(2,1)} %all-gather.2.cloned.1.call-done, bf16[256,64]{1,0:T(8,128)(2,1)S(1)} %collective-permute-done.1), dimensions={1} | concatenate | bytes 4325376 | tf_op jit(solution)/shard_map/concatenate | solution.py:16
  58.3 109.5 %while.12 = (s32[]{:T(128)}, bf16[16,256,512]{1,2,0:T(8,128)(2,1)}, s32[16]{0:T(128)S(1)}, bf16[256,4224]{1,0:T(8,128)(2,1)S(1)}, s32[16,3,64,8]{2,3,0,1:T(8,128...) while((s32[]{:T(128)}, bf16[16,256,512]{1,2,0:T(8,128)(2,1)}, ...), condition=%wide.region_1.2_spmd.clone.clone, body=%wide.region_0.1_spmd.clone.clone.sunk | while | flops 605554176 | bytes 819427 | solution.py:69
  63.5 1.7 fusion.142
  77.2 1.7 fusion.142
  90.8 1.7 fusion.142
  97.7 1.7 fusion.142
  104.5 1.7 fusion.142
  111.4 1.7 fusion.142
  118.2 1.7 fusion.142
  125.1 1.7 fusion.142
  131.9 1.7 fusion.142
  138.8 1.7 fusion.142
  159.3 1.7 fusion.142
  166.1 1.7 fusion.142
  167.8 2.9 copy_bitcast_fusion
  170.9 6.3 %collective-permute-start.3 = (bf16[256,64,1]{0,2,1:T(2,128)(2,1)S(1)}, bf16[256,64,1]{0,2,1:T(2,128)(2,1)S(1)}, u32[]{:S(2)}, u32[]{:S(2)}) collective-permute-start(bf16[256,64,1]{0,2,1:T(2,128)(2,1)S(1)} %get-tuple-element.121), channel_id=1, source_target_pairs={{4,0},{8,4},{12,8},{16,12},{20,16},{24,20},{28,24},{32,28},{36,32}... | collective-permute-start | bytes 98312 | tf_op jit(solution)/shard_map/ppermute | solution.py:15
  177.3 3.2 %fusion.93 = f32[64,128,128]{2,1,0:T(8,128)} fusion(bf16[9,128,256]{2,1,0:T(8,128)(2,1)S(1)} %copy-done.1, bf16[16,256,512]{1,2,0:T(8,128)(2,1)S(1)} %copy-done), kind=kOutput, calls=%fused_computation.109 | convolution fusion | flops 536870912 | bytes 8454144 | tf_op jit(solution)/shard_map/oc,clw->olw/dot_general | solution.py:25
  180.5 2.1 fusion.23
  182.6 3.2 %fusion.27 = f32[64,128,128]{2,1,0:T(8,128)} fusion(bf16[256,66,130]{0,2,1:T(8,128)(2,1)S(1)} %fusion.23, bf16[9,128,256]{2,1,0:T(8,128)(2,1)S(1)} %copy-done.1), kind=kOutput, calls=%fused_computation.43 | convolution fusion | flops 536870912 | bytes 8454144 | tf_op jit(solution)/shard_map/oc,clw->olw/dot_general | solution.py:25
  185.8 3.2 %fusion.29 = f32[64,128,128]{2,1,0:T(8,128)} fusion(bf16[256,66,130]{0,2,1:T(8,128)(2,1)S(1)} %fusion.23, bf16[9,128,256]{2,1,0:T(8,128)(2,1)S(1)} %copy-done.1), kind=kOutput, calls=%fused_computation.45 | convolution fusion | flops 536870912 | bytes 8454144 | tf_op jit(solution)/shard_map/oc,clw->olw/dot_general | solution.py:25
  189.1 3.3 %fusion.35 = f32[64,128,128]{2,1,0:T(8,128)} fusion(bf16[256,66,130]{0,2,1:T(8,128)(2,1)S(1)} %fusion.23, bf16[9,128,256]{2,1,0:T(8,128)(2,1)S(1)} %copy-done.1), kind=kOutput, calls=%fused_computation.53 | convolution fusion | flops 536870912 | bytes 8454144 | tf_op jit(solution)/shard_map/oc,clw->olw/dot_general | solution.py:25
  192.3 3.2 %fusion.37 = f32[64,128,128]{2,1,0:T(8,128)} fusion(bf16[256,66,130]{0,2,1:T(8,128)(2,1)S(1)} %fusion.23, bf16[9,128,256]{2,1,0:T(8,128)(2,1)S(1)} %copy-done.1), kind=kOutput, calls=%fused_computation.55 | convolution fusion | flops 536870912 | bytes 8454144 | tf_op jit(solution)/shard_map/oc,clw->olw/dot_general | solution.py:25
  195.5 3.2 %fusion.39 = f32[64,128,128]{2,1,0:T(8,128)} fusion(bf16[256,66,130]{0,2,1:T(8,128)(2,1)S(1)} %fusion.23, bf16[9,128,256]{2,1,0:T(8,128)(2,1)S(1)} %copy-done.1), kind=kOutput, calls=%fused_computation.57 | convolution fusion | flops 536870912 | bytes 8454144 | tf_op jit(solution)/shard_map/oc,clw->olw/dot_general | solution.py:25
  198.8 3.2 %fusion.31 = f32[64,128,128]{2,1,0:T(8,128)} fusion(bf16[256,64,1]{0,2,1:T(2,128)(2,1)S(1)} %collective-permute-done.3, bf16[256,64,128]{0,2,1:T(8,128)(2,1)S(1)} %copy_bitcast_fusion, bf16[9,128,256]{2,1,0:T(8,128)(2,1)S(1)} %copy-done.1), kind=kOutput, calls=%fused_computation.48 | convolution fusion | flops 545259520 | bytes 8519680 | tf_op jit(solution)/shard_map/oc,clw->olw/dot_general | solution.py:25
  202.0 3.2 %fusion.33 = f32[64,128,128]{2,1,0:T(8,128)} fusion(bf16[256,64,128]{0,2,1:T(8,128)(2,1)S(1)} %copy_bitcast_fusion, bf16[256,64,1]{0,2,1:T(2,128)(2,1)S(1)} %collective-permute-done.2, bf16[9,128,256]{2,1,0:T(8,128)(2,1)S(1)} %copy-done.1), kind=kOutput, calls=%fused_computation.51 | convolution fusion | flops 545259520 | bytes 8519680 | tf_op jit(solution)/shard_map/oc,clw->olw/dot_general | solution.py:25
  205.2 12.3 %fusion.44 = bf16[128,64,128]{0,2,1:T(8,128)(2,1)S(1)} fusion(f32[64,128,128]{2,1,0:T(8,128)} %fusion.27, f32[64,128,128]{2,1,0:T(8,128)} %fusion.29, f32[64,128,128]{2,1,0:T(8,128)} %fusion.31, f32[64,128,128]{2,1,0:T(8,128)} %fusion.93, f32[64,128,128]{2,1,0:T(8,128)} %fusion.33, f32[64,128,128]{2,1,0:T(8,128)} %fusion.35, f32[64,128,128]{2,1,0:T(8,128)} %fusion.39, ...), kind=kOutput, calls=%fused_computation.66 | convolution fusion | flops 551550976 | bytes 39911936 | tf_op jit(solution)/shard_map/oc,clw->olw/dot_general | solution.py:25
  217.7 5.3 %collective-permute-start.5 = (bf16[128,64,1]{0,2,1:T(2,128)(2,1)S(1)}, bf16[128,64,1]{0,2,1:T(2,128)(2,1)S(1)}, u32[]{:S(2)}, u32[]{:S(2)}) collective-permute-start(bf16[128,64,1]{0,2,1:T(2,128)(2,1)S(1)} %get-tuple-element.123), channel_id=1, source_target_pairs={{4,0},{8,4},{12,8},{16,12},{20,16},{24,20},{28,24},{32,28},{36,32}... | collective-permute-start | bytes 49160 | tf_op jit(solution)/shard_map/ppermute | solution.py:15
  224.2 2.3 fusion.49
  237.3 25.5 %reduce-scatter.2.cloned.1.call-done = f32[6,64,128]{2,1,0:T(8,128)} async-done(((f32[24,64,128]{2,1,0:T(8,128)}), f32[6,64,128]{2,1,0:T(8,128)}) %reduce-scatter.2.cloned.1.call-update) | async-done | bytes 196624 | tf_op jit(solution)/shard_map/reduce_scatter | solution.py:79
  263.9 23.6 %all_to_all.12 = f32[6,64,128]{2,0,1:T(8,128)S(1)} all-to-all(f32[6,64,128]{2,0,1:T(8,128)S(1)} %copy.67), channel_id=1, replica_groups=mesh['tile'=64,'var'=4] {'tile'}, dimensions={1} | all-to-all | bytes 393216 | tf_op jit(solution)/shard_map/all_to_all | solution.py:83
  (320 shorter events, 77.1 us)
Async XLA Ops:
  6.5 39.8 %all-gather.2.cloned.1.call-start = ((), (), s32[]{:S(2)}) async-start(), calls=%async_computation.2 | async-start | bytes 2621440 | tf_op jit(solution)/shard_map/all_gather | solution.py:53
  7.3 255.5 %reduce-scatter.2.cloned.1.call-start = ((), (), s32[]{:S(2)}) async-start(), calls=%async_computation.3 | async-start | bytes 983040 | tf_op jit(solution)/shard_map/reduce_scatter | solution.py:79
  47.3 3.9 %collective-permute-start.1 = (bf16[256,64]{1,0:T(8,128)(2,1)S(1)}, bf16[256,64]{1,0:T(8,128)(2,1)S(1)}, u32[]{:S(2)}, u32[]{:S(2)}) collective-permute-start(bf16[256,64]{1,0:T(8,128)(2,1)S(1)} %get-tuple-element.124), channel_id=1, source_target_pairs={{4,0},{8,4},{12,8},{16,12},{20,16},{24,20},{28,24},{32,28},{36,32}... | collective-permute-start | bytes 98312 | tf_op jit(solution)/shard_map/ppermute | solution.py:15
  48.1 5.7 %collective-permute-start = (bf16[256,64]{1,0:T(8,128)(2,1)S(1)}, bf16[256,64]{1,0:T(8,128)(2,1)S(1)}, u32[]{:S(2)}, u32[]{:S(2)}) collective-permute-start(bf16[256,64]{1,0:T(8,128)(2,1)S(1)} %get-tuple-element.125), channel_id=1, source_target_pairs={{0,4},{4,8},{8,12},{12,16},{16,20},{20,24},{24,28},{28,32},{32,36}... | collective-permute-start | bytes 98312 | tf_op jit(solution)/shard_map/ppermute | solution.py:14
  167.8 9.4 %copy-start = (bf16[16,256,512]{1,2,0:T(8,128)(2,1)S(1)}, bf16[16,256,512]{1,2,0:T(8,128)(2,1)}, u32[]{:S(2)}) copy-start(bf16[16,256,512]{1,2,0:T(8,128)(2,1)} %get-tuple-element.48) | copy-start | bytes 12582916
  167.8 9.4 %copy-start.1 = (bf16[9,128,256]{2,1,0:T(8,128)(2,1)S(1)}, bf16[9,128,256]{2,1,0:T(8,128)(2,1)}, u32[]{:S(2)}) copy-start(bf16[9,128,256]{2,1,0:T(8,128)(2,1)} %param.12) | copy-start | bytes 1769476
  170.8 9.7 %collective-permute-start.2 = (bf16[256,64,1]{0,2,1:T(2,128)(2,1)S(1)}, bf16[256,64,1]{0,2,1:T(2,128)(2,1)S(1)}, u32[]{:S(2)}, u32[]{:S(2)}) collective-permute-start(bf16[256,64,1]{0,2,1:T(2,128)(2,1)S(1)} %get-tuple-element.120), channel_id=1, source_target_pairs={{0,4},{4,8},{8,12},{12,16},{16,20},{20,24},{24,28},{28,32},{32,36}... | collective-permute-start | bytes 98312 | tf_op jit(solution)/shard_map/ppermute | solution.py:14
  170.9 9.6 %collective-permute-start.3 = (bf16[256,64,1]{0,2,1:T(2,128)(2,1)S(1)}, bf16[256,64,1]{0,2,1:T(2,128)(2,1)S(1)}, u32[]{:S(2)}, u32[]{:S(2)}) collective-permute-start(bf16[256,64,1]{0,2,1:T(2,128)(2,1)S(1)} %get-tuple-element.121), channel_id=1, source_target_pairs={{4,0},{8,4},{12,8},{16,12},{20,16},{24,20},{28,24},{32,28},{36,32}... | collective-permute-start | bytes 98312 | tf_op jit(solution)/shard_map/ppermute | solution.py:15
  202.0 3.2 %copy-start.4 = (f32[128]{0:T(128)S(1)}, f32[128]{0:T(128)}, u32[]{:S(2)}) copy-start(f32[128]{0:T(128)} %param.13) | copy-start | bytes 1540
  205.2 17.7 %copy-start.2 = (bf16[9,24,128]{2,1,0:T(8,128)(2,1)S(1)}, bf16[9,24,128]{2,1,0:T(8,128)(2,1)}, u32[]{:S(2)}) copy-start(bf16[9,24,128]{2,1,0:T(8,128)(2,1)} %param.14) | copy-start | bytes 165892
  217.6 6.6 %collective-permute-start.4 = (bf16[128,64,1]{0,2,1:T(2,128)(2,1)S(1)}, bf16[128,64,1]{0,2,1:T(2,128)(2,1)S(1)}, u32[]{:S(2)}, u32[]{:S(2)}) collective-permute-start(bf16[128,64,1]{0,2,1:T(2,128)(2,1)S(1)} %get-tuple-element.122), channel_id=1, source_target_pairs={{0,4},{4,8},{8,12},{12,16},{16,20},{20,24},{24,28},{28,32},{32,36}... | collective-permute-start | bytes 49160 | tf_op jit(solution)/shard_map/ppermute | solution.py:14
  217.7 6.5 %collective-permute-start.5 = (bf16[128,64,1]{0,2,1:T(2,128)(2,1)S(1)}, bf16[128,64,1]{0,2,1:T(2,128)(2,1)S(1)}, u32[]{:S(2)}, u32[]{:S(2)}) collective-permute-start(bf16[128,64,1]{0,2,1:T(2,128)(2,1)S(1)} %get-tuple-element.123), channel_id=1, source_target_pairs={{4,0},{8,4},{12,8},{16,12},{20,16},{24,20},{28,24},{32,28},{36,32}... | collective-permute-start | bytes 49160 | tf_op jit(solution)/shard_map/ppermute | solution.py:15
  235.0 27.8 %copy-start.3 = (f32[6]{0:T(128)S(1)}, f32[6]{0:T(128)}, u32[]{:S(2)}) copy-start(f32[6]{0:T(128)} %param.15) | copy-start | bytes 76
Sparse Core Ops, SparseCore 0:
  9.2 37.1 all-gather.1
  237.4 25.3 reduce-scatter.1
where the time goes:
time: 296 us; the launch traced here: 295 us
  matrix products  76.1 us (26%)
  waiting for transfers between devices  67.6 us (23%)
  local copies, waits for them, and re-layouts  40.2 us (14%)
  loops' own time  33.1 us (11%)
  other arithmetic  27.3 us (9%)
  blocking collectives  23.6 us (8%)
  starting transfers between devices  13.8 us (5%)
  between operations  13.6 us (5%)
    dot_general x18, matrix products, sweep(): jnp.einsum('oc,clw->olw', weight[3 * row_off + col_off], padded[:, row_of...  49 us
    all_gather x1, waiting for transfers between devices, body(): lax.all_gather(mesh_latents, 'var', axis=0, tiled=True)  37.9 us
    another operation x1, loops' own time, body(): result = lax.map(one_block, (starts, block_idx, block_wts))  33.1 us
    dot_general x16, matrix products, one_block(): jnp.dot(part_src, table, precision=lax.Precision.HIGHEST, preferred_eleme...  27.1 us
    reduce_scatter x1, waiting for transfers between devices, body(): lax.psum_scatter(sweep(hid_pad, conv2_weight, lon_dev), 'var', scatter_di...  25.5 us
    all_to_all x1, blocking collectives, body(): lax.all_to_all(fields, 'tile', split_axis=1, concat_axis=2, tiled=True)  23.6 us
    sub x32, other arithmetic, one_block(): rel = (idx_block[k] - start).reshape(1, lat_rows * span)  21.8 us
    ppermute x3, starting transfers between devices, extended(): after = lax.ppermute(leading, axis, down)  12.4 us
  transfers between devices with their start and end apart: 8, of which 4 were waited for; matrix products, arithmetic and copies ran while one was open for 2% of the time, Pallas kernels for 0%

commit v1 on v0

v1 whole, which is shorter than its diff:
```python
import jax
import jax.numpy as jnp
from jax import lax
from jax.experimental import pallas as pl
from jax.experimental.pallas import tpu as pltpu
from jax.sharding import PartitionSpec as P


GRP = 8


def prep(edge_idx, edge_weight, tile_at, mesh_dev, nmesh, rim):
    u = jnp.mod(edge_idx - tile_at * mesh_dev + rim, nmesh)
    u = u.transpose(0, 2, 1).reshape(3, -1, 128)
    wt = edge_weight.transpose(0, 2, 1).reshape(3, -1, 128)
    lo = jnp.min(u, axis=(0, 2)) // 64
    hi = jnp.max(u, axis=(0, 2)) // 64
    return u, wt, lo, hi

def decode_kernel(lo_ref, hi_ref, u_ref, wt_ref, lat_ref, left_ref, right_ref, out_ref, first_ref, last_ref, lats, parts, accs):
    ch, nodes = lat_ref.shape
    rim = left_ref.shape[1]
    ext = nodes + 2 * rim
    nblk = u_ref.shape[1]
    per = nblk // 4
    width = lats.shape[2]
    bf = lat_ref.dtype
    main = lat_ref[...]
    zeros = lambda n: jnp.zeros((ch, n), bf)
    lats[0] = jnp.concatenate([left_ref[...], main, right_ref[...], zeros(width - ext)], axis=1)
    lats[1] = jnp.concatenate([main, right_ref[...], zeros(width - ext + rim)], axis=1)

    u0, u1, u2 = u_ref[0], u_ref[1], u_ref[2]
    w0, w1, w2 = wt_ref[0], wt_ref[1], wt_ref[2]
    w0 = w0 + jnp.where(u1 == u0, w1, 0.0) + jnp.where(u2 == u0, w2, 0.0)
    w1 = w1 + jnp.where(u2 == u1, w2, 0.0)
    for k, w in enumerate((w0, w1, w2)):
        top = w.astype(bf).astype(jnp.float32)
        parts[k] = top
        parts[3 + k] = w - top

    node = lax.broadcasted_iota(jnp.int32, (256, 128), 0).astype(jnp.float32).astype(bf)

    def window(b, at):
        src = lats[at & 1, :, pl.ds(pl.multiple_of((at >> 1) * 128, 128), 256)]
        tops = jnp.zeros((256, 128), bf)
        rests = jnp.zeros((256, 128), bf)
        for k in (2, 1, 0):
            rel = (u_ref[k, pl.ds(b, 1), :] - at * 64).astype(jnp.float32).astype(bf)
            here = node == rel
            tops = jnp.where(here, parts[k, pl.ds(b, 1), :].astype(bf), tops)
            rests = jnp.where(here, parts[3 + k, pl.ds(b, 1), :].astype(bf), rests)
        table = jnp.concatenate([tops, rests], axis=1)
        both = jnp.dot(src, table, preferred_element_type=jnp.float32)
        return both[:, :128] + both[:, 128:]

    def group(g, _):
        more = jnp.int32(0)
        for j in range(GRP):
            b = g * GRP + j
            at = lo_ref[b]
            accs[j] = window(b, at)
            more = more + jnp.where(hi_ref[b] - at >= 4, 1, 0)

        @pl.when(more > 0)
        def _():
            for j in range(GRP):
                b = g * GRP + j
                at = lo_ref[b]

                @pl.loop(1, ((hi_ref[b] - at) >> 2) + 1)
                def _(step):
                    accs[j] += window(b, at + 4 * step)

        for j in range(GRP):
            b = g * GRP + j
            val = accs[j].astype(out_ref.dtype)
            piece, at = b // per, b % per
            out_ref[piece, :, pl.ds(pl.multiple_of(at * 128 + 128, 128), 128)] = val
            if j == 0:
                @pl.when(jnp.logical_and(at == 0, piece > 0))
                def _():
                    out_ref[piece - 1, :, (per + 1) * 128:] = val
                @pl.when(b == 0)
                def _():
                    first_ref[...] = val
            if j == GRP - 1:
                @pl.when(jnp.logical_and(at == per - 1, piece < 3))
                def _():
                    out_ref[piece + 1, :, :128] = val
                @pl.when(b == nblk - 1)
                def _():
                    last_ref[...] = val
        return 0
    lax.fori_loop(0, nblk // GRP, group, 0)
    out_ref[0, :, :128] = zeros(128)
    out_ref[3, :, (per + 1) * 128:] = zeros(128)

def decode(u, wt, lo, hi, lat, left, right):
    ch, nodes = lat.shape
    nblk = u.shape[1]
    smem = pl.BlockSpec(memory_space=pltpu.SMEM)
    vmem = pl.BlockSpec(memory_space=pltpu.VMEM)
    return pl.pallas_call(
        decode_kernel,
        out_shape=(
            jax.ShapeDtypeStruct((4, ch, (nblk // 4 + 2) * 128), lat.dtype),
            jax.ShapeDtypeStruct((ch, 128), lat.dtype),
            jax.ShapeDtypeStruct((ch, 128), lat.dtype),
        ),
        in_specs=[smem] * 2 + [vmem] * 5,
        out_specs=(vmem,) * 3,
        scratch_shapes=[pltpu.VMEM((2, ch, nodes + 384), lat.dtype), pltpu.VMEM((6, nblk, 128), jnp.float32), pltpu.VMEM((GRP, ch, 128), jnp.float32)],
        compiler_params=pltpu.CompilerParams(vmem_limit_bytes=40 << 20),
    )(lo, hi, u, wt, lat, left, right)


def conv_kernel(at_ref, grid_ref, h0, h1, h2, h3, *rest):
    weights = rest[:8]
    out_ref, shifted, mix, taps, rows = rest[8:]
    ch, cells = grid_ref.shape
    part = h0.shape[0]
    bf = grid_ref.dtype
    halos = (h0, h1, h2, h3)
    at = at_ref[0]
    lat = 64
    hid_cells = cells - 2 * lat
    out_cells = cells - 4 * lat

    place = lax.broadcasted_iota(jnp.int32, (1, cells), 1) % lat
    x = shifted
    x[1] = grid_ref[...]

    @pl.when(at == 0)
    def _():
        for d in range(4):
            s = (4 - d) % 4
            x[1, s * part:(s + 1) * part, :128] = halos[d][...]

    @pl.when(at == 3)
    def _():
        for d in range(4):
            s = 3 - d
            x[1, s * part:(s + 1) * part, cells - 128:] = halos[d][...]

    step = 64
    for c0 in range(0, ch, step):
        rs = slice(c0, c0 + step)
        v = x[1, rs, :].astype(jnp.float32)
        up = jnp.where(place == 0, 0.0, pltpu.roll(v, 1, 1))
        down = jnp.where(place == lat - 1, 0.0, pltpu.roll(v, cells - 1, 1))
        x[0, rs, :] = up.astype(bf)
        x[2, rs, :] = down.astype(bf)
        for r, u in enumerate((up, v, down)):
            x[3 + r, rs, :] = pltpu.roll(u, cells - lat, 1).astype(bf)

    last = jnp.concatenate([w[:, 9].reshape(64, 256) for w in weights], axis=0).astype(jnp.float32)
    mix[...] = last.T[:216].astype(bf)
    bias = last[:, 216:217] + last[:, 217:218] + last[:, 218:219]

    def tile(start, width):
        kernel_w = jnp.concatenate(
            [jnp.concatenate([w[:, k].reshape(64, 256) for w in weights], axis=0) for k in range(9)], axis=1)
        cols = []
        for r in range(3):
            for s in range(3):
                src, off = (3 + r, 0) if s == 1 else (r, s * lat)
                cols.append(x[src, :, pl.ds(start + off, width)])
        pre = jnp.dot(kernel_w, jnp.concatenate(cols, axis=0), preferred_element_type=jnp.float32) + bias
        hidden = pre * (0.5 * jnp.tanh(0.5 * pre) + 0.5)
        taps[:, pl.ds(start, width)] = jnp.dot(mix[...], hidden.astype(bf), preferred_element_type=jnp.float32)

    @pl.loop(0, hid_cells // 256)
    def _(n):
        tile(pl.multiple_of(n * 256, 256), 256)

    if hid_cells % 256:
        tile(hid_cells // 256 * 256, hid_cells % 256)

    def total(r):
        y = [taps[(3 * r + s) * 24:(3 * r + s + 1) * 24, :] for s in range(3)]
        mid = pltpu.roll(y[1], taps.shape[1] - lat, 1)
        return y[0][:, :out_cells] + mid[:, :out_cells] + y[2][:, 2 * lat:2 * lat + out_cells]

    spot = place[:, :out_cells]
    full = jnp.where(spot == 0, 0.0, pltpu.roll(total(0), 1, 1))
    full = full + total(1)
    full = full + jnp.where(spot == lat - 1, 0.0, pltpu.roll(total(2), out_cells - 1, 1))

    rows[...] = jnp.zeros_like(rows)
    for l in range(32):
        col = full[:, l * lat:(l + 1) * lat]
        for g in range(4):
            rows[pl.ds(g * 256 + l, 6, stride=32), :] = col[g * 6:g * 6 + 6]
    turned = rows[...].T
    for g in range(4):
        for h in range(2):
            out_ref[g * lat:(g + 1) * lat, h, :] = turned[:, g * 256 + h * 128:g * 256 + h * 128 + 128]

def convolve(at, grid, halos, weights):
    ch, cells = grid.shape
    smem = pl.BlockSpec(memory_space=pltpu.SMEM)
    vmem = pl.BlockSpec(memory_space=pltpu.VMEM)
    return pl.pallas_call(
        conv_kernel,
        out_shape=jax.ShapeDtypeStruct((256, 2, 128), jnp.float32),
        in_specs=[smem] + [vmem] * 13,
        out_specs=vmem,
        scratch_shapes=[
            pltpu.VMEM((6, ch, cells), grid.dtype),
            pltpu.VMEM((216, 512), grid.dtype),
            pltpu.VMEM((216, cells), jnp.float32),
            pltpu.VMEM((1024, 64), jnp.float32),
        ],
        compiler_params=pltpu.CompilerParams(vmem_limit_bytes=48 << 20),
    )(at, grid, *halos, *weights)
def finish_kernel(got_ref, bias_ref, out_ref):
    for k in range(6):
        half, lane = k // 4, k % 4 * 32
        out_ref[k] = jnp.concatenate(
            [got_ref[64 * v:64 * v + 64, half, lane:lane + 32] for v in range(4)], axis=1) + bias_ref[k]

def finish(got, bias):
    smem = pl.BlockSpec(memory_space=pltpu.SMEM)
    vmem = pl.BlockSpec(memory_space=pltpu.VMEM)
    return pl.pallas_call(
        finish_kernel,
        out_shape=jax.ShapeDtypeStruct((6, 64, 128), jnp.float32),
        in_specs=[vmem, smem],
        out_specs=vmem,
    )(got, bias)


def gathered_weights(conv1_weight, conv1_bias, conv2_weight):
    tile_at = lax.axis_index("tile")
    share = 2 * (tile_at // 16) + tile_at % 2
    first = lax.dynamic_slice_in_dim(conv1_weight, 16 * share, 16, 1)
    second = lax.dynamic_slice_in_dim(conv2_weight, 16 * share, 16, 2).reshape(216, 16).T
    bias = lax.dynamic_slice_in_dim(conv1_bias, 16 * share, 16, 0)
    terms = []
    for _ in range(3):
        term = lax.reduce_precision(bias, 8, 7)
        bias = bias - term
        terms.append(term.astype(jnp.bfloat16)[:, None])
    rest = jnp.pad(jnp.concatenate([second] + terms, axis=1), ((0, 0), (0, 37)))
    mine = jnp.concatenate([first, rest[None]], axis=0)
    var_count, tiles = lax.axis_size("var"), lax.axis_size("tile")
    parts = [mine]
    for d in range(1, var_count):
        parts.append(lax.ppermute(mine, "var", [(i, (i + d) % var_count) for i in range(var_count)]))
    column = jnp.stack(parts)
    blocks = [column]
    for e in range(1, 4):
        blocks.append(lax.ppermute(column, "tile", [(i, (i + 16 * e) % tiles) for i in range(tiles)]))
    swap = [(i, i ^ 1) for i in range(tiles)]
    return blocks + [lax.ppermute(b, "tile", swap) for b in blocks]


def body(mesh_latents, edge_idx, edge_weight, conv1_weight, conv1_bias, conv2_weight, conv2_bias):
    tile_at, var_at = lax.axis_index("tile"), lax.axis_index("var")
    tiles, var_count = lax.axis_size("tile"), lax.axis_size("var")
    mesh_dev = mesh_latents.shape[1]
    rim = 64
    up = [(i, (i + 1) % tiles) for i in range(tiles)]
    down = [(j, i) for i, j in up]
    left = lax.ppermute(mesh_latents[:, mesh_dev - rim:], "tile", up)
    right = lax.ppermute(mesh_latents[:, :rim], "tile", down)
    u, wt, lo, hi = prep(edge_idx, edge_weight, tile_at, mesh_dev, mesh_dev * tiles, rim)
    pieces, first, last = decode(u, wt, lo, hi, mesh_latents, left, right)

    halos = []
    for d in range(4):
        to_first = [(4 * t + (4 - d) % 4, (t + 1) % tiles * 4) for t in range(tiles)]
        to_last = [(4 * t + 3 - d, (t - 1) % tiles * 4 + 3) for t in range(tiles)]
        edge = jnp.where(var_at == (4 - d) % 4, last, first)
        halos.append(lax.ppermute(edge, ("tile", "var"), to_first + to_last))

    weights = gathered_weights(conv1_weight, conv1_bias, conv2_weight)
    grid = lax.all_to_all(pieces, "var", split_axis=0, concat_axis=0, tiled=True)
    grid = grid.reshape(grid.shape[0] * grid.shape[1], grid.shape[2])
    fields = convolve(var_at.reshape(1), grid, halos, weights)
    got = lax.all_to_all(fields, ("var", "tile"), split_axis=0, concat_axis=0, tiled=True)
    return finish(got, conv2_bias).reshape(6, 1, tiles * 128)


def solution(mesh):
    return jax.shard_map(
        body,
        mesh=mesh,
        in_specs=(
            P("var", "tile"),
            P(None, None, "tile"),
            P(None, None, "tile"),
            P(None, "var", None),
            P("var"),
            P(None, None, "var"),
            P("var"),
        ),
        out_specs=P("var", "tile", None),
        check_vma=False,
    )
```

time: 296 us -> 138 us (0.47)
  matrix products: 76.1 us -> 0 us
  local copies, waits for them, and re-layouts: 40.2 us -> 2.91 us
  waiting for transfers between devices: 67.6 us -> 33.9 us
  loops' own time: 33.1 us -> 0 us
  starting transfers between devices: 13.8 us -> 45.2 us
  other arithmetic: 27.3 us -> 2.08 us
  Pallas kernels: 0 us -> 20.6 us
  between operations: 13.6 us -> 0.22 us
  blocking collectives: 23.6 us -> 32.5 us
    dot_general x34 -> x0, matrix products: 76.1 us -> none  [the longest x18 49 us: sweep(): jnp.einsum('oc,clw->olw', weight[3 * row_off + col_off], padded[:, row_of...]
    all_gather x1 -> x0, waiting for transfers between devices: 37.9 us -> none  [body(): lax.all_gather(mesh_latents, 'var', axis=0, tiled=True)]
    another operation x1 -> x0, loops' own time: 33.1 us -> none  [body(): result = lax.map(one_block, (starts, block_idx, block_wts))]
    ppermute x6 -> x16, waiting for transfers between devices: 3.43 us -> 33.9 us  [the longest x4 25.2 us: body(): halos.append(lax.ppermute(edge, ('tile', 'var'), to_first + to_last))]
    ppermute x6 -> x16, starting transfers between devices: 13.8 us -> 41.5 us  [the longest x4 14.7 us: gathered_weights(): return blocks + [lax.ppermute(b, 'tile', swap) for b in blocks]]
    reduce_scatter x1 -> x0, waiting for transfers between devices: 25.5 us -> none  [body(): lax.psum_scatter(sweep(hid_pad, conv2_weight, lon_dev), 'var', scatter_di...]
    sub x32 -> x0, other arithmetic: 21.8 us -> none  [one_block(): rel = (idx_block[k] - start).reshape(1, lat_rows * span)]
    pallas_call x0 -> x3, Pallas kernels: none -> 20.6 us  [the longest x1 13.3 us: convolve(): pl.pallas_call(conv_kernel, out_shape=jax.ShapeDtypeStruct((256, 2, 128),...]
  transfers between devices with their start and end apart: 8 -> 17, of which waited for: 4 -> 7; matrix products, arithmetic and copies ran while one was open for 2% -> 3% of each run, Pallas kernels for 0% -> 0%
where the time goes in v1:
time: 138 us; the launch traced here: 137 us
  starting transfers between devices  45.2 us (33%)
  waiting for transfers between devices  33.9 us (25%)
  blocking collectives  32.5 us (24%)
  Pallas kernels  20.6 us (15%)
  local copies, waits for them, and re-layouts  2.91 us (2%)
  other arithmetic  2.08 us (2%)
    all_to_all x1, blocking collectives, body(): lax.all_to_all(fields, ('var', 'tile'), split_axis=0, concat_axis=0, tile...  32.5 us
    ppermute x4, waiting for transfers between devices, body(): halos.append(lax.ppermute(edge, ('tile', 'var'), to_first + to_last))  25.2 us
    ppermute x4, starting transfers between devices, gathered_weights(): return blocks + [lax.ppermute(b, 'tile', swap) for b in blocks]  14.7 us
    pallas_call x1, Pallas kernels, convolve(): pl.pallas_call(conv_kernel, out_shape=jax.ShapeDtypeStruct((256, 2, 128),...  13.3 us
    ppermute x4, starting transfers between devices, body(): halos.append(lax.ppermute(edge, ('tile', 'var'), to_first + to_last))  13.1 us
    ppermute x3, waiting for transfers between devices, gathered_weights(): lax.ppermute(mine, 'var', [(i, (i + d) % var_count) for i in range(var_co...  8.69 us
    ppermute x3, starting transfers between devices, gathered_weights(): lax.ppermute(column, 'tile', [(i, (i + 16 * e) % tiles) for i in range(ti...  6.5 us
    pallas_call x1, Pallas kernels, decode(): pl.pallas_call(decode_kernel, out_shape=(jax.ShapeDtypeStruct((4, ch, (nb...  5.29 us
  transfers between devices with their start and end apart: 17, of which 7 were waited for; matrix products, arithmetic and copies ran while one was open for 3% of the time, Pallas kernels for 0%

profile of v1, /device:TPU:1, one launch (start us, length us, event | category | flops | bytes accessed | tf_op | source)
XLA Modules:
  0.0 137.5 jit_solution(2628280002867311004)
XLA Ops:
  0.0 0.9 fusion.18
  0.9 3.0 %collective-permute-start = (bf16[64,64]{1,0:T(8,128)(2,1)S(1)}, bf16[64,64]{1,0:T(8,128)(2,1)S(1)}, u32[]{:S(2)}, u32[]{:S(2)}) collective-permute-start(bf16[64,64]{1,0:T(8,128)(2,1)S(1)} %get-tuple-element.14), channel_id=1, source_target_pairs={{0,4},{4,8},{8,12},{12,16},{16,20},{20,24},{24,28},{28,32},{32,36}... | collective-permute-start | bytes 24584 | tf_op jit(solution)/shard_map/ppermute | solution.py:266
  4.0 0.3 collective-permute-start.1
  4.3 1.0 fusion.16
  5.4 0.1 reduce_min.14
  5.5 0.7 fusion.9
  6.6 0.9 constant_dynamic-slice_fusion
  8.4 5.3 %shard_map.73 = (bf16[4,64,2304]{2,1,0:T(8,128)(2,1)}, bf16[64,128]{1,0:T(8,128)(2,1)S(1)}, bf16[64,128]{1,0:T(8,128)(2,1)S(1)}) custom-call(s32[64]{0:T(128)S(1)} %get-tuple-element.26.lo_ref, s32[64]{0:T(128)S(1)} %get-tuple-element.25.hi_ref, s32[3,64,128]{2,1,0:T(8,128)S(1)} %reshape.21.u_ref, f32[3,64,128]{2,1,0:T(8,128)S(1)} %reshape.22.wt_ref, ...), custom_call_target="tpu_custom_call" | custom-call | tf_op jit(solution)/shard_map/pallas_call | solution.py:104
  13.7 3.7 %all-to-all-start = ((bf16[4,64,2304]{2,1,0:T(8,128)(2,1)}), bf16[4,64,2304]{2,1,0:T(8,128)(2,1)S(1)}, u32[]{:S(2)}, u32[]{:S(2)}) async-start(bf16[4,64,2304]{2,1,0:T(8,128)(2,1)} %get-tuple-element.8), calls=%async_computation | async-start | bytes 2359296 | tf_op jit(solution)/shard_map/all_to_all | solution.py:279
  17.4 2.8 %collective-permute-start.8 = (bf16[10,16,256]{2,1,0:T(8,128)(2,1)S(1)}, bf16[10,16,256]{2,1,0:T(8,128)(2,1)S(1)}, u32[]{:S(2)}, u32[]{:S(2)}) collective-permute-start(bf16[10,16,256]{2,1,0:T(8,128)(2,1)S(1)} %get-tuple-element.17), channel_id=1, source_target_pairs={{0,3},{1,0},{2,1},{3,2},{4,7},{5,4},{6,5},{7,6},{8,11},{9,8},{10,9... | collective-permute-start | bytes 245768 | tf_op jit(solution)/shard_map/ppermute | solution.py:250
  20.2 0.6 collective-permute-start.7
  20.8 0.6 collective-permute-start.6
  21.3 6.3 %collective-permute-done.8 = bf16[10,16,256]{2,1,0:T(8,128)(2,1)S(1)} collective-permute-done((bf16[10,16,256]{2,1,0:T(8,128)(2,1)S(1)}, bf16[10,16,256]{2,1,0:T(8,128)(2,1)S(1)}, u32[]{:S(2)}, u32[]{:S(2)}) %collective-permute-start.8) | collective-permute-done | bytes 81952 | tf_op jit(solution)/shard_map/ppermute | solution.py:250
  27.6 1.3 collective-permute-done.7
  28.9 1.1 collective-permute-done.6
  30.1 2.8 %collective-permute-start.9 = (bf16[4,10,16,256]{3,2,1,0:T(8,128)(2,1)S(1)}, bf16[4,10,16,256]{3,2,1,0:T(8,128)(2,1)S(1)}, u32[]{:S(2)}, u32[]{:S(2)}) collective-permute-start(bf16[4,10,16,256]{3,2,1,0:T(8,128)(2,1)S(1)} %pad_maximum_fusion.rest_0_), channel_id=1, source_target_pairs={{0,64},{4,68},{8,72},{12,76},{16,80},{20,84},{24,88},{28,92},{32,9... | collective-permute-start | bytes 983048 | tf_op jit(solution)/shard_map/ppermute | solution.py:254
  32.9 2.3 %collective-permute-start.10 = (bf16[4,10,16,256]{3,2,1,0:T(8,128)(2,1)S(1)}, bf16[4,10,16,256]{3,2,1,0:T(8,128)(2,1)S(1)}, u32[]{:S(2)}, u32[]{:S(2)}) collective-permute-start(bf16[4,10,16,256]{3,2,1,0:T(8,128)(2,1)S(1)} %pad_maximum_fusion.rest_0_), channel_id=1, source_target_pairs={{0,128},{4,132},{8,136},{12,140},{16,144},{20,148},{24,152},{28,15... | collective-permute-start | bytes 983048 | tf_op jit(solution)/shard_map/ppermute | solution.py:254
  35.2 1.4 collective-permute-start.11
  36.6 7.5 %collective-permute-start.12 = (bf16[4,10,16,256]{3,2,1,0:T(8,128)(2,1)S(1)}, bf16[4,10,16,256]{3,2,1,0:T(8,128)(2,1)S(1)}, u32[]{:S(2)}, u32[]{:S(2)}) collective-permute-start(bf16[4,10,16,256]{3,2,1,0:T(8,128)(2,1)S(1)} %pad_maximum_fusion.rest_0_), channel_id=1, source_target_pairs={{0,4},{4,0},{8,12},{12,8},{16,20},{20,16},{24,28},{28,24},{32,36},... | collective-permute-start | bytes 983048 | tf_op jit(solution)/shard_map/ppermute | solution.py:256
  44.0 3.4 %collective-permute-start.13 = (bf16[4,10,16,256]{3,2,1,0:T(8,128)(2,1)S(1)}, bf16[4,10,16,256]{3,2,1,0:T(8,128)(2,1)}, u32[]{:S(2)}, u32[]{:S(2)}) collective-permute-start(bf16[4,10,16,256]{3,2,1,0:T(8,128)(2,1)S(1)} %collective-permute-done.9.rest_1_), channel_id=1, source_target_pairs={{0,4},{4,0},{8,12},{12,8},{16,20},{20,16},{24,28},{28,24},{32,36},... | collective-permute-start | bytes 983048 | tf_op jit(solution)/shard_map/ppermute | solution.py:256
  47.4 3.9 %collective-permute-start.14 = (bf16[4,10,16,256]{3,2,1,0:T(8,128)(2,1)S(1)}, bf16[4,10,16,256]{3,2,1,0:T(8,128)(2,1)}, u32[]{:S(2)}, u32[]{:S(2)}) collective-permute-start(bf16[4,10,16,256]{3,2,1,0:T(8,128)(2,1)S(1)} %collective-permute-done.10.rest_2_), channel_id=1, source_target_pairs={{0,4},{4,0},{8,12},{12,8},{16,20},{20,16},{24,28},{28,24},{32,36},... | collective-permute-start | bytes 983048 | tf_op jit(solution)/shard_map/ppermute | solution.py:256
  51.3 8.7 %collective-permute-start.2 = (bf16[64,128]{1,0:T(8,128)(2,1)S(1)}, bf16[64,128]{1,0:T(8,128)(2,1)S(1)}, u32[]{:S(2)}, u32[]{:S(2)}) collective-permute-start(bf16[64,128]{1,0:T(8,128)(2,1)S(1)} %get-tuple-element.21), channel_id=1, source_target_pairs={{0,4},{4,8},{8,12},{12,16},{16,20},{20,24},{24,28},{28,32},{32,36}... | collective-permute-start | bytes 49160 | tf_op jit(solution)/shard_map/ppermute | solution.py:276
  59.9 0.8 collective-permute-done.2.h0
  60.8 1.3 collective-permute-start.3
  62.1 10.2 %collective-permute-done.3.h1 = bf16[64,128]{1,0:T(8,128)(2,1)S(1)} collective-permute-done((bf16[64,128]{1,0:T(8,128)(2,1)S(1)}, bf16[64,128]{1,0:T(8,128)(2,1)S(1)}, u32[]{:S(2)}, u32[]{:S(2)}) %collective-permute-start.3) | collective-permute-done | bytes 16416 | tf_op jit(solution)/shard_map/ppermute | solution.py:276
  72.3 1.3 collective-permute-start.4
  73.6 7.4 %collective-permute-done.4.h2 = bf16[64,128]{1,0:T(8,128)(2,1)S(1)} collective-permute-done((bf16[64,128]{1,0:T(8,128)(2,1)S(1)}, bf16[64,128]{1,0:T(8,128)(2,1)S(1)}, u32[]{:S(2)}, u32[]{:S(2)}) %collective-permute-start.4) | collective-permute-done | bytes 16416 | tf_op jit(solution)/shard_map/ppermute | solution.py:276
  81.0 1.9 %collective-permute-start.5 = (bf16[64,128]{1,0:T(8,128)(2,1)S(1)}, bf16[64,128]{1,0:T(8,128)(2,1)S(1)}, u32[]{:S(2)}, u32[]{:S(2)}) collective-permute-start(bf16[64,128]{1,0:T(8,128)(2,1)S(1)} %get-tuple-element.18), channel_id=1, source_target_pairs={{1,4},{5,8},{9,12},{13,16},{17,20},{21,24},{25,28},{29,32},{33,36}... | collective-permute-start | bytes 49160 | tf_op jit(solution)/shard_map/ppermute | solution.py:276
  82.9 6.7 %collective-permute-done.5.h3 = bf16[64,128]{1,0:T(8,128)(2,1)S(1)} collective-permute-done((bf16[64,128]{1,0:T(8,128)(2,1)S(1)}, bf16[64,128]{1,0:T(8,128)(2,1)S(1)}, u32[]{:S(2)}, u32[]{:S(2)}) %collective-permute-start.5) | collective-permute-done | bytes 16416 | tf_op jit(solution)/shard_map/ppermute | solution.py:276
  89.6 13.3 %shard_map.74 = f32[256,2,128]{2,1,0:T(2,128)S(1)} custom-call(s32[1]{0:T(128)} %bitcast.at_ref, bf16[256,2304]{1,0:T(8,128)(2,1)S(1)} %bitcast.21, bf16[64,128]{1,0:T(8,128)(2,1)S(1)} %collective-permute-done.2.h0, bf16[64,128]{1,0:T(8,128)(2,1)S(1)} %collective-permute-done.3.h1, bf16[64,128]{1,0:T(8,128)(2,1)S(1)} %collective-permute-done.4.h2, ...), custom_call_target="tpu_custom_call" | custom-call | tf_op jit(solution)/shard_map/pallas_call | solution.py:204
  103.0 32.5 %all_to_all.10.got_ref = f32[256,2,128]{2,1,0:T(2,128)} all-to-all(f32[256,2,128]{2,1,0:T(2,128)S(1)} %shard_map.74), channel_id=1, replica_groups=mesh['tile'=64,'var'=4] {'var','tile'}, dimensions={0} | all-to-all | bytes 524288 | tf_op jit(solution)/shard_map/all_to_all | solution.py:282
  135.5 2.0 %shard_map.75 = f32[6,64,128]{2,1,0:T(8,128)} custom-call(f32[256,2,128]{2,1,0:T(2,128)} %all_to_all.10.got_ref, f32[6]{0:T(128)} %bias_ref.1), custom_call_target="tpu_custom_call" | custom-call | tf_op jit(solution)/shard_map/pallas_call | solution.py:226
  (34 shorter events, 1.4 us)
Async XLA Ops:
  0.0 7.5 %copy-start = (bf16[9,128,256]{2,1,0:T(8,128)(2,1)S(1)}, bf16[9,128,256]{2,1,0:T(8,128)(2,1)}, u32[]{:S(2)}) copy-start(bf16[9,128,256]{2,1,0:T(8,128)(2,1)} %param.10) | copy-start | bytes 1769476
  0.0 8.4 %copy-start.1 = (bf16[64,4096]{1,0:T(8,128)(2,1)S(1)}, bf16[64,4096]{1,0:T(8,128)(2,1)}, u32[]{:S(2)}) copy-start(bf16[64,4096]{1,0:T(8,128)(2,1)} %lat_ref.1) | copy-start | bytes 1572868
  0.0 8.1 %copy-start.2 = (f32[3,64,128]{2,1,0:T(8,128)S(1)}, f32[3,64,128]{2,1,0:T(8,128)}, u32[]{:S(2)}) copy-start(f32[3,64,128]{2,1,0:T(8,128)} %param.9) | copy-start | bytes 294916
  0.9 7.4 %collective-permute-start = (bf16[64,64]{1,0:T(8,128)(2,1)S(1)}, bf16[64,64]{1,0:T(8,128)(2,1)S(1)}, u32[]{:S(2)}, u32[]{:S(2)}) collective-permute-start(bf16[64,64]{1,0:T(8,128)(2,1)S(1)} %get-tuple-element.14), channel_id=1, source_target_pairs={{0,4},{4,8},{8,12},{12,16},{16,20},{20,24},{24,28},{28,32},{32,36}... | collective-permute-start | bytes 24584 | tf_op jit(solution)/shard_map/ppermute | solution.py:266
  4.0 4.4 %collective-permute-start.1 = (bf16[64,64]{1,0:T(8,128)(2,1)S(1)}, bf16[64,64]{1,0:T(8,128)(2,1)S(1)}, u32[]{:S(2)}, u32[]{:S(2)}) collective-permute-start(bf16[64,64]{1,0:T(8,128)(2,1)S(1)} %get-tuple-element.13), channel_id=1, source_target_pairs={{4,0},{8,4},{12,8},{16,12},{20,16},{24,20},{28,24},{32,28},{36,32}... | collective-permute-start | bytes 24584 | tf_op jit(solution)/shard_map/ppermute | solution.py:267
  13.7 76.0 %all-to-all-start = ((bf16[4,64,2304]{2,1,0:T(8,128)(2,1)}), bf16[4,64,2304]{2,1,0:T(8,128)(2,1)S(1)}, u32[]{:S(2)}, u32[]{:S(2)}) async-start(bf16[4,64,2304]{2,1,0:T(8,128)(2,1)} %get-tuple-element.8), calls=%async_computation | async-start | bytes 2359296 | tf_op jit(solution)/shard_map/all_to_all | solution.py:279
  17.4 10.2 %collective-permute-start.8 = (bf16[10,16,256]{2,1,0:T(8,128)(2,1)S(1)}, bf16[10,16,256]{2,1,0:T(8,128)(2,1)S(1)}, u32[]{:S(2)}, u32[]{:S(2)}) collective-permute-start(bf16[10,16,256]{2,1,0:T(8,128)(2,1)S(1)} %get-tuple-element.17), channel_id=1, source_target_pairs={{0,3},{1,0},{2,1},{3,2},{4,7},{5,4},{6,5},{7,6},{8,11},{9,8},{10,9... | collective-permute-start | bytes 245768 | tf_op jit(solution)/shard_map/ppermute | solution.py:250
  20.2 8.7 %collective-permute-start.7 = (bf16[10,16,256]{2,1,0:T(8,128)(2,1)S(1)}, bf16[10,16,256]{2,1,0:T(8,128)(2,1)S(1)}, u32[]{:S(2)}, u32[]{:S(2)}) collective-permute-start(bf16[10,16,256]{2,1,0:T(8,128)(2,1)S(1)} %get-tuple-element.17), channel_id=1, source_target_pairs={{0,2},{1,3},{2,0},{3,1},{4,6},{5,7},{6,4},{7,5},{8,10},{9,11},{10,... | collective-permute-start | bytes 245768 | tf_op jit(solution)/shard_map/ppermute | solution.py:250
  20.8 9.3 %collective-permute-start.6 = (bf16[10,16,256]{2,1,0:T(8,128)(2,1)S(1)}, bf16[10,16,256]{2,1,0:T(8,128)(2,1)S(1)}, u32[]{:S(2)}, u32[]{:S(2)}) collective-permute-start(bf16[10,16,256]{2,1,0:T(8,128)(2,1)S(1)} %get-tuple-element.17), channel_id=1, source_target_pairs={{0,1},{1,2},{2,3},{3,0},{4,5},{5,6},{6,7},{7,4},{8,9},{9,10},{10,1... | collective-permute-start | bytes 245768 | tf_op jit(solution)/shard_map/ppermute | solution.py:250
  30.1 14.0 %collective-permute-start.9 = (bf16[4,10,16,256]{3,2,1,0:T(8,128)(2,1)S(1)}, bf16[4,10,16,256]{3,2,1,0:T(8,128)(2,1)S(1)}, u32[]{:S(2)}, u32[]{:S(2)}) collective-permute-start(bf16[4,10,16,256]{3,2,1,0:T(8,128)(2,1)S(1)} %pad_maximum_fusion.rest_0_), channel_id=1, source_target_pairs={{0,64},{4,68},{8,72},{12,76},{16,80},{20,84},{24,88},{28,92},{32,9... | collective-permute-start | bytes 983048 | tf_op jit(solution)/shard_map/ppermute | solution.py:254
  32.9 14.5 %collective-permute-start.10 = (bf16[4,10,16,256]{3,2,1,0:T(8,128)(2,1)S(1)}, bf16[4,10,16,256]{3,2,1,0:T(8,128)(2,1)S(1)}, u32[]{:S(2)}, u32[]{:S(2)}) collective-permute-start(bf16[4,10,16,256]{3,2,1,0:T(8,128)(2,1)S(1)} %pad_maximum_fusion.rest_0_), channel_id=1, source_target_pairs={{0,128},{4,132},{8,136},{12,140},{16,144},{20,148},{24,152},{28,15... | collective-permute-start | bytes 983048 | tf_op jit(solution)/shard_map/ppermute | solution.py:254
  35.2 16.0 %collective-permute-start.11 = (bf16[4,10,16,256]{3,2,1,0:T(8,128)(2,1)S(1)}, bf16[4,10,16,256]{3,2,1,0:T(8,128)(2,1)S(1)}, u32[]{:S(2)}, u32[]{:S(2)}) collective-permute-start(bf16[4,10,16,256]{3,2,1,0:T(8,128)(2,1)S(1)} %pad_maximum_fusion.rest_0_), channel_id=1, source_target_pairs={{0,192},{4,196},{8,200},{12,204},{16,208},{20,212},{24,216},{28,22... | collective-permute-start | bytes 983048 | tf_op jit(solution)/shard_map/ppermute | solution.py:254
  36.6 53.0 %collective-permute-start.12 = (bf16[4,10,16,256]{3,2,1,0:T(8,128)(2,1)S(1)}, bf16[4,10,16,256]{3,2,1,0:T(8,128)(2,1)S(1)}, u32[]{:S(2)}, u32[]{:S(2)}) collective-permute-start(bf16[4,10,16,256]{3,2,1,0:T(8,128)(2,1)S(1)} %pad_maximum_fusion.rest_0_), channel_id=1, source_target_pairs={{0,4},{4,0},{8,12},{12,8},{16,20},{20,16},{24,28},{28,24},{32,36},... | collective-permute-start | bytes 983048 | tf_op jit(solution)/shard_map/ppermute | solution.py:256
  44.0 45.6 %collective-permute-start.13 = (bf16[4,10,16,256]{3,2,1,0:T(8,128)(2,1)S(1)}, bf16[4,10,16,256]{3,2,1,0:T(8,128)(2,1)}, u32[]{:S(2)}, u32[]{:S(2)}) collective-permute-start(bf16[4,10,16,256]{3,2,1,0:T(8,128)(2,1)S(1)} %collective-permute-done.9.rest_1_), channel_id=1, source_target_pairs={{0,4},{4,0},{8,12},{12,8},{16,20},{20,16},{24,28},{28,24},{32,36},... | collective-permute-start | bytes 983048 | tf_op jit(solution)/shard_map/ppermute | solution.py:256
  47.4 42.2 %collective-permute-start.14 = (bf16[4,10,16,256]{3,2,1,0:T(8,128)(2,1)S(1)}, bf16[4,10,16,256]{3,2,1,0:T(8,128)(2,1)}, u32[]{:S(2)}, u32[]{:S(2)}) collective-permute-start(bf16[4,10,16,256]{3,2,1,0:T(8,128)(2,1)S(1)} %collective-permute-done.10.rest_2_), channel_id=1, source_target_pairs={{0,4},{4,0},{8,12},{12,8},{16,20},{20,16},{24,28},{28,24},{32,36},... | collective-permute-start | bytes 983048 | tf_op jit(solution)/shard_map/ppermute | solution.py:256
  51.2 38.4 %collective-permute-start.15 = (bf16[4,10,16,256]{3,2,1,0:T(8,128)(2,1)S(1)}, bf16[4,10,16,256]{3,2,1,0:T(8,128)(2,1)}, u32[]{:S(2)}, u32[]{:S(2)}) collective-permute-start(bf16[4,10,16,256]{3,2,1,0:T(8,128)(2,1)S(1)} %collective-permute-done.11.rest_3_), channel_id=1, source_target_pairs={{0,4},{4,0},{8,12},{12,8},{16,20},{20,16},{24,28},{28,24},{32,36},... | collective-permute-start | bytes 983048 | tf_op jit(solution)/shard_map/ppermute | solution.py:256
  51.3 9.5 %collective-permute-start.2 = (bf16[64,128]{1,0:T(8,128)(2,1)S(1)}, bf16[64,128]{1,0:T(8,128)(2,1)S(1)}, u32[]{:S(2)}, u32[]{:S(2)}) collective-permute-start(bf16[64,128]{1,0:T(8,128)(2,1)S(1)} %get-tuple-element.21), channel_id=1, source_target_pairs={{0,4},{4,8},{8,12},{12,16},{16,20},{20,24},{24,28},{28,32},{32,36}... | collective-permute-start | bytes 49160 | tf_op jit(solution)/shard_map/ppermute | solution.py:276
  60.8 11.5 %collective-permute-start.3 = (bf16[64,128]{1,0:T(8,128)(2,1)S(1)}, bf16[64,128]{1,0:T(8,128)(2,1)S(1)}, u32[]{:S(2)}, u32[]{:S(2)}) collective-permute-start(bf16[64,128]{1,0:T(8,128)(2,1)S(1)} %get-tuple-element.20), channel_id=1, source_target_pairs={{3,4},{7,8},{11,12},{15,16},{19,20},{23,24},{27,28},{31,32},{35,36... | collective-permute-start | bytes 49160 | tf_op jit(solution)/shard_map/ppermute | solution.py:276
  72.3 8.6 %collective-permute-start.4 = (bf16[64,128]{1,0:T(8,128)(2,1)S(1)}, bf16[64,128]{1,0:T(8,128)(2,1)S(1)}, u32[]{:S(2)}, u32[]{:S(2)}) collective-permute-start(bf16[64,128]{1,0:T(8,128)(2,1)S(1)} %get-tuple-element.19), channel_id=1, source_target_pairs={{2,4},{6,8},{10,12},{14,16},{18,20},{22,24},{26,28},{30,32},{34,36... | collective-permute-start | bytes 49160 | tf_op jit(solution)/shard_map/ppermute | solution.py:276
  81.0 8.7 %collective-permute-start.5 = (bf16[64,128]{1,0:T(8,128)(2,1)S(1)}, bf16[64,128]{1,0:T(8,128)(2,1)S(1)}, u32[]{:S(2)}, u32[]{:S(2)}) collective-permute-start(bf16[64,128]{1,0:T(8,128)(2,1)S(1)} %get-tuple-element.18), channel_id=1, source_target_pairs={{1,4},{5,8},{9,12},{13,16},{17,20},{21,24},{25,28},{29,32},{33,36}... | collective-permute-start | bytes 49160 | tf_op jit(solution)/shard_map/ppermute | solution.py:276

commit v2 on v1

v2 whole, which is shorter than its diff:
```python
import functools

import jax
import jax.numpy as jnp
from jax import lax
from jax.experimental import pallas as pl
from jax.experimental.pallas import tpu as pltpu
from jax.sharding import PartitionSpec as P


GRP = 8
TILE = 2304


def prep(edge_idx, edge_weight, tile_at, mesh_dev, nmesh, rim):
    u = jnp.mod(edge_idx - tile_at * mesh_dev + rim, nmesh)
    u = u.transpose(0, 2, 1).reshape(3, -1, 128)
    wt = edge_weight.transpose(0, 2, 1).reshape(3, -1, 128)
    lo = jnp.min(u, axis=(0, 2)) // 64
    hi = jnp.max(u, axis=(0, 2)) // 64
    return u, wt, lo, hi

def decode_kernel(blocks, lo_ref, hi_ref, u_ref, wt_ref, lat_ref, left_ref, right_ref, *rest):
    outs, (lats, parts, accs) = rest[:-3], rest[-3:]
    ch, nodes = lat_ref.shape
    rim = left_ref.shape[1]
    ext = nodes + 2 * rim
    nblk = u_ref.shape[1]
    width = lats.shape[2]
    bf = lat_ref.dtype
    main = lat_ref[...]
    zeros = lambda n: jnp.zeros((ch, n), bf)
    lats[0] = jnp.concatenate([left_ref[...], main, right_ref[...], zeros(width - ext)], axis=1)
    lats[1] = jnp.concatenate([main, right_ref[...], zeros(width - ext + rim)], axis=1)

    u0, u1, u2 = u_ref[0], u_ref[1], u_ref[2]
    w0, w1, w2 = wt_ref[0], wt_ref[1], wt_ref[2]
    w0 = w0 + jnp.where(u1 == u0, w1, 0.0) + jnp.where(u2 == u0, w2, 0.0)
    w1 = w1 + jnp.where(u2 == u1, w2, 0.0)
    for k, w in enumerate((w0, w1, w2)):
        top = w.astype(bf).astype(jnp.float32)
        parts[k] = top
        parts[3 + k] = w - top

    node = lax.broadcasted_iota(jnp.int32, (256, 128), 0).astype(jnp.float32).astype(bf)

    def window(b, at):
        src = lats[at & 1, :, pl.ds(pl.multiple_of((at >> 1) * 128, 128), 256)]
        tops = jnp.zeros((256, 128), bf)
        rests = jnp.zeros((256, 128), bf)
        for k in (2, 1, 0):
            rel = (u_ref[k, pl.ds(b, 1), :] - at * 64).astype(jnp.float32).astype(bf)
            here = node == rel
            tops = jnp.where(here, parts[k, pl.ds(b, 1), :].astype(bf), tops)
            rests = jnp.where(here, parts[3 + k, pl.ds(b, 1), :].astype(bf), rests)
        table = jnp.concatenate([tops, rests], axis=1)
        both = jnp.dot(src, table, preferred_element_type=jnp.float32)
        return both[:, :128] + both[:, 128:]

    def several(ids):
        more = jnp.int32(0)
        for j, b in enumerate(ids):
            at = lo_ref[b]
            accs[j] = window(b, at)
            more = more + jnp.where(hi_ref[b] - at >= 4, 1, 0)

        @pl.when(more > 0)
        def _():
            for j, b in enumerate(ids):
                at = lo_ref[b]

                @pl.loop(1, ((hi_ref[b] - at) >> 2) + 1)
                def _(step):
                    accs[j] += window(b, at + 4 * step)

    if blocks is not None:
        several(blocks)
        for j, out in enumerate(outs):
            out[...] = accs[j].astype(out.dtype)
        return

    out_ref, = outs
    per = nblk // 4

    def group(g, _):
        several([g * GRP + j for j in range(GRP)])
        for j in range(GRP):
            b = g * GRP + j
            val = accs[j].astype(out_ref.dtype)
            piece, at = b // per, b % per
            out_ref[piece, :, pl.ds(pl.multiple_of(at * 128 + 128, 128), 128)] = val
            if j == 0:
                @pl.when(jnp.logical_and(at == 0, piece > 0))
                def _():
                    out_ref[piece - 1, :, (per + 1) * 128:] = val
            if j == GRP - 1:
                @pl.when(jnp.logical_and(at == per - 1, piece < 3))
                def _():
                    out_ref[piece + 1, :, :128] = val
        return 0
    lax.fori_loop(0, nblk // GRP, group, 0)


def decode(u, wt, lo, hi, lat, left, right, blocks=None):
    ch, nodes = lat.shape
    nblk = u.shape[1]
    smem = pl.BlockSpec(memory_space=pltpu.SMEM)
    vmem = pl.BlockSpec(memory_space=pltpu.VMEM)
    if blocks is None:
        shapes, done = (jax.ShapeDtypeStruct((4, ch, (nblk // 4 + 2) * 128), lat.dtype),), nblk
    else:
        shapes, done = (jax.ShapeDtypeStruct((ch, 128), lat.dtype),) * len(blocks), len(blocks)
    return pl.pallas_call(
        functools.partial(decode_kernel, blocks),
        out_shape=shapes,
        in_specs=[smem] * 2 + [vmem] * 5,
        out_specs=(vmem,) * len(shapes),
        scratch_shapes=[
            pltpu.VMEM((2, ch, nodes + 384), lat.dtype),
            pltpu.VMEM((6, nblk, 128), jnp.float32),
            pltpu.VMEM((GRP, ch, 128), jnp.float32),
        ],
        cost_estimate=pl.CostEstimate(flops=done * 256 * 128 * 4 * ch * 16, bytes_accessed=2 * ch * nodes * 2, transcendentals=0),
        compiler_params=pltpu.CompilerParams(vmem_limit_bytes=24 << 20),
    )(lo, hi, u, wt, lat, left, right)


def conv_kernel(var_ref, grid_ref, *rest):
    sources = rest[:8]
    out_ref, wts, shifted, mix, taps, rows, pairs, sems = rest[8:]
    copies = [pltpu.make_async_copy(src, wts.at[g], sems.at[g]) for g, src in enumerate(sources)]
    for copy in copies:
        copy.start()
    ch, cells = grid_ref.shape
    bf = grid_ref.dtype
    lat = 64
    out_cells = cells - 4 * lat

    place = lax.broadcasted_iota(jnp.int32, (1, cells), 1) % lat
    x = shifted
    x[1, :, :cells] = grid_ref[...]

    x[:, :, cells:] = jnp.zeros((6, ch, 128), bf)
    step = 64
    for c0 in range(0, ch, step):
        rs = slice(c0, c0 + step)
        v = grid_ref[rs, :].astype(jnp.float32)
        up = jnp.where(place == 0, 0.0, pltpu.roll(v, 1, 1))
        down = jnp.where(place == lat - 1, 0.0, pltpu.roll(v, cells - 1, 1))
        x[0, rs, :cells] = up.astype(bf)
        x[2, rs, :cells] = down.astype(bf)
        for r, u in enumerate((up, v, down)):
            x[3 + r, rs, :cells] = pltpu.roll(u, cells - lat, 1).astype(bf)

    for copy in copies:
        copy.wait()
    weights = [wts.at[g] for g in range(8)]

    last = jnp.concatenate([w[9] for w in weights], axis=0).astype(jnp.float32)
    mix[...] = last.T[:216].astype(bf)
    bias = last[:, 216:217] + last[:, 217:218] + last[:, 218:219]

    def tile(start, width):
        kernel_w = jnp.concatenate(
            [jnp.concatenate([w[k] for w in weights], axis=0) for k in range(9)], axis=1)
        cols = []
        for r in range(3):
            for s in range(3):
                src, off = (3 + r, 0) if s == 1 else (r, s * lat)
                cols.append(x[src, :, pl.ds(start + off, width)])
        pre = jnp.dot(kernel_w, jnp.concatenate(cols, axis=0), preferred_element_type=jnp.float32) + bias
        hidden = pre * (0.5 * jnp.tanh(0.5 * pre) + 0.5)
        taps[:, pl.ds(start, width)] = jnp.dot(mix[...], hidden.astype(bf), preferred_element_type=jnp.float32)

    @pl.loop(0, cells // TILE)
    def _(n):
        tile(pl.multiple_of(n * TILE, 128), TILE)

    def total(r):
        y = [taps[(3 * r + s) * 24:(3 * r + s + 1) * 24, :] for s in range(3)]
        mid = pltpu.roll(y[1], taps.shape[1] - lat, 1)
        return y[0][:, :out_cells] + mid[:, :out_cells] + y[2][:, 2 * lat:2 * lat + out_cells]

    spot = place[:, :out_cells]
    full = jnp.where(spot == 0, 0.0, pltpu.roll(total(0), 1, 1))
    full = full + total(1)
    full = full + jnp.where(spot == lat - 1, 0.0, pltpu.roll(total(2), out_cells - 1, 1))

    shift = []
    for g in range(4):
        terms = wts[(var_ref[0] - g) & 3, 9, 0:16, :].astype(jnp.float32)[:6]
        shift.append(terms[:, 219:220] + terms[:, 220:221] + terms[:, 221:222])
    full = full + jnp.concatenate(shift, axis=0)

    rows[...] = jnp.zeros_like(rows)
    for l in range(32):
        col = full[:, l * lat:(l + 1) * lat]
        for g in range(4):
            rows[pl.ds(g * 256 + l, 6, stride=32), :] = col[g * 6:g * 6 + 6]
    turned = rows[...].T
    for g in range(4):
        for h in range(2):
            pairs[pl.ds(g * 2 * lat + h, lat, stride=2), :] = turned[:, g * 256 + h * 128:g * 256 + h * 128 + 128]
    out_ref[...] = pairs[...].astype(out_ref.dtype)

def convolve(var_at, grid, weights):
    ch, cells = grid.shape
    vmem = pl.BlockSpec(memory_space=pltpu.VMEM)
    return pl.pallas_call(
        conv_kernel,
        out_shape=jax.ShapeDtypeStruct((512, 128), grid.dtype),
        in_specs=[pl.BlockSpec(memory_space=pltpu.SMEM), vmem] + [pl.BlockSpec(memory_space=pltpu.HBM)] * 8,
        out_specs=vmem,
        scratch_shapes=[
            pltpu.VMEM((8,) + weights[0].shape, grid.dtype),
            pltpu.VMEM((6, ch, cells + 128), grid.dtype),
            pltpu.VMEM((216, 512), grid.dtype),
            pltpu.VMEM((216, cells), jnp.float32),
            pltpu.VMEM((1024, 64), jnp.float32),
            pltpu.VMEM((512, 128), jnp.float32),
            pltpu.SemaphoreType.DMA((8,)),
        ],
        compiler_params=pltpu.CompilerParams(vmem_limit_bytes=24 << 20),
    )(var_at, grid, *weights)
def finish_kernel(got_ref, out_ref, pairs):
    pairs[...] = got_ref[...].astype(jnp.float32)
    for k in range(6):
        half, lane = k // 4, k % 4 * 32
        out_ref[k] = jnp.concatenate(
            [pairs[pl.ds(128 * v + half, 64, stride=2), :][:, lane:lane + 32] for v in range(4)], axis=1)


def finish(got):
    vmem = pl.BlockSpec(memory_space=pltpu.VMEM)
    return pl.pallas_call(
        finish_kernel,
        out_shape=jax.ShapeDtypeStruct((6, 64, 128), jnp.float32),
        in_specs=[vmem],
        out_specs=vmem,
        scratch_shapes=[pltpu.VMEM((512, 128), jnp.float32)],
    )(got)


def bf16_terms(value):
    terms = []
    for _ in range(3):
        term = lax.reduce_precision(value, 8, 7)
        value = value - term
        terms.append(term.astype(jnp.bfloat16)[:, None])
    return terms


def gathered_weights(conv1_weight, conv1_bias, conv2_weight, conv2_bias):
    tile_at = lax.axis_index("tile")
    half = conv1_weight.shape[1] // 2
    start = half * (tile_at % 2)
    first = lax.dynamic_slice_in_dim(conv1_weight, start, half, 1)
    second = lax.dynamic_slice_in_dim(conv2_weight, start, half, 2).reshape(216, half).T
    bias = lax.dynamic_slice_in_dim(conv1_bias, start, half, 0)
    terms = bf16_terms(bias)
    terms += [jnp.pad(t, ((0, half - t.shape[0]), (0, 0))) for t in bf16_terms(conv2_bias)]
    rest = jnp.pad(jnp.concatenate([second] + terms, axis=1), ((0, 0), (0, 34)))
    mine = jnp.concatenate([first, rest[None]], axis=0)
    count = lax.axis_size("var")
    return [mine] + [lax.ppermute(mine, "var", [(i, (i + d) % count) for i in range(count)]) for d in range(1, count)]


def exchanged_weights(blocks):
    tiles = lax.axis_size("tile")
    return blocks + [lax.ppermute(b, "tile", [(i, i ^ 1) for i in range(tiles)]) for b in blocks]


def body(mesh_latents, edge_idx, edge_weight, conv1_weight, conv1_bias, conv2_weight, conv2_bias):
    tile_at = lax.axis_index("tile")
    tiles = lax.axis_size("tile")
    mesh_dev = mesh_latents.shape[1]
    rim = 64
    up = [(i, (i + 1) % tiles) for i in range(tiles)]
    down = [(j, i) for i, j in up]
    left = lax.ppermute(mesh_latents[:, mesh_dev - rim:], "tile", up)
    right = lax.ppermute(mesh_latents[:, :rim], "tile", down)
    blocks = gathered_weights(conv1_weight, conv1_bias, conv2_weight, conv2_bias)
    u, wt, lo, hi = prep(edge_idx, edge_weight, tile_at, mesh_dev, mesh_dev * tiles, rim)
    first, last = decode(u, wt, lo, hi, mesh_latents, left, right, (0, u.shape[1] - 1))
    before = lax.ppermute(last, "tile", up)
    after = lax.ppermute(first, "tile", down)
    pieces, = decode(u, wt, lo, hi, mesh_latents, left, right)
    pieces = lax.dynamic_update_slice(pieces, before[None], (0, 0, 0))
    pieces = lax.dynamic_update_slice(pieces, after[None], (3, 0, pieces.shape[2] - 128))

    pieces, blocks = lax.optimization_barrier((pieces, blocks))
    weights = exchanged_weights(blocks)
    grid = lax.all_to_all(pieces, "var", split_axis=0, concat_axis=0, tiled=True)
    grid = grid.reshape(grid.shape[0] * grid.shape[1], grid.shape[2])
    fields = convolve(lax.axis_index("var").reshape(1), grid, weights)
    got = lax.all_to_all(fields.reshape(256, 2, 128), ("var", "tile"), split_axis=0, concat_axis=0, tiled=True)
    return finish(got.reshape(512, 128)).reshape(6, 1, tiles * 128)


def solution(mesh):
    return jax.shard_map(
        body,
        mesh=mesh,
        in_specs=(
            P("var", "tile"),
            P(None, None, "tile"),
            P(None, None, "tile"),
            P(None, "var", None),
            P("var"),
            P(None, None, "var"),
            P("var"),
        ),
        out_specs=P("var", "tile", None),
        check_vma=False,
    )
```

time: 138 us -> 82.8 us (0.60)
  waiting for transfers between devices: 33.9 us -> 10.3 us
  starting transfers between devices: 45.2 us -> 22.8 us
  blocking collectives: 32.5 us -> 26.4 us
  Pallas kernels: 20.6 us -> 17.2 us
    ppermute x14 -> x9, waiting for transfers between devices: 33.9 us -> 2.19 us  [the longest x4 2.18 us: exchanged_weights(): lax.ppermute(b, 'tile', [(i, i ^ 1) for i in range(tiles)])]
    ppermute x14 -> x9, starting transfers between devices: 38.2 us -> 16.2 us  [the longest x1 5.89 us: body(): after = lax.ppermute(first, 'tile', down)]
    all_to_all x1, blocking collectives: 32.5 us -> 26.4 us  [body(): lax.all_to_all(fields.reshape(256, 2, 128), ('var', 'tile'), split_axis=0...]
    ppermute x1, waiting for transfers between devices: 0.01 us -> 4.34 us  [body(): left = lax.ppermute(mesh_latents[:, mesh_dev - rim:], 'tile', up)]
    all_to_all x1, waiting for transfers between devices: 0.01 us -> 3.25 us  [body(): lax.all_to_all(pieces, 'var', split_axis=0, concat_axis=0, tiled=True)]
    pallas_call x2 -> x3, Pallas kernels: 18.6 us -> 15.4 us  [the longest x1 9.26 us: convolve(): pl.pallas_call(conv_kernel, out_shape=jax.ShapeDtypeStruct((512, 128), gr...]
    ppermute x1, starting transfers between devices: 3.04 us -> 1.61 us  [body(): left = lax.ppermute(mesh_latents[:, mesh_dev - rim:], 'tile', up)]
  transfers between devices with their start and end apart: 17 -> 12, of which waited for: 7 -> 7; matrix products, arithmetic and copies ran while one was open for 3% -> 3% of each run, Pallas kernels for 0% -> 7%
where the time goes in v2:
time: 82.8 us; the launch traced here: 82.6 us
  blocking collectives  26.4 us (32%)
  starting transfers between devices  22.8 us (28%)
  Pallas kernels  17.2 us (21%)
  waiting for transfers between devices  10.3 us (12%)
  local copies, waits for them, and re-layouts  3.82 us (5%)
  other arithmetic  1.84 us (2%)
    all_to_all x1, blocking collectives, body(): lax.all_to_all(fields.reshape(256, 2, 128), ('var', 'tile'), split_axis=0...  26.4 us
    pallas_call x1, Pallas kernels, convolve(): pl.pallas_call(conv_kernel, out_shape=jax.ShapeDtypeStruct((512, 128), gr...  9.26 us
    pallas_call x2, Pallas kernels, decode(): pl.pallas_call(functools.partial(decode_kernel, blocks), out_shape=shapes...  6.1 us
    ppermute x1, starting transfers between devices, body(): after = lax.ppermute(first, 'tile', down)  5.89 us
    ppermute x4, starting transfers between devices, exchanged_weights(): lax.ppermute(b, 'tile', [(i, i ^ 1) for i in range(tiles)])  5.67 us
    ppermute x3, starting transfers between devices, gathered_weights(): lax.ppermute(mine, 'var', [(i, (i + d) % count) for i in range(count)])  4.51 us
    ppermute x1, waiting for transfers between devices, body(): left = lax.ppermute(mesh_latents[:, mesh_dev - rim:], 'tile', up)  4.34 us
    all_to_all x1, starting transfers between devices, body(): lax.all_to_all(pieces, 'var', split_axis=0, concat_axis=0, tiled=True)  3.54 us
  transfers between devices with their start and end apart: 12, of which 7 were waited for; matrix products, arithmetic and copies ran while one was open for 3% of the time, Pallas kernels for 7%

profile of v2, /device:TPU:1, one launch (start us, length us, event | category | flops | bytes accessed | tf_op | source)
XLA Modules:
  0.0 82.6 jit_solution(8658284376135905398)
XLA Ops:
  0.0 0.8 fusion.10
  1.1 0.7 fusion.5
  1.9 0.1 copy.26
  2.2 0.9 %constant_dynamic-slice_fusion = bf16[9,24,64]{2,1,0:T(8,128)(2,1)S(1)} fusion(bf16[9,24,128]{2,1,0:T(8,128)(2,1)} %param.12, s32[]{:T(128)S(6)} %select_n.30), kind=kLoop, calls=%fused_computation.16 | loop fusion | bytes 55300 | tf_op jit(solution)/shard_map/dynamic_slice | solution.py:258
  3.5 3.4 %collective-permute-start.6 = (bf16[10,64,256]{2,1,0:T(8,128)(2,1)S(1)}, bf16[10,64,256]{2,1,0:T(8,128)(2,1)S(1)}, u32[]{:S(2)}, u32[]{:S(2)}) collective-permute-start(bf16[10,64,256]{2,1,0:T(8,128)(2,1)S(1)} %pad_maximum_fusion.rest_0_), channel_id=1, source_target_pairs={{0,3},{1,0},{2,1},{3,2},{4,7},{5,4},{6,5},{7,6},{8,11},{9,8},{10,9... | collective-permute-start | bytes 983048 | tf_op jit(solution)/shard_map/ppermute | solution.py:265
  6.8 0.5 collective-permute-start.5
  7.4 0.6 collective-permute-start.4
  8.1 1.5 %collective-permute-start.1 = (bf16[64,64]{1,0:T(8,128)(2,1)S(1)}, bf16[64,64]{1,0:T(8,128)(2,1)S(1)}, u32[]{:S(2)}, u32[]{:S(2)}) collective-permute-start(bf16[64,64]{1,0:T(8,128)(2,1)S(1)} %get-tuple-element.21), channel_id=1, source_target_pairs={{4,0},{8,4},{12,8},{16,12},{20,16},{24,20},{28,24},{32,28},{36,32}... | collective-permute-start | bytes 24584 | tf_op jit(solution)/shard_map/ppermute | solution.py:281
  9.6 1.6 %collective-permute-start = (bf16[64,64]{1,0:T(8,128)(2,1)S(1)}, bf16[64,64]{1,0:T(8,128)(2,1)S(1)}, u32[]{:S(2)}, u32[]{:S(2)}) collective-permute-start(bf16[64,64]{1,0:T(8,128)(2,1)S(1)} %get-tuple-element.22), channel_id=1, source_target_pairs={{0,4},{4,8},{8,12},{12,16},{16,20},{20,24},{24,28},{28,32},{32,36}... | collective-permute-start | bytes 24584 | tf_op jit(solution)/shard_map/ppermute | solution.py:280
  11.3 0.1 reduce_max.14
  11.4 0.1 reduce_min.14
  11.5 0.1 reduce_max.18
  11.8 0.1 copy.18
  12.0 0.1 copy.19
  12.3 0.6 collective-permute-done.1.right_ref
  12.8 4.3 %collective-permute-done.left_ref = bf16[64,64]{1,0:T(8,128)(2,1)S(1)} collective-permute-done((bf16[64,64]{1,0:T(8,128)(2,1)S(1)}, bf16[64,64]{1,0:T(8,128)(2,1)S(1)}, u32[]{:S(2)}, u32[]{:S(2)}) %collective-permute-start) | collective-permute-done | bytes 8224 | tf_op jit(solution)/shard_map/ppermute | solution.py:280
  17.2 0.9 %shard_map.74 = (bf16[64,128]{1,0:T(8,128)(2,1)S(1)}, bf16[64,128]{1,0:T(8,128)(2,1)S(1)}) custom-call(s32[64]{0:T(128)S(1)} %get-tuple-element.31.lo_ref, s32[64]{0:T(128)S(1)} %get-tuple-element.30.hi_ref, s32[3,64,128]{2,1,0:T(8,128)S(1)} %reshape.27.u_ref, f32[3,64,128]{2,1,0:T(8,128)S(1)} %reshape.28.wt_ref, bf16[64,4096]{1,0:T(8,128)(2,1)S(1)} %copy-done.1, ...), custom_call_target="tpu_custom_call" | custom-call | flops 268435456 | bytes 1048576 | tf_op jit(solution)/shard_map/pallas_call | solution.py:113
  18.2 5.9 %collective-permute-start.3 = (bf16[64,128]{1,0:T(8,128)(2,1)S(1)}, bf16[64,128]{1,0:T(8,128)(2,1)S(1)}, u32[]{:S(2)}, u32[]{:S(2)}) collective-permute-start(bf16[64,128]{1,0:T(8,128)(2,1)S(1)} %get-tuple-element.13), channel_id=1, source_target_pairs={{4,0},{8,4},{12,8},{16,12},{20,16},{24,20},{28,24},{32,28},{36,32}... | collective-permute-start | bytes 49160 | tf_op jit(solution)/shard_map/ppermute | solution.py:286
  24.0 5.2 %shard_map.73 = bf16[4,64,2304]{2,1,0:T(8,128)(2,1)} custom-call(s32[64]{0:T(128)S(1)} %get-tuple-element.31.lo_ref, s32[64]{0:T(128)S(1)} %get-tuple-element.30.hi_ref, s32[3,64,128]{2,1,0:T(8,128)S(1)} %reshape.27.u_ref, f32[3,64,128]{2,1,0:T(8,128)S(1)} %reshape.28.wt_ref, bf16[64,4096]{1,0:T(8,128)(2,1)S(1)} %copy-done.1, ...), custom_call_target="tpu_custom_call" | custom-call | flops 8589934592 | bytes 1048576 | tf_op jit(solution)/shard_map/pallas_call | solution.py:113
  29.3 0.6 bitcast_dynamic-update-slice_fusion.1
  29.9 0.6 bitcast_dynamic-update-slice_fusion
  30.5 3.5 %all-to-all-start = ((bf16[4,64,2304]{2,1,0:T(8,128)(2,1)}), bf16[4,64,2304]{2,1,0:T(8,128)(2,1)S(1)}, u32[]{:S(2)}, u32[]{:S(2)}) async-start(bf16[4,64,2304]{2,1,0:T(8,128)(2,1)} %bitcast_dynamic-update-slice_fusion), calls=%async_computation | async-start | bytes 2359296 | tf_op jit(solution)/shard_map/all_to_all | solution.py:293
  34.0 5.1 %collective-permute-start.7 = (bf16[10,64,256]{2,1,0:T(8,128)(2,1)S(1)}, bf16[10,64,256]{2,1,0:T(8,128)(2,1)S(1)}, u32[]{:S(2)}, u32[]{:S(2)}) collective-permute-start(bf16[10,64,256]{2,1,0:T(8,128)(2,1)S(1)} %pad_maximum_fusion.rest_0_), channel_id=1, source_target_pairs={{0,4},{4,0},{8,12},{12,8},{16,20},{20,16},{24,28},{28,24},{32,36},... | collective-permute-start | bytes 983048 | tf_op jit(solution)/shard_map/ppermute | solution.py:270
  39.2 0.4 collective-permute-start.9
  39.7 0.6 collective-permute-done.7.rest_4_
  40.3 0.6 collective-permute-done.8.rest_5_
  40.9 0.5 collective-permute-done.9.rest_6_
  41.4 0.5 collective-permute-done.10.rest_7_
  41.9 3.2 %all-to-all-done = bf16[4,64,2304]{2,1,0:T(8,128)(2,1)S(1)} async-done(((bf16[4,64,2304]{2,1,0:T(8,128)(2,1)}), bf16[4,64,2304]{2,1,0:T(8,128)(2,1)S(1)}, u32[]{:S(2)}, u32[]{:S(2)}) %all-to-all-start) | async-done | bytes 1179680 | tf_op jit(solution)/shard_map/all_to_all | solution.py:293
  45.1 9.3 %shard_map.75 = bf16[512,128]{1,0:T(8,128)(2,1)S(1)} custom-call(s32[1]{0:T(128)} %bitcast.var_ref, bf16[256,2304]{1,0:T(8,128)(2,1)S(1)} %bitcast.28, bf16[10,64,256]{2,1,0:T(8,128)(2,1)S(1)} %pad_maximum_fusion.rest_0_, bf16[10,64,256]{2,1,0:T(8,128)(2,1)S(1)} %collective-permute-done.4.rest_1_, bf16[10,64,256]{2,1,0:T(8,128)(2,1)S(1)} %collective-permute-done.5.rest_2_, ...), custom_call_target="tpu_custom_call" | custom-call | tf_op jit(solution)/shard_map/pallas_call | solution.py:209
  54.4 26.4 %all_to_all.10 = bf16[256,2,128]{2,1,0:T(2,128)(2,1)} all-to-all(bf16[256,2,128]{2,1,0:T(2,128)(2,1)S(1)} %bitcast.29), channel_id=1, replica_groups=mesh['tile'=64,'var'=4] {'var','tile'}, dimensions={0} | all-to-all | bytes 262144 | tf_op jit(solution)/shard_map/all_to_all | solution.py:296
  80.8 1.8 %shard_map.76 = f32[6,64,128]{2,1,0:T(8,128)} custom-call(bf16[512,128]{1,0:T(8,128)(2,1)} %bitcast.30), custom_call_target="tpu_custom_call" | custom-call | tf_op jit(solution)/shard_map/pallas_call | solution.py:235
  (35 shorter events, 1.6 us)
Async XLA Ops:
  0.0 3.4 %copy-start = (bf16[9,128,256]{2,1,0:T(8,128)(2,1)S(1)}, bf16[9,128,256]{2,1,0:T(8,128)(2,1)}, u32[]{:S(2)}) copy-start(bf16[9,128,256]{2,1,0:T(8,128)(2,1)} %param.10) | copy-start | bytes 1769476
  0.0 8.0 %copy-start.1 = (bf16[64,4096]{1,0:T(8,128)(2,1)S(1)}, bf16[64,4096]{1,0:T(8,128)(2,1)}, u32[]{:S(2)}) copy-start(bf16[64,4096]{1,0:T(8,128)(2,1)} %lat_ref.3) | copy-start | bytes 1572868
  0.0 11.2 %copy-start.2 = (s32[3,64,128]{2,1,0:T(8,128)S(1)}, s32[3,64,128]{2,1,0:T(8,128)}, u32[]{:S(2)}) copy-start(s32[3,64,128]{2,1,0:T(8,128)} %param.8) | copy-start | bytes 294916
  3.3 8.7 %copy-start.3 = (f32[3,64,128]{2,1,0:T(8,128)S(1)}, f32[3,64,128]{2,1,0:T(8,128)}, u32[]{:S(2)}) copy-start(f32[3,64,128]{2,1,0:T(8,128)} %param.9) | copy-start | bytes 294916
  3.5 27.0 %collective-permute-start.6 = (bf16[10,64,256]{2,1,0:T(8,128)(2,1)S(1)}, bf16[10,64,256]{2,1,0:T(8,128)(2,1)S(1)}, u32[]{:S(2)}, u32[]{:S(2)}) collective-permute-start(bf16[10,64,256]{2,1,0:T(8,128)(2,1)S(1)} %pad_maximum_fusion.rest_0_), channel_id=1, source_target_pairs={{0,3},{1,0},{2,1},{3,2},{4,7},{5,4},{6,5},{7,6},{8,11},{9,8},{10,9... | collective-permute-start | bytes 983048 | tf_op jit(solution)/shard_map/ppermute | solution.py:265
  6.8 23.6 %collective-permute-start.5 = (bf16[10,64,256]{2,1,0:T(8,128)(2,1)S(1)}, bf16[10,64,256]{2,1,0:T(8,128)(2,1)S(1)}, u32[]{:S(2)}, u32[]{:S(2)}) collective-permute-start(bf16[10,64,256]{2,1,0:T(8,128)(2,1)S(1)} %pad_maximum_fusion.rest_0_), channel_id=1, source_target_pairs={{0,2},{1,3},{2,0},{3,1},{4,6},{5,7},{6,4},{7,5},{8,10},{9,11},{10,... | collective-permute-start | bytes 983048 | tf_op jit(solution)/shard_map/ppermute | solution.py:265
  7.4 23.1 %collective-permute-start.4 = (bf16[10,64,256]{2,1,0:T(8,128)(2,1)S(1)}, bf16[10,64,256]{2,1,0:T(8,128)(2,1)S(1)}, u32[]{:S(2)}, u32[]{:S(2)}) collective-permute-start(bf16[10,64,256]{2,1,0:T(8,128)(2,1)S(1)} %pad_maximum_fusion.rest_0_), channel_id=1, source_target_pairs={{0,1},{1,2},{2,3},{3,0},{4,5},{5,6},{6,7},{7,4},{8,9},{9,10},{10,1... | collective-permute-start | bytes 983048 | tf_op jit(solution)/shard_map/ppermute | solution.py:265
  8.1 4.8 %collective-permute-start.1 = (bf16[64,64]{1,0:T(8,128)(2,1)S(1)}, bf16[64,64]{1,0:T(8,128)(2,1)S(1)}, u32[]{:S(2)}, u32[]{:S(2)}) collective-permute-start(bf16[64,64]{1,0:T(8,128)(2,1)S(1)} %get-tuple-element.21), channel_id=1, source_target_pairs={{4,0},{8,4},{12,8},{16,12},{20,16},{24,20},{28,24},{32,28},{36,32}... | collective-permute-start | bytes 24584 | tf_op jit(solution)/shard_map/ppermute | solution.py:281
  9.6 7.6 %collective-permute-start = (bf16[64,64]{1,0:T(8,128)(2,1)S(1)}, bf16[64,64]{1,0:T(8,128)(2,1)S(1)}, u32[]{:S(2)}, u32[]{:S(2)}) collective-permute-start(bf16[64,64]{1,0:T(8,128)(2,1)S(1)} %get-tuple-element.22), channel_id=1, source_target_pairs={{0,4},{4,8},{8,12},{12,16},{16,20},{20,24},{24,28},{28,32},{32,36}... | collective-permute-start | bytes 24584 | tf_op jit(solution)/shard_map/ppermute | solution.py:280
  18.1 11.2 %collective-permute-start.2 = (bf16[64,128]{1,0:T(8,128)(2,1)S(1)}, bf16[64,128]{1,0:T(8,128)(2,1)S(1)}, u32[]{:S(2)}, u32[]{:S(2)}) collective-permute-start(bf16[64,128]{1,0:T(8,128)(2,1)S(1)} %get-tuple-element.12), channel_id=1, source_target_pairs={{0,4},{4,8},{8,12},{12,16},{16,20},{20,24},{24,28},{28,32},{32,36}... | collective-permute-start | bytes 49160 | tf_op jit(solution)/shard_map/ppermute | solution.py:285
  18.2 11.7 %collective-permute-start.3 = (bf16[64,128]{1,0:T(8,128)(2,1)S(1)}, bf16[64,128]{1,0:T(8,128)(2,1)S(1)}, u32[]{:S(2)}, u32[]{:S(2)}) collective-permute-start(bf16[64,128]{1,0:T(8,128)(2,1)S(1)} %get-tuple-element.13), channel_id=1, source_target_pairs={{4,0},{8,4},{12,8},{16,12},{20,16},{24,20},{28,24},{32,28},{36,32}... | collective-permute-start | bytes 49160 | tf_op jit(solution)/shard_map/ppermute | solution.py:286
  30.5 14.7 %all-to-all-start = ((bf16[4,64,2304]{2,1,0:T(8,128)(2,1)}), bf16[4,64,2304]{2,1,0:T(8,128)(2,1)S(1)}, u32[]{:S(2)}, u32[]{:S(2)}) async-start(bf16[4,64,2304]{2,1,0:T(8,128)(2,1)} %bitcast_dynamic-update-slice_fusion), calls=%async_computation | async-start | bytes 2359296 | tf_op jit(solution)/shard_map/all_to_all | solution.py:293
  34.0 6.3 %collective-permute-start.7 = (bf16[10,64,256]{2,1,0:T(8,128)(2,1)S(1)}, bf16[10,64,256]{2,1,0:T(8,128)(2,1)S(1)}, u32[]{:S(2)}, u32[]{:S(2)}) collective-permute-start(bf16[10,64,256]{2,1,0:T(8,128)(2,1)S(1)} %pad_maximum_fusion.rest_0_), channel_id=1, source_target_pairs={{0,4},{4,0},{8,12},{12,8},{16,20},{20,16},{24,28},{28,24},{32,36},... | collective-permute-start | bytes 983048 | tf_op jit(solution)/shard_map/ppermute | solution.py:270
  39.1 1.9 %collective-permute-start.8 = (bf16[10,64,256]{2,1,0:T(8,128)(2,1)S(1)}, bf16[10,64,256]{2,1,0:T(8,128)(2,1)}, u32[]{:S(2)}, u32[]{:S(2)}) collective-permute-start(bf16[10,64,256]{2,1,0:T(8,128)(2,1)S(1)} %collective-permute-done.4.rest_1_), channel_id=1, source_target_pairs={{0,4},{4,0},{8,12},{12,8},{16,20},{20,16},{24,28},{28,24},{32,36},... | collective-permute-start | bytes 983048 | tf_op jit(solution)/shard_map/ppermute | solution.py:270
  39.2 2.2 %collective-permute-start.9 = (bf16[10,64,256]{2,1,0:T(8,128)(2,1)S(1)}, bf16[10,64,256]{2,1,0:T(8,128)(2,1)}, u32[]{:S(2)}, u32[]{:S(2)}) collective-permute-start(bf16[10,64,256]{2,1,0:T(8,128)(2,1)S(1)} %collective-permute-done.5.rest_2_), channel_id=1, source_target_pairs={{0,4},{4,0},{8,12},{12,8},{16,20},{20,16},{24,28},{28,24},{32,36},... | collective-permute-start | bytes 983048 | tf_op jit(solution)/shard_map/ppermute | solution.py:270
  39.6 2.3 %collective-permute-start.10 = (bf16[10,64,256]{2,1,0:T(8,128)(2,1)S(1)}, bf16[10,64,256]{2,1,0:T(8,128)(2,1)}, u32[]{:S(2)}, u32[]{:S(2)}) collective-permute-start(bf16[10,64,256]{2,1,0:T(8,128)(2,1)S(1)} %collective-permute-done.6.rest_3_), channel_id=1, source_target_pairs={{0,4},{4,0},{8,12},{12,8},{16,20},{20,16},{24,28},{28,24},{32,36},... | collective-permute-start | bytes 983048 | tf_op jit(solution)/shard_map/ppermute | solution.py:270

commit v3 on v2

v3 whole, which is shorter than its diff:
```python
import functools

import jax
import jax.numpy as jnp
from jax import lax
from jax.experimental import pallas as pl
from jax.experimental.pallas import tpu as pltpu
from jax.sharding import PartitionSpec as P


def prep(edge_idx, edge_weight, tile_at, mesh_dev, nmesh, rim):
    u = jnp.mod(edge_idx - tile_at * mesh_dev + rim, nmesh)
    u = u.transpose(0, 2, 1).reshape(3, -1, 128)
    wt = edge_weight.transpose(0, 2, 1).reshape(3, -1, 128)
    lo = jnp.min(u, axis=(0, 2)) // 64
    hi = jnp.max(u, axis=(0, 2)) // 64
    return u, wt, lo, hi

LIMIT = 16


def decode_kernel(part, at_ref, lo_ref, hi_ref, u_ref, wt_ref, lat_ref, near_ref, far_ref, *rest):
    even = at_ref[1] == 0
    sides = lambda near, far: (jnp.where(even, far, near), jnp.where(even, near, far))
    left, right = sides(near_ref[...], far_ref[...])
    if part == "outer":
        near_out_ref, far_out_ref, *rest = rest
        before, after = sides(near_out_ref[...], far_out_ref[...])
    outs, (lats, parts, accs) = rest[:-3], rest[-3:]
    ch, nodes = lat_ref.shape
    rim = near_ref.shape[1]
    ext = nodes + 2 * rim
    nblk = u_ref.shape[1]
    width = lats.shape[2]
    bf = lat_ref.dtype
    main = lat_ref[...]
    zeros = lambda n: jnp.zeros((ch, n), bf)
    lats[0] = jnp.concatenate([left, main, right, zeros(width - ext)], axis=1)
    lats[1] = jnp.concatenate([main, right, zeros(width - ext + rim)], axis=1)

    u0, u1, u2 = u_ref[0], u_ref[1], u_ref[2]
    w0, w1, w2 = wt_ref[0], wt_ref[1], wt_ref[2]
    w0 = w0 + jnp.where(u1 == u0, w1, 0.0) + jnp.where(u2 == u0, w2, 0.0)
    w1 = w1 + jnp.where(u2 == u1, w2, 0.0)
    for k, w in enumerate((w0, w1, w2)):
        top = w.astype(bf).astype(jnp.float32)
        parts[k] = top
        parts[3 + k] = w - top

    node = lax.broadcasted_iota(jnp.int32, (256, 128), 0).astype(jnp.float32).astype(bf)

    def window(b, at):
        src = lats[at & 1, :, pl.ds(pl.multiple_of((at >> 1) * 128, 128), 256)]
        tops = jnp.zeros((256, 128), bf)
        rests = jnp.zeros((256, 128), bf)
        for k in (2, 1, 0):
            rel = (u_ref[k, pl.ds(b, 1), :] - at * 64).astype(jnp.float32).astype(bf)
            here = node == rel
            tops = jnp.where(here, parts[k, pl.ds(b, 1), :].astype(bf), tops)
            rests = jnp.where(here, parts[3 + k, pl.ds(b, 1), :].astype(bf), rests)
        table = jnp.concatenate([tops, rests], axis=1)
        both = jnp.dot(src, table, preferred_element_type=jnp.float32)
        return both[:, :128] + both[:, 128:]

    def several(ids):
        more = jnp.int32(0)
        for j, b in enumerate(ids):
            at = lo_ref[b]
            accs[j] = window(b, at)
            more = more + jnp.where(hi_ref[b] - at >= 4, 1, 0)

        @pl.when(more > 0)
        def _():
            for j, b in enumerate(ids):
                at = lo_ref[b]

                @pl.loop(1, ((hi_ref[b] - at) >> 2) + 1)
                def _(step):
                    accs[j] += window(b, at + 4 * step)

    if part == "edges":
        several((0, nblk - 1))
        first, last = accs[0].astype(bf), accs[1].astype(bf)
        outs[0][...] = jnp.where(even, last, first)
        outs[1][...] = jnp.where(even, first, last)
        return

    per = nblk // 4
    inner = per // 2 + 1
    outer = per + 1 - inner
    for d in range(4):
        v = (at_ref[0] + d) & 3
        if part == "inner":
            several([v * per + j for j in range(inner)])
            for j in range(inner):
                outs[0][v, :, j * 128:j * 128 + 128] = accs[j].astype(bf)
            continue
        several([jnp.minimum(v * per + inner + j, nblk - 1) for j in range(outer)])
        for j in range(outer - 1):
            outs[d][:, j * 128 + 128:j * 128 + 256] = accs[j].astype(bf)
        outs[d][:, outer * 128:] = jnp.where(v == 3, after, accs[outer - 1].astype(bf))
        outs[(d + 1) % 4][:, :128] = jnp.where(v == 3, before, accs[outer - 2].astype(bf))


def decode(part, at, u, wt, lo, hi, lat, near, far, *halos):
    ch, nodes = lat.shape
    nblk = u.shape[1]
    smem = pl.BlockSpec(memory_space=pltpu.SMEM)
    vmem = pl.BlockSpec(memory_space=pltpu.VMEM)
    group = nblk // 8 + 1
    if part == "edges":
        shapes, done = (jax.ShapeDtypeStruct((ch, 128), lat.dtype),) * 2, 2
    elif part == "inner":
        shapes, done = (jax.ShapeDtypeStruct((4, ch, group * 128), lat.dtype),), nblk // 2
    else:
        shapes, done = (jax.ShapeDtypeStruct((ch, group * 128), lat.dtype),) * 4, nblk // 2
    return pl.pallas_call(
        functools.partial(decode_kernel, part),
        out_shape=shapes,
        in_specs=[smem] * 3 + [vmem] * (5 + len(halos)),
        out_specs=(vmem,) * len(shapes),
        scratch_shapes=[
            pltpu.VMEM((2, ch, nodes + 384), lat.dtype),
            pltpu.VMEM((6, nblk, 128), jnp.float32),
            pltpu.VMEM((group, ch, 128), jnp.float32),
        ],
        cost_estimate=pl.CostEstimate(flops=done * 256 * 128 * 4 * ch * 16, bytes_accessed=2 * ch * nodes * 2, transcendentals=0),
        compiler_params=pltpu.CompilerParams(vmem_limit_bytes=8 << 20),
    )(at, lo, hi, u, wt, lat, near, far, *halos)


def spread(var_at, x, parts):
    ch, cells = parts[0].shape
    lat = 64
    place = lax.broadcasted_iota(jnp.int32, (1, cells), 1) % lat
    for d, v in enumerate(parts):
        rs = pl.ds(pl.multiple_of(((var_at - d) & 3) * ch, ch), ch)
        zero = jnp.zeros_like(v)
        up = jnp.where(place == 0, zero, pltpu.roll(v, 1, 1))
        down = jnp.where(place == lat - 1, zero, pltpu.roll(v, cells - 1, 1))
        for r, u in enumerate((up, v, down)):
            x[r, rs, :] = u
            x[3 + r, rs, :] = pltpu.roll(u, cells - lat, 1)


def hidden_taps(x, weights):
    bf = x.dtype
    lat = 64
    width = x.shape[2] - 2 * lat
    last = jnp.concatenate([w[9] for w in weights], axis=0).astype(jnp.float32)
    mix = last.T[:216].astype(bf)
    bias = last[:, 216:217] + last[:, 217:218] + last[:, 218:219]
    kernel_w = jnp.concatenate(
        [jnp.concatenate([w[k] for w in weights], axis=0) for k in range(9)], axis=1)
    cols = []
    for r in range(3):
        for s in range(3):
            src, off = (3 + r, 0) if s == 1 else (r, s * lat)
            cols.append(x[src, :, off:off + width])
    pre = jnp.dot(kernel_w, jnp.concatenate(cols, axis=0), preferred_element_type=jnp.float32) + bias
    hidden = pre * (0.5 * jnp.tanh(0.5 * pre) + 0.5)
    return jnp.dot(mix, hidden.astype(bf), preferred_element_type=jnp.float32)


def inner_kernel(var_ref, inner_ref, *rest):
    weights = rest[:8]
    taps_ref, x = rest[8:]
    spread(var_ref[0], x, [inner_ref[(var_ref[0] - d) & 3] for d in range(4)])
    taps_ref[...] = hidden_taps(x, weights)


def outer_kernel(var_ref, inner_taps_ref, inner_ref, *rest):
    outer, weights = rest[:4], rest[4:12]
    out_ref, x, taps, rows, pairs = rest[12:]
    lat = 64
    cells = inner_ref.shape[2]
    inner = [inner_ref[(var_ref[0] - d) & 3] for d in range(4)]
    hid_cells = 2 * cells - 2 * lat
    out_cells = hid_cells - 2 * lat

    spread(var_ref[0], x, [
        jnp.concatenate([o[:, :128], i[:, :128], i[:, cells - 128:], o[:, 128:]], axis=1)
        for i, o in zip(inner, outer)])
    mine = hidden_taps(x, weights)
    taps[:, :128] = mine[:, :128]
    taps[:, 128:cells] = inner_taps_ref[...]
    taps[:, cells:] = mine[:, 256:]

    def total(r):
        y = [taps[(3 * r + s) * 24:(3 * r + s + 1) * 24, :] for s in range(3)]
        mid = pltpu.roll(y[1], hid_cells - lat, 1)
        return y[0][:, :out_cells] + mid[:, :out_cells] + y[2][:, 2 * lat:2 * lat + out_cells]

    spot = lax.broadcasted_iota(jnp.int32, (1, out_cells), 1) % lat
    full = jnp.where(spot == 0, 0.0, pltpu.roll(total(0), 1, 1))
    full = full + total(1)
    full = full + jnp.where(spot == lat - 1, 0.0, pltpu.roll(total(2), out_cells - 1, 1))
    shift = []
    for g in range(4):
        at = (var_ref[0] - g) & 3
        terms = jnp.zeros((16, 256), jnp.float32)
        for d in range(4):
            terms = jnp.where(at == d, weights[d][9, 0:16, :].astype(jnp.float32), terms)
        shift.append((terms[:, 219:220] + terms[:, 220:221] + terms[:, 221:222])[:6])
    full = full + jnp.concatenate(shift, axis=0)

    rows[...] = jnp.zeros_like(rows)
    for l in range(32):
        col = full[:, l * lat:(l + 1) * lat]
        for g in range(4):
            rows[pl.ds(g * 256 + l, 6, stride=32), :] = col[g * 6:g * 6 + 6]
    turned = rows[...].T
    for g in range(4):
        for h in range(2):
            pairs[pl.ds(g * 2 * lat + h, lat, stride=2), :] = turned[:, g * 256 + h * 128:g * 256 + h * 128 + 128]
    out_ref[...] = pairs[...].astype(out_ref.dtype)


def convolve_inner(var_at, inner, weights):
    _, ch, cells = inner.shape
    smem = pl.BlockSpec(memory_space=pltpu.SMEM)
    vmem = pl.BlockSpec(memory_space=pltpu.VMEM)
    return pl.pallas_call(
        inner_kernel,
        out_shape=jax.ShapeDtypeStruct((216, cells - 128), jnp.float32),
        in_specs=[smem] + [vmem] * 9,
        out_specs=vmem,
        scratch_shapes=[pltpu.VMEM((6, 4 * ch, cells), inner.dtype)],
        cost_estimate=pl.CostEstimate(flops=2 * 512 * 2304 * cells, bytes_accessed=1 << 22, transcendentals=512 * cells),
        compiler_params=pltpu.CompilerParams(vmem_limit_bytes=LIMIT << 20),
    )(var_at, inner, *weights)


def convolve_outer(var_at, inner_taps, inner, outer, weights):
    _, ch, cells = inner.shape
    smem = pl.BlockSpec(memory_space=pltpu.SMEM)
    vmem = pl.BlockSpec(memory_space=pltpu.VMEM)
    return pl.pallas_call(
        outer_kernel,
        out_shape=jax.ShapeDtypeStruct((512, 128), inner.dtype),
        in_specs=[smem] + [vmem] * 14,
        out_specs=vmem,
        scratch_shapes=[
            pltpu.VMEM((6, 4 * ch, cells + 256), inner.dtype),
            pltpu.VMEM((216, 2 * cells - 128), jnp.float32),
            pltpu.VMEM((1024, 64), jnp.float32),
            pltpu.VMEM((512, 128), jnp.float32),
        ],
        cost_estimate=pl.CostEstimate(flops=2 * 512 * 2304 * cells, bytes_accessed=1 << 22, transcendentals=512 * cells),
        compiler_params=pltpu.CompilerParams(vmem_limit_bytes=LIMIT << 20),
    )(var_at, inner_taps, inner, *outer, *weights)


def finish_kernel(got_ref, out_ref, pairs):
    pairs[...] = got_ref[...].astype(jnp.float32)
    for k in range(6):
        half, lane = k // 4, k % 4 * 32
        out_ref[k] = jnp.concatenate(
            [pairs[pl.ds(128 * v + half, 64, stride=2), :][:, lane:lane + 32] for v in range(4)], axis=1)


def finish(got):
    vmem = pl.BlockSpec(memory_space=pltpu.VMEM)
    return pl.pallas_call(
        finish_kernel,
        out_shape=jax.ShapeDtypeStruct((6, 64, 128), jnp.float32),
        in_specs=[vmem],
        out_specs=vmem,
        scratch_shapes=[pltpu.VMEM((512, 128), jnp.float32)],
    )(got)


def pack_kernel(core_ref, bias2_ref, first_ref, second_ref, bias1_ref, out_ref):
    half = first_ref.shape[1] // 2
    bf = out_ref.dtype
    at = core_ref[0]
    out_ref[:9] = first_ref[:, pl.ds(pl.multiple_of(at * half, half), half), :]
    lane = lax.broadcasted_iota(jnp.int32, (1, 2 * half), 1) % half
    bias2 = jnp.zeros((1, 2 * half), jnp.float32)
    for k in range(bias2_ref.shape[0]):
        bias2 = jnp.where(lane == k, bias2_ref[k], bias2)
    terms = []
    for value in (bias1_ref[...], bias2):
        for _ in range(3):
            term = value.astype(bf).astype(jnp.float32)
            value = value - term
            terms.append(term)
    second = [second_ref[k].astype(jnp.float32) for k in range(9)]
    columns = jnp.concatenate(second + terms + [jnp.zeros((34, 2 * half), jnp.float32)], axis=0).T
    out_ref[9] = jnp.where(at == 0, columns[:half], columns[half:]).astype(bf)


def over_var(parts):
    count = lax.axis_size("var")
    return [parts[0]] + [
        lax.ppermute(parts[d], "var", [(i, (i + d) % count) for i in range(count)]) for d in range(1, count)]


def gathered_weights(conv1_weight, conv1_bias, conv2_weight, conv2_bias):
    smem = pl.BlockSpec(memory_space=pltpu.SMEM)
    vmem = pl.BlockSpec(memory_space=pltpu.VMEM)
    taps, channels, inputs = conv1_weight.shape
    mine = pl.pallas_call(
        pack_kernel,
        out_shape=jax.ShapeDtypeStruct((taps + 1, channels // 2, inputs), conv1_weight.dtype),
        in_specs=[smem] * 2 + [vmem] * 3,
        out_specs=vmem,
    )((lax.axis_index("tile") % 2).reshape(1), conv2_bias, conv1_weight, conv2_weight, conv1_bias.reshape(1, channels))
    return over_var([mine] * 4)


def exchanged_weights(blocks):
    tiles = lax.axis_size("tile")
    return blocks + [lax.ppermute(b, "tile", [(i, i ^ 1) for i in range(tiles)]) for b in blocks]


def body(mesh_latents, edge_idx, edge_weight, conv1_weight, conv1_bias, conv2_weight, conv2_bias):
    tile_at = lax.axis_index("tile")
    tiles = lax.axis_size("tile")
    mesh_dev = mesh_latents.shape[1]
    rim = 64
    core = tile_at % 2
    near = [(i, i ^ 1) for i in range(tiles)]
    far = [(i, (i + 1 if i % 2 else i - 1) % tiles) for i in range(tiles)]
    head, tail = mesh_latents[:, :rim], mesh_latents[:, mesh_dev - rim:]
    near_halo = lax.ppermute(jnp.where(core == 0, tail, head), "tile", near)
    far_halo = lax.ppermute(jnp.where(core == 0, head, tail), "tile", far)
    blocks = gathered_weights(conv1_weight, conv1_bias, conv2_weight, conv2_bias)
    u, wt, lo, hi = prep(edge_idx, edge_weight, tile_at, mesh_dev, mesh_dev * tiles, rim)
    var_at = lax.axis_index("var").reshape(1)
    at = jnp.concatenate([var_at, core.reshape(1)])
    nodes = (at, u, wt, lo, hi, mesh_latents, near_halo, far_halo)
    to_near, to_far = decode("edges", *nodes)
    near_out = lax.ppermute(to_near, "tile", near)
    far_out = lax.ppermute(to_far, "tile", far)
    nodes, _, _ = lax.optimization_barrier((nodes, to_near, to_far))
    inner, = decode("inner", *nodes)
    inner, near_out, far_out = lax.optimization_barrier((inner, near_out, far_out))
    inner = lax.all_to_all(inner, "var", split_axis=0, concat_axis=0, tiled=True)
    outer = decode("outer", *nodes, near_out, far_out)
    outer, blocks = lax.optimization_barrier((outer, blocks))
    weights = exchanged_weights(blocks)
    outer = over_var(outer)
    inner_taps = convolve_inner(var_at, inner, weights)
    fields = convolve_outer(var_at, inner_taps, inner, outer, weights)
    got = lax.all_to_all(fields.reshape(256, 2, 128), ("var", "tile"), split_axis=0, concat_axis=0, tiled=True)
    return finish(got.reshape(512, 128)).reshape(6, 1, tiles * 128)


def solution(mesh):
    return jax.shard_map(
        body,
        mesh=mesh,
        in_specs=(
            P("var", "tile"),
            P(None, None, "tile"),
            P(None, None, "tile"),
            P(None, "var", None),
            P("var"),
            P(None, None, "var"),
            P("var"),
        ),
        out_specs=P("var", "tile", None),
        check_vma=False,
    )
```

time: 82.8 us -> 75.7 us (0.914)
  waiting for transfers between devices: 10.3 us -> 2.63 us
  blocking collectives: 26.4 us -> 21.6 us
  starting transfers between devices: 22.8 us -> 27.1 us
  Pallas kernels: 17.2 us -> 20.4 us
  other arithmetic: 1.84 us -> 0.47 us
    all_to_all x1, blocking collectives: 26.4 us -> 21.6 us  [body(): lax.all_to_all(fields.reshape(256, 2, 128), ('var', 'tile'), split_axis=0...]
    ppermute x7 -> x10, starting transfers between devices: 13.6 us -> 18.4 us  [the longest x6 9.76 us: over_var(): lax.ppermute(parts[d], 'var', [(i, (i + d) % count) for i in range(count)])]
    all_to_all x1, waiting for transfers between devices: 3.25 us -> 0.01 us  [body(): lax.all_to_all(inner, 'var', split_axis=0, concat_axis=0, tiled=True)]
    pallas_call x3 -> x6, Pallas kernels: 15.4 us -> 18.6 us  [the longest x3 7.04 us: decode(): pl.pallas_call(functools.partial(decode_kernel, part), out_shape=shapes,...]
    unnamed x8 -> x12, local copies, waits for them, and re-layouts: 0.02 us -> 2.38 us
    ppermute x7 -> x10, waiting for transfers between devices: 4.9 us -> 2.62 us  [the longest x6 2.34 us: over_var(): lax.ppermute(parts[d], 'var', [(i, (i + d) % count) for i in range(count)])]
    ppermute x4, waiting for transfers between devices: 2.18 us -> 0.01 us  [exchanged_weights(): lax.ppermute(b, 'tile', [(i, i ^ 1) for i in range(tiles)])]
    broadcast_in_dim x2 -> x0, other arithmetic: 1.5 us -> none  [bf16_terms(): terms.append(term.astype(jnp.bfloat16)[:, None])]
  transfers between devices with their start and end apart: 12 -> 15, of which waited for: 7 -> 3; matrix products, arithmetic and copies ran while one was open for 3% -> 2% of each run, Pallas kernels for 7% -> 14%
where the time goes in v3:
time: 75.7 us; the launch traced here: 75.4 us
  starting transfers between devices  27.1 us (36%)
  blocking collectives  21.6 us (29%)
  Pallas kernels  20.4 us (27%)
  local copies, waits for them, and re-layouts  3.07 us (4%)
  waiting for transfers between devices  2.63 us (3%)
    all_to_all x1, blocking collectives, body(): lax.all_to_all(fields.reshape(256, 2, 128), ('var', 'tile'), split_axis=0...  21.6 us
    ppermute x6, starting transfers between devices, over_var(): lax.ppermute(parts[d], 'var', [(i, (i + d) % count) for i in range(count)])  9.76 us
    pallas_call x3, Pallas kernels, decode(): pl.pallas_call(functools.partial(decode_kernel, part), out_shape=shapes,...  7.04 us
    pallas_call x1, Pallas kernels, convolve_outer(): pl.pallas_call(outer_kernel, out_shape=jax.ShapeDtypeStruct((512, 128), i...  6 us
    ppermute x1, starting transfers between devices, body(): near_halo = lax.ppermute(jnp.where(core == 0, tail, head), 'tile', near)  5.38 us
    ppermute x4, starting transfers between devices, exchanged_weights(): lax.ppermute(b, 'tile', [(i, i ^ 1) for i in range(tiles)])  5.23 us
    pallas_call x1, Pallas kernels, convolve_inner(): pl.pallas_call(inner_kernel, out_shape=jax.ShapeDtypeStruct((216, cells -...  3.56 us
    all_to_all x1, starting transfers between devices, body(): lax.all_to_all(inner, 'var', split_axis=0, concat_axis=0, tiled=True)  3.48 us
  transfers between devices with their start and end apart: 15, of which 3 were waited for; matrix products, arithmetic and copies ran while one was open for 2% of the time, Pallas kernels for 14%

profile of v3, /device:TPU:1, one launch (start us, length us, event | category | flops | bytes accessed | tf_op | source)
XLA Modules:
  0.0 75.4 jit_solution(5838271828845491237)
XLA Ops:
  0.0 2.0 %shard_map.76.rest_0_.rest_4_ = bf16[10,64,256]{2,1,0:T(8,128)(2,1)} custom-call(s32[1]{0:T(128)} %bitcast.1.core_ref, f32[6]{0:T(128)} %bias2_ref.1, bf16[9,128,256]{2,1,0:T(8,128)(2,1)} %first_ref.1, bf16[9,24,128]{2,1,0:T(8,128)(2,1)} %second_ref.1, f32[1,128]{1,0:T(1,128)} %bitcast.12), custom_call_target="tpu_custom_call" | custom-call | tf_op jit(solution)/shard_map/pallas_call | solution.py:303
  2.0 3.3 %collective-permute-start.6 = (bf16[10,64,256]{2,1,0:T(8,128)(2,1)}, bf16[10,64,256]{2,1,0:T(8,128)(2,1)S(1)}, u32[]{:S(2)}, u32[]{:S(2)}) collective-permute-start(bf16[10,64,256]{2,1,0:T(8,128)(2,1)} %shard_map.76.rest_0_.rest_4_), channel_id=1, source_target_pairs={{0,3},{1,0},{2,1},{3,2},{4,7},{5,4},{6,5},{7,6},{8,11},{9,8},{10,9... | collective-permute-start | bytes 983048 | tf_op jit(solution)/shard_map/ppermute | solution.py:296
  5.3 0.5 collective-permute-start.5
  5.8 0.6 collective-permute-start.4
  6.5 3.1 %collective-permute-start.1 = (bf16[64,64]{1,0:T(8,128)(2,1)S(1)}, bf16[64,64]{1,0:T(8,128)(2,1)S(1)}, u32[]{:S(2)}, u32[]{:S(2)}) collective-permute-start(bf16[64,64]{1,0:T(8,128)(2,1)S(1)} %get-tuple-element.57), channel_id=1, source_target_pairs={{0,252},{4,8},{8,4},{12,16},{16,12},{20,24},{24,20},{28,32},{32,28... | collective-permute-start | bytes 24584 | tf_op jit(solution)/shard_map/ppermute | solution.py:327
  9.6 5.4 %collective-permute-start = (bf16[64,64]{1,0:T(8,128)(2,1)S(1)}, bf16[64,64]{1,0:T(8,128)(2,1)S(1)}, u32[]{:S(2)}, u32[]{:S(2)}) collective-permute-start(bf16[64,64]{1,0:T(8,128)(2,1)S(1)} %get-tuple-element.58), channel_id=1, source_target_pairs={{0,4},{4,0},{8,12},{12,8},{16,20},{20,16},{24,28},{28,24},{32,36},... | collective-permute-start | bytes 24584 | tf_op jit(solution)/shard_map/ppermute | solution.py:326
  15.1 0.1 reduce_max.14
  15.2 0.1 reduce_min.14
  15.3 0.1 reduce_max.18
  15.4 0.1 reduce_min.18
  15.7 0.1 copy.11
  15.9 0.8 %copy-done.5 = f32[3,64,128]{2,1,0:T(8,128)S(1)} copy-done((f32[3,64,128]{2,1,0:T(8,128)S(1)}, f32[3,64,128]{2,1,0:T(8,128)}, u32[]{:S(2)}) %copy-start.5) | copy-done | bytes 98328
  16.7 0.1 copy.12
  16.9 0.9 %shard_map.73 = (bf16[64,128]{1,0:T(8,128)(2,1)S(1)}, bf16[64,128]{1,0:T(8,128)(2,1)S(1)}) custom-call(s32[2]{0:T(128)S(1)} %pad_add_fusion.at_ref, s32[64]{0:T(128)S(1)} %get-tuple-element.33.lo_ref, s32[64]{0:T(128)S(1)} %get-tuple-element.34.hi_ref, s32[3,64,128]{2,1,0:T(8,128)S(1)} %reshape.29.u_ref, f32[3,64,128]{2,1,0:T(8,128)S(1)} %reshape.30.wt_ref, ...), custom_call_target="tpu_custom_call" | custom-call | flops 268435456 | bytes 1048576 | tf_op jit(solution)/shard_map/pallas_call | solution.py:117
  18.1 3.2 %shard_map.74 = bf16[4,64,1152]{2,1,0:T(8,128)(2,1)} custom-call(s32[2]{0:T(128)S(1)} %pad_add_fusion.at_ref, s32[64]{0:T(128)S(1)} %get-tuple-element.33.lo_ref, s32[64]{0:T(128)S(1)} %get-tuple-element.34.hi_ref, s32[3,64,128]{2,1,0:T(8,128)S(1)} %reshape.29.u_ref, f32[3,64,128]{2,1,0:T(8,128)S(1)} %reshape.30.wt_ref, bf16[64,4096]{1,0:T(8,128)(2,1)S(1)} %copy-done.1, ...), custom_call_target="tpu_custom_call" | custom-call | flops 4294967296 | bytes 1048576 | tf_op jit(solution)/shard_map/pallas_call | solution.py:117
  21.2 0.3 collective-permute-done.3.rest_1_
  21.5 3.5 %all-to-all-start = ((bf16[4,64,1152]{2,1,0:T(8,128)(2,1)}), bf16[4,64,1152]{2,1,0:T(8,128)(2,1)S(1)}, u32[]{:S(2)}, u32[]{:S(2)}) async-start(bf16[4,64,1152]{2,1,0:T(8,128)(2,1)} %shard_map.74), calls=%async_computation | async-start | bytes 1179648 | tf_op jit(solution)/shard_map/all_to_all | solution.py:339
  25.0 3.0 %shard_map.75 = (bf16[64,1152]{1,0:T(8,128)(2,1)S(1)}, bf16[64,1152]{1,0:T(8,128)(2,1)}, bf16[64,1152]{1,0:T(8,128)(2,1)}, bf16[64,1152]{1,0:T(8,128)(2,1)S(1)}) custom-call(s32[2]{0:T(128)S(1)} %pad_add_fusion.at_ref, s32[64]{0:T(128)S(1)} %get-tuple-element.33.lo_ref, s32[64]{0:T(128)S(1)} %get-tuple-element.34.hi_ref, s32[3,64,128]{2,1,0:T(8,128)S(1)} %reshape.29.u_ref, ...), custom_call_target="tpu_custom_call" | custom-call | flops 4294967296 | bytes 1048576 | tf_op jit(solution)/shard_map/pallas_call | solution.py:117
  28.0 0.7 copy-done.2
  28.6 4.6 %collective-permute-start.7 = (bf16[10,64,256]{2,1,0:T(8,128)(2,1)S(1)}, bf16[10,64,256]{2,1,0:T(8,128)(2,1)S(1)}, u32[]{:S(2)}, u32[]{:S(2)}) collective-permute-start(bf16[10,64,256]{2,1,0:T(8,128)(2,1)S(1)} %copy-done), channel_id=1, source_target_pairs={{0,4},{4,0},{8,12},{12,8},{16,20},{20,16},{24,28},{28,24},{32,36},... | collective-permute-start | bytes 983048 | tf_op jit(solution)/shard_map/ppermute | solution.py:314
  33.3 0.1 collective-permute-start.8
  33.4 0.4 collective-permute-start.9
  33.8 0.1 collective-permute-start.10
  33.9 1.7 %collective-permute-start.11 = (bf16[64,1152]{1,0:T(8,128)(2,1)}, bf16[64,1152]{1,0:T(8,128)(2,1)}, u32[]{:S(2)}, u32[]{:S(2)}) collective-permute-start(bf16[64,1152]{1,0:T(8,128)(2,1)} %get-tuple-element.52), channel_id=1, source_target_pairs={{0,1},{1,2},{2,3},{3,0},{4,5},{5,6},{6,7},{7,4},{8,9},{9,10},{10,1... | collective-permute-start | bytes 442376 | tf_op jit(solution)/shard_map/ppermute | solution.py:296
  35.6 2.4 %collective-permute-start.12 = (bf16[64,1152]{1,0:T(8,128)(2,1)}, bf16[64,1152]{1,0:T(8,128)(2,1)}, u32[]{:S(2)}, u32[]{:S(2)}) collective-permute-start(bf16[64,1152]{1,0:T(8,128)(2,1)} %get-tuple-element.53), channel_id=1, source_target_pairs={{0,2},{1,3},{2,0},{3,1},{4,6},{5,7},{6,4},{7,5},{8,10},{9,11},{10,... | collective-permute-start | bytes 442376 | tf_op jit(solution)/shard_map/ppermute | solution.py:296
  38.0 1.2 %collective-permute-start.13 = (bf16[64,1152]{1,0:T(8,128)(2,1)S(1)}, bf16[64,1152]{1,0:T(8,128)(2,1)}, u32[]{:S(2)}, u32[]{:S(2)}) collective-permute-start(bf16[64,1152]{1,0:T(8,128)(2,1)S(1)} %get-tuple-element.54), channel_id=1, source_target_pairs={{0,3},{1,0},{2,1},{3,2},{4,7},{5,4},{6,5},{7,6},{8,11},{9,8},{10,9... | collective-permute-start | bytes 442376 | tf_op jit(solution)/shard_map/ppermute | solution.py:296
  39.2 3.6 %shard_map.77.inner_taps_ref = f32[216,1024]{1,0:T(8,128)S(1)} custom-call(s32[1]{0:T(128)} %bitcast.var_ref, bf16[4,64,1152]{2,1,0:T(8,128)(2,1)S(1)} %all-to-all-done.inner_ref, bf16[10,64,256]{2,1,0:T(8,128)(2,1)S(1)} %copy-done, bf16[10,64,256]{2,1,0:T(8,128)(2,1)S(1)} %collective-permute-done.4.rest_1_.rest_5_, ...), custom_call_target="tpu_custom_call" | custom-call | flops 2717908992 | bytes 4194304 | tf_op jit(solution)/shard_map/pallas_call | solution.py:223
  42.8 2.2 %collective-permute-done.12.rest_2_ = bf16[64,1152]{1,0:T(8,128)(2,1)} collective-permute-done((bf16[64,1152]{1,0:T(8,128)(2,1)}, bf16[64,1152]{1,0:T(8,128)(2,1)}, u32[]{:S(2)}, u32[]{:S(2)}) %collective-permute-start.12) | collective-permute-done | bytes 147488 | tf_op jit(solution)/shard_map/ppermute | solution.py:296
  45.1 0.9 %copy-done.3 = bf16[64,1152]{1,0:T(8,128)(2,1)S(1)} copy-done((bf16[64,1152]{1,0:T(8,128)(2,1)S(1)}, bf16[64,1152]{1,0:T(8,128)(2,1)}, u32[]{:S(2)}) %copy-start.3) | copy-done | bytes 147480
  46.0 6.0 %shard_map.78 = bf16[512,128]{1,0:T(8,128)(2,1)S(1)} custom-call(s32[1]{0:T(128)} %bitcast.var_ref, f32[216,1024]{1,0:T(8,128)S(1)} %shard_map.77.inner_taps_ref, bf16[4,64,1152]{2,1,0:T(8,128)(2,1)S(1)} %all-to-all-done.inner_ref, bf16[64,1152]{1,0:T(8,128)(2,1)S(1)} %copy-done.3, bf16[64,1152]{1,0:T(8,128)(2,1)} %collective-permute-done.11.rest_1_, ...), custom_call_target="tpu_custom_call" | custom-call | flops 2717908992 | bytes 4194304 | tf_op jit(solution)/shard_map/pallas_call | solution.py:238
  52.0 21.6 %all_to_all.10 = bf16[256,2,128]{2,1,0:T(2,128)(2,1)} all-to-all(bf16[256,2,128]{2,1,0:T(2,128)(2,1)S(1)} %bitcast.9), channel_id=1, replica_groups=mesh['tile'=64,'var'=4] {'var','tile'}, dimensions={0} | all-to-all | bytes 262144 | tf_op jit(solution)/shard_map/all_to_all | solution.py:346
  73.6 1.8 %shard_map.79 = f32[6,64,128]{2,1,0:T(8,128)} custom-call(bf16[512,128]{1,0:T(8,128)(2,1)} %bitcast.10), custom_call_target="tpu_custom_call" | custom-call | tf_op jit(solution)/shard_map/pallas_call | solution.py:264
  (30 shorter events, 0.7 us)
Async XLA Ops:
  0.0 6.4 %copy-start.1 = (bf16[64,4096]{1,0:T(8,128)(2,1)S(1)}, bf16[64,4096]{1,0:T(8,128)(2,1)}, u32[]{:S(2)}) copy-start(bf16[64,4096]{1,0:T(8,128)(2,1)} %lat_ref.3) | copy-start | bytes 1572868
  0.0 15.0 %copy-start.4 = (s32[3,64,128]{2,1,0:T(8,128)S(1)}, s32[3,64,128]{2,1,0:T(8,128)}, u32[]{:S(2)}) copy-start(s32[3,64,128]{2,1,0:T(8,128)} %param.8) | copy-start | bytes 294916
  2.0 26.6 %collective-permute-start.6 = (bf16[10,64,256]{2,1,0:T(8,128)(2,1)}, bf16[10,64,256]{2,1,0:T(8,128)(2,1)S(1)}, u32[]{:S(2)}, u32[]{:S(2)}) collective-permute-start(bf16[10,64,256]{2,1,0:T(8,128)(2,1)} %shard_map.76.rest_0_.rest_4_), channel_id=1, source_target_pairs={{0,3},{1,0},{2,1},{3,2},{4,7},{5,4},{6,5},{7,6},{8,11},{9,8},{10,9... | collective-permute-start | bytes 983048 | tf_op jit(solution)/shard_map/ppermute | solution.py:296
  5.3 23.3 %collective-permute-start.5 = (bf16[10,64,256]{2,1,0:T(8,128)(2,1)}, bf16[10,64,256]{2,1,0:T(8,128)(2,1)S(1)}, u32[]{:S(2)}, u32[]{:S(2)}) collective-permute-start(bf16[10,64,256]{2,1,0:T(8,128)(2,1)} %shard_map.76.rest_0_.rest_4_), channel_id=1, source_target_pairs={{0,2},{1,3},{2,0},{3,1},{4,6},{5,7},{6,4},{7,5},{8,10},{9,11},{10,... | collective-permute-start | bytes 983048 | tf_op jit(solution)/shard_map/ppermute | solution.py:296
  5.8 22.8 %collective-permute-start.4 = (bf16[10,64,256]{2,1,0:T(8,128)(2,1)}, bf16[10,64,256]{2,1,0:T(8,128)(2,1)S(1)}, u32[]{:S(2)}, u32[]{:S(2)}) collective-permute-start(bf16[10,64,256]{2,1,0:T(8,128)(2,1)} %shard_map.76.rest_0_.rest_4_), channel_id=1, source_target_pairs={{0,1},{1,2},{2,3},{3,0},{4,5},{5,6},{6,7},{7,4},{8,9},{9,10},{10,1... | collective-permute-start | bytes 983048 | tf_op jit(solution)/shard_map/ppermute | solution.py:296
  6.5 10.4 %collective-permute-start.1 = (bf16[64,64]{1,0:T(8,128)(2,1)S(1)}, bf16[64,64]{1,0:T(8,128)(2,1)S(1)}, u32[]{:S(2)}, u32[]{:S(2)}) collective-permute-start(bf16[64,64]{1,0:T(8,128)(2,1)S(1)} %get-tuple-element.57), channel_id=1, source_target_pairs={{0,252},{4,8},{8,4},{12,16},{16,12},{20,24},{24,20},{28,32},{32,28... | collective-permute-start | bytes 24584 | tf_op jit(solution)/shard_map/ppermute | solution.py:327
  9.6 7.3 %collective-permute-start = (bf16[64,64]{1,0:T(8,128)(2,1)S(1)}, bf16[64,64]{1,0:T(8,128)(2,1)S(1)}, u32[]{:S(2)}, u32[]{:S(2)}) collective-permute-start(bf16[64,64]{1,0:T(8,128)(2,1)S(1)} %get-tuple-element.58), channel_id=1, source_target_pairs={{0,4},{4,0},{8,12},{12,8},{16,20},{20,16},{24,28},{28,24},{32,36},... | collective-permute-start | bytes 24584 | tf_op jit(solution)/shard_map/ppermute | solution.py:326
  15.8 0.9 %copy-start.5 = (f32[3,64,128]{2,1,0:T(8,128)S(1)}, f32[3,64,128]{2,1,0:T(8,128)}, u32[]{:S(2)}) copy-start(f32[3,64,128]{2,1,0:T(8,128)} %param.9) | copy-start | bytes 294916
  17.9 3.4 %collective-permute-start.2 = (bf16[64,128]{1,0:T(8,128)(2,1)S(1)}, bf16[64,128]{1,0:T(8,128)(2,1)S(1)}, u32[]{:S(2)}, u32[]{:S(2)}) collective-permute-start(bf16[64,128]{1,0:T(8,128)(2,1)S(1)} %get-tuple-element.30), channel_id=1, source_target_pairs={{0,4},{4,0},{8,12},{12,8},{16,20},{20,16},{24,28},{28,24},{32,36},... | collective-permute-start | bytes 49160 | tf_op jit(solution)/shard_map/ppermute | solution.py:334
  18.0 3.5 %collective-permute-start.3 = (bf16[64,128]{1,0:T(8,128)(2,1)S(1)}, bf16[64,128]{1,0:T(8,128)(2,1)S(1)}, u32[]{:S(2)}, u32[]{:S(2)}) collective-permute-start(bf16[64,128]{1,0:T(8,128)(2,1)S(1)} %get-tuple-element.31), channel_id=1, source_target_pairs={{0,252},{4,8},{8,4},{12,16},{16,12},{20,24},{24,20},{28,32},{32,28... | collective-permute-start | bytes 49160 | tf_op jit(solution)/shard_map/ppermute | solution.py:335
  21.5 17.7 %all-to-all-start = ((bf16[4,64,1152]{2,1,0:T(8,128)(2,1)}), bf16[4,64,1152]{2,1,0:T(8,128)(2,1)S(1)}, u32[]{:S(2)}, u32[]{:S(2)}) async-start(bf16[4,64,1152]{2,1,0:T(8,128)(2,1)} %shard_map.74), calls=%async_computation | async-start | bytes 1179648 | tf_op jit(solution)/shard_map/all_to_all | solution.py:339
  25.0 3.6 %copy-start = (bf16[10,64,256]{2,1,0:T(8,128)(2,1)S(1)}, bf16[10,64,256]{2,1,0:T(8,128)(2,1)}, u32[]{:S(2)}) copy-start(bf16[10,64,256]{2,1,0:T(8,128)(2,1)} %shard_map.76.rest_0_.rest_4_) | copy-start | bytes 983044
  28.0 0.7 copy-start.2
  28.6 7.0 %collective-permute-start.7 = (bf16[10,64,256]{2,1,0:T(8,128)(2,1)S(1)}, bf16[10,64,256]{2,1,0:T(8,128)(2,1)S(1)}, u32[]{:S(2)}, u32[]{:S(2)}) collective-permute-start(bf16[10,64,256]{2,1,0:T(8,128)(2,1)S(1)} %copy-done), channel_id=1, source_target_pairs={{0,4},{4,0},{8,12},{12,8},{16,20},{20,16},{24,28},{28,24},{32,36},... | collective-permute-start | bytes 983048 | tf_op jit(solution)/shard_map/ppermute | solution.py:314
  33.3 4.8 %collective-permute-start.8 = (bf16[10,64,256]{2,1,0:T(8,128)(2,1)S(1)}, bf16[10,64,256]{2,1,0:T(8,128)(2,1)S(1)}, u32[]{:S(2)}, u32[]{:S(2)}) collective-permute-start(bf16[10,64,256]{2,1,0:T(8,128)(2,1)S(1)} %collective-permute-done.4.rest_1_.rest_5_), channel_id=1, source_target_pairs={{0,4},{4,0},{8,12},{12,8},{16,20},{20,16},{24,28},{28,24},{32,36},... | collective-permute-start | bytes 983048 | tf_op jit(solution)/shard_map/ppermute | solution.py:314
  33.4 5.8 %collective-permute-start.9 = (bf16[10,64,256]{2,1,0:T(8,128)(2,1)S(1)}, bf16[10,64,256]{2,1,0:T(8,128)(2,1)S(1)}, u32[]{:S(2)}, u32[]{:S(2)}) collective-permute-start(bf16[10,64,256]{2,1,0:T(8,128)(2,1)S(1)} %collective-permute-done.5.rest_2_.rest_6_), channel_id=1, source_target_pairs={{0,4},{4,0},{8,12},{12,8},{16,20},{20,16},{24,28},{28,24},{32,36},... | collective-permute-start | bytes 983048 | tf_op jit(solution)/shard_map/ppermute | solution.py:314
  33.8 5.4 %collective-permute-start.10 = (bf16[10,64,256]{2,1,0:T(8,128)(2,1)S(1)}, bf16[10,64,256]{2,1,0:T(8,128)(2,1)S(1)}, u32[]{:S(2)}, u32[]{:S(2)}) collective-permute-start(bf16[10,64,256]{2,1,0:T(8,128)(2,1)S(1)} %collective-permute-done.6.rest_3_.rest_7_), channel_id=1, source_target_pairs={{0,4},{4,0},{8,12},{12,8},{16,20},{20,16},{24,28},{28,24},{32,36},... | collective-permute-start | bytes 983048 | tf_op jit(solution)/shard_map/ppermute | solution.py:314
  33.9 8.9 %collective-permute-start.11 = (bf16[64,1152]{1,0:T(8,128)(2,1)}, bf16[64,1152]{1,0:T(8,128)(2,1)}, u32[]{:S(2)}, u32[]{:S(2)}) collective-permute-start(bf16[64,1152]{1,0:T(8,128)(2,1)} %get-tuple-element.52), channel_id=1, source_target_pairs={{0,1},{1,2},{2,3},{3,0},{4,5},{5,6},{6,7},{7,4},{8,9},{9,10},{10,1... | collective-permute-start | bytes 442376 | tf_op jit(solution)/shard_map/ppermute | solution.py:296
  35.6 9.4 %collective-permute-start.12 = (bf16[64,1152]{1,0:T(8,128)(2,1)}, bf16[64,1152]{1,0:T(8,128)(2,1)}, u32[]{:S(2)}, u32[]{:S(2)}) collective-permute-start(bf16[64,1152]{1,0:T(8,128)(2,1)} %get-tuple-element.53), channel_id=1, source_target_pairs={{0,2},{1,3},{2,0},{3,1},{4,6},{5,7},{6,4},{7,5},{8,10},{9,11},{10,... | collective-permute-start | bytes 442376 | tf_op jit(solution)/shard_map/ppermute | solution.py:296
  38.0 7.1 %collective-permute-start.13 = (bf16[64,1152]{1,0:T(8,128)(2,1)S(1)}, bf16[64,1152]{1,0:T(8,128)(2,1)}, u32[]{:S(2)}, u32[]{:S(2)}) collective-permute-start(bf16[64,1152]{1,0:T(8,128)(2,1)S(1)} %get-tuple-element.54), channel_id=1, source_target_pairs={{0,3},{1,0},{2,1},{3,2},{4,7},{5,4},{6,5},{7,6},{8,11},{9,8},{10,9... | collective-permute-start | bytes 442376 | tf_op jit(solution)/shard_map/ppermute | solution.py:296
  45.1 0.9 %copy-start.3 = (bf16[64,1152]{1,0:T(8,128)(2,1)S(1)}, bf16[64,1152]{1,0:T(8,128)(2,1)}, u32[]{:S(2)}) copy-start(bf16[64,1152]{1,0:T(8,128)(2,1)} %copy-done.2) | copy-start | bytes 442372

commit v4 on v3

--- a/solution.py
+++ b/solution.py
@@ -17,13 +17,14 @@
     return u, wt, lo, hi
 
 LIMIT = 16
+INNER = 10
 
 
 def decode_kernel(part, at_ref, lo_ref, hi_ref, u_ref, wt_ref, lat_ref, near_ref, far_ref, *rest):
     even = at_ref[1] == 0
     sides = lambda near, far: (jnp.where(even, far, near), jnp.where(even, near, far))
     left, right = sides(near_ref[...], far_ref[...])
-    if part == "outer":
+    if part in ("outer", "own"):
         near_out_ref, far_out_ref, *rest = rest
         before, after = sides(near_out_ref[...], far_out_ref[...])
     outs, (lats, parts, accs) = rest[:-3], rest[-3:]
@@ -86,20 +87,20 @@
         return
 
     per = nblk // 4
-    inner = per // 2 + 1
-    outer = per + 1 - inner
-    for d in range(4):
+    outer = per + 1 - INNER
+    for d in {"inner": range(4), "outer": range(1, 4), "own": range(1)}[part]:
         v = (at_ref[0] + d) & 3
         if part == "inner":
-            several([v * per + j for j in range(inner)])
-            for j in range(inner):
+            several([v * per + j for j in range(INNER)])
+            for j in range(INNER):
                 outs[0][v, :, j * 128:j * 128 + 128] = accs[j].astype(bf)
             continue
-        several([jnp.minimum(v * per + inner + j, nblk - 1) for j in range(outer)])
-        for j in range(outer - 1):
-            outs[d][:, j * 128 + 128:j * 128 + 256] = accs[j].astype(bf)
-        outs[d][:, outer * 128:] = jnp.where(v == 3, after, accs[outer - 1].astype(bf))
-        outs[(d + 1) % 4][:, :128] = jnp.where(v == 3, before, accs[outer - 2].astype(bf))
+        out = outs[max(d - 1, 0)]
+        several([jnp.maximum(v * per - 1, 0)] + [jnp.minimum(v * per + INNER + j, nblk - 1) for j in range(outer)])
+        out[:, :128] = jnp.where(v == 0, before, accs[0].astype(bf))
+        for j in range(1, outer):
+            out[:, j * 128:j * 128 + 128] = accs[j].astype(bf)
+        out[:, outer * 128:] = jnp.where(v == 3, after, accs[outer].astype(bf))
 
 
 def decode(part, at, u, wt, lo, hi, lat, near, far, *halos):
@@ -107,13 +108,14 @@
     nblk = u.shape[1]
     smem = pl.BlockSpec(memory_space=pltpu.SMEM)
     vmem = pl.BlockSpec(memory_space=pltpu.VMEM)
-    group = nblk // 8 + 1
+    group = INNER
     if part == "edges":
         shapes, done = (jax.ShapeDtypeStruct((ch, 128), lat.dtype),) * 2, 2
     elif part == "inner":
         shapes, done = (jax.ShapeDtypeStruct((4, ch, group * 128), lat.dtype),), nblk // 2
     else:
-        shapes, done = (jax.ShapeDtypeStruct((ch, group * 128), lat.dtype),) * 4, nblk // 2
+        count = 3 if part == "outer" else 1
+        shapes, done = (jax.ShapeDtypeStruct((ch, (nblk // 4 + 2 - group) * 128), lat.dtype),) * count, 8 * count
     return pl.pallas_call(
         functools.partial(decode_kernel, part),
         out_shape=shapes,
@@ -174,8 +176,8 @@
     out_ref, x, taps, rows, pairs = rest[12:]
     lat = 64
     cells = inner_ref.shape[2]
+    hid_cells = cells + outer[0].shape[1] - 2 * lat
     inner = [inner_ref[(var_ref[0] - d) & 3] for d in range(4)]
-    hid_cells = 2 * cells - 2 * lat
     out_cells = hid_cells - 2 * lat
 
     spread(var_ref[0], x, [
@@ -233,6 +235,7 @@
 
 def convolve_outer(var_at, inner_taps, inner, outer, weights):
     _, ch, cells = inner.shape
+    rest = outer[0].shape[1]
     smem = pl.BlockSpec(memory_space=pltpu.SMEM)
     vmem = pl.BlockSpec(memory_space=pltpu.VMEM)
     return pl.pallas_call(
@@ -241,8 +244,8 @@
         in_specs=[smem] + [vmem] * 14,
         out_specs=vmem,
         scratch_shapes=[
-            pltpu.VMEM((6, 4 * ch, cells + 256), inner.dtype),
-            pltpu.VMEM((216, 2 * cells - 128), jnp.float32),
+            pltpu.VMEM((6, 4 * ch, rest + 256), inner.dtype),
+            pltpu.VMEM((216, cells + rest - 128), jnp.float32),
             pltpu.VMEM((1024, 64), jnp.float32),
             pltpu.VMEM((512, 128), jnp.float32),
         ],
@@ -340,8 +343,10 @@
     outer = decode("outer", *nodes, near_out, far_out)
     outer, blocks = lax.optimization_barrier((outer, blocks))
     weights = exchanged_weights(blocks)
-    outer = over_var(outer)
+    outer = over_var([None] + list(outer))
     inner_taps = convolve_inner(var_at, inner, weights)
+    nodes, near_out, far_out, inner_taps = lax.optimization_barrier((nodes, near_out, far_out, inner_taps))
+    outer[0], = decode("own", *nodes, near_out, far_out)
     fields = convolve_outer(var_at, inner_taps, inner, outer, weights)
     got = lax.all_to_all(fields.reshape(256, 2, 128), ("var", "tile"), split_axis=0, concat_axis=0, tiled=True)
     return finish(got.reshape(512, 128)).reshape(6, 1, tiles * 128)

time: 75.7 us -> 73.3 us (0.968)
  Pallas kernels: 20.4 us -> 23.3 us
  waiting for transfers between devices: 2.63 us -> 0.14 us
  local copies, waits for them, and re-layouts: 3.07 us -> 1.51 us
  blocking collectives: 21.6 us -> 20.1 us
    ppermute x6, waiting for transfers between devices: 2.34 us -> 0.02 us  [over_var(): lax.ppermute(parts[d], 'var', [(i, (i + d) % count) for i in range(count)])]
    pallas_call x1, Pallas kernels: 3.56 us -> 5.41 us  [convolve_inner(): pl.pallas_call(inner_kernel, out_shape=jax.ShapeDtypeStruct((216, cells -...]
    unnamed x12 -> x8, local copies, waits for them, and re-layouts: 2.38 us -> 0.81 us
    all_to_all x1, blocking collectives: 21.6 us -> 20.1 us  [body(): lax.all_to_all(fields.reshape(256, 2, 128), ('var', 'tile'), split_axis=0...]
    pallas_call x3 -> x4, Pallas kernels: 7.04 us -> 7.94 us  [decode(): pl.pallas_call(functools.partial(decode_kernel, part), out_shape=shapes,...]
  transfers between devices with their start and end apart: 15 -> 15, of which waited for: 3 -> 1; matrix products, arithmetic and copies ran while one was open for 2% -> 2% of each run, Pallas kernels for 14% -> 18%
where the time goes in v4:
time: 73.3 us; the launch traced here: 73 us
  starting transfers between devices  27.3 us (37%)
  Pallas kernels  23.3 us (32%)
  blocking collectives  20.1 us (27%)
  local copies, waits for them, and re-layouts  1.51 us (2%)
    all_to_all x1, blocking collectives, body(): lax.all_to_all(fields.reshape(256, 2, 128), ('var', 'tile'), split_axis=0...  20.1 us
    ppermute x6, starting transfers between devices, over_var(): lax.ppermute(parts[d], 'var', [(i, (i + d) % count) for i in range(count)])  9.75 us
    pallas_call x4, Pallas kernels, decode(): pl.pallas_call(functools.partial(decode_kernel, part), out_shape=shapes,...  7.94 us
    pallas_call x1, Pallas kernels, convolve_outer(): pl.pallas_call(outer_kernel, out_shape=jax.ShapeDtypeStruct((512, 128), i...  6.16 us
    pallas_call x1, Pallas kernels, convolve_inner(): pl.pallas_call(inner_kernel, out_shape=jax.ShapeDtypeStruct((216, cells -...  5.41 us
    ppermute x4, starting transfers between devices, exchanged_weights(): lax.ppermute(b, 'tile', [(i, i ^ 1) for i in range(tiles)])  5.4 us
    ppermute x1, starting transfers between devices, body(): near_halo = lax.ppermute(jnp.where(core == 0, tail, head), 'tile', near)  5.38 us
    all_to_all x1, starting transfers between devices, body(): lax.all_to_all(inner, 'var', split_axis=0, concat_axis=0, tiled=True)  3.48 us
  transfers between devices with their start and end apart: 15, of which 1 were waited for; matrix products, arithmetic and copies ran while one was open for 2% of the time, Pallas kernels for 18%

profile of v4, /device:TPU:1, one launch (start us, length us, event | category | flops | bytes accessed | tf_op | source)
XLA Modules:
  0.0 73.0 jit_solution(2464408028187772242)
XLA Ops:
  0.0 2.0 %shard_map.76.rest_0_.rest_4_ = bf16[10,64,256]{2,1,0:T(8,128)(2,1)} custom-call(s32[1]{0:T(128)} %bitcast.1.core_ref, f32[6]{0:T(128)} %bias2_ref.1, bf16[9,128,256]{2,1,0:T(8,128)(2,1)} %first_ref.1, bf16[9,24,128]{2,1,0:T(8,128)(2,1)} %second_ref.1, f32[1,128]{1,0:T(1,128)} %bitcast.12), custom_call_target="tpu_custom_call" | custom-call | tf_op jit(solution)/shard_map/pallas_call | solution.py:306
  2.0 3.3 %collective-permute-start.6 = (bf16[10,64,256]{2,1,0:T(8,128)(2,1)}, bf16[10,64,256]{2,1,0:T(8,128)(2,1)S(1)}, u32[]{:S(2)}, u32[]{:S(2)}) collective-permute-start(bf16[10,64,256]{2,1,0:T(8,128)(2,1)} %shard_map.76.rest_0_.rest_4_), channel_id=1, source_target_pairs={{0,3},{1,0},{2,1},{3,2},{4,7},{5,4},{6,5},{7,6},{8,11},{9,8},{10,9... | collective-permute-start | bytes 983048 | tf_op jit(solution)/shard_map/ppermute | solution.py:299
  5.3 0.5 collective-permute-start.5
  5.8 0.6 collective-permute-start.4
  6.5 3.1 %collective-permute-start.1 = (bf16[64,64]{1,0:T(8,128)(2,1)S(1)}, bf16[64,64]{1,0:T(8,128)(2,1)S(1)}, u32[]{:S(2)}, u32[]{:S(2)}) collective-permute-start(bf16[64,64]{1,0:T(8,128)(2,1)S(1)} %get-tuple-element.75), channel_id=1, source_target_pairs={{0,252},{4,8},{8,4},{12,16},{16,12},{20,24},{24,20},{28,32},{32,28... | collective-permute-start | bytes 24584 | tf_op jit(solution)/shard_map/ppermute | solution.py:330
  9.6 5.4 %collective-permute-start = (bf16[64,64]{1,0:T(8,128)(2,1)S(1)}, bf16[64,64]{1,0:T(8,128)(2,1)S(1)}, u32[]{:S(2)}, u32[]{:S(2)}) collective-permute-start(bf16[64,64]{1,0:T(8,128)(2,1)S(1)} %get-tuple-element.76), channel_id=1, source_target_pairs={{0,4},{4,0},{8,12},{12,8},{16,20},{20,16},{24,28},{28,24},{32,36},... | collective-permute-start | bytes 24584 | tf_op jit(solution)/shard_map/ppermute | solution.py:329
  15.0 0.1 reduce_max.14
  15.2 0.1 reduce_min.14
  15.3 0.1 reduce_max.18
  15.4 0.1 reduce_min.18
  15.6 0.1 copy.11
  15.9 0.8 %copy-done.3 = f32[3,64,128]{2,1,0:T(8,128)S(1)} copy-done((f32[3,64,128]{2,1,0:T(8,128)S(1)}, f32[3,64,128]{2,1,0:T(8,128)}, u32[]{:S(2)}) %copy-start.3) | copy-done | bytes 98328
  16.7 0.1 copy.12
  16.9 0.9 %shard_map.73 = (bf16[64,128]{1,0:T(8,128)(2,1)S(1)}, bf16[64,128]{1,0:T(8,128)(2,1)S(1)}) custom-call(s32[2]{0:T(128)S(1)} %pad_add_fusion.at_ref, s32[64]{0:T(128)S(1)} %get-tuple-element.61.lo_ref, s32[64]{0:T(128)S(1)} %get-tuple-element.62.hi_ref, s32[3,64,128]{2,1,0:T(8,128)S(1)} %reshape.29.u_ref, f32[3,64,128]{2,1,0:T(8,128)S(1)} %reshape.30.wt_ref, ...), custom_call_target="tpu_custom_call" | custom-call | flops 268435456 | bytes 1048576 | tf_op jit(solution)/shard_map/pallas_call | solution.py:119
  17.8 0.1 collective-permute-start.2
  17.9 0.1 collective-permute-start.3
  18.0 3.3 %shard_map.74 = bf16[4,64,1280]{2,1,0:T(8,128)(2,1)} custom-call(s32[2]{0:T(128)S(1)} %pad_add_fusion.at_ref, s32[64]{0:T(128)S(1)} %get-tuple-element.61.lo_ref, s32[64]{0:T(128)S(1)} %get-tuple-element.62.hi_ref, s32[3,64,128]{2,1,0:T(8,128)S(1)} %reshape.29.u_ref, f32[3,64,128]{2,1,0:T(8,128)S(1)} %reshape.30.wt_ref, bf16[64,4096]{1,0:T(8,128)(2,1)S(1)} %copy-done.1, ...), custom_call_target="tpu_custom_call" | custom-call | flops 4294967296 | bytes 1048576 | tf_op jit(solution)/shard_map/pallas_call | solution.py:119
  21.4 0.1 collective-permute-done.3.rest_1_
  21.5 3.5 %all-to-all-start = ((bf16[4,64,1280]{2,1,0:T(8,128)(2,1)}), bf16[4,64,1280]{2,1,0:T(8,128)(2,1)S(1)}, u32[]{:S(2)}, u32[]{:S(2)}) async-start(bf16[4,64,1280]{2,1,0:T(8,128)(2,1)} %shard_map.74), calls=%async_computation | async-start | bytes 1310720 | tf_op jit(solution)/shard_map/all_to_all | solution.py:342
  25.0 2.6 %shard_map.75 = (bf16[64,1024]{1,0:T(8,128)(2,1)}, bf16[64,1024]{1,0:T(8,128)(2,1)}, bf16[64,1024]{1,0:T(8,128)(2,1)S(1)}) custom-call(s32[2]{0:T(128)S(1)} %pad_add_fusion.at_ref, s32[64]{0:T(128)S(1)} %get-tuple-element.61.lo_ref, s32[64]{0:T(128)S(1)} %get-tuple-element.62.hi_ref, s32[3,64,128]{2,1,0:T(8,128)S(1)} %reshape.29.u_ref, ...), custom_call_target="tpu_custom_call" | custom-call | flops 3221225472 | bytes 1048576 | tf_op jit(solution)/shard_map/pallas_call | solution.py:119
  27.6 4.6 %collective-permute-start.7 = (bf16[10,64,256]{2,1,0:T(8,128)(2,1)S(1)}, bf16[10,64,256]{2,1,0:T(8,128)(2,1)S(1)}, u32[]{:S(2)}, u32[]{:S(2)}) collective-permute-start(bf16[10,64,256]{2,1,0:T(8,128)(2,1)S(1)} %copy-done), channel_id=1, source_target_pairs={{0,4},{4,0},{8,12},{12,8},{16,20},{20,16},{24,28},{28,24},{32,36},... | collective-permute-start | bytes 983048 | tf_op jit(solution)/shard_map/ppermute | solution.py:317
  32.2 0.3 collective-permute-start.8
  32.5 0.2 collective-permute-start.9
  32.7 0.3 collective-permute-start.10
  33.0 1.7 %collective-permute-start.11 = (bf16[64,1024]{1,0:T(8,128)(2,1)}, bf16[64,1024]{1,0:T(8,128)(2,1)}, u32[]{:S(2)}, u32[]{:S(2)}) collective-permute-start(bf16[64,1024]{1,0:T(8,128)(2,1)} %get-tuple-element.70), channel_id=1, source_target_pairs={{0,1},{1,2},{2,3},{3,0},{4,5},{5,6},{6,7},{7,4},{8,9},{9,10},{10,1... | collective-permute-start | bytes 393224 | tf_op jit(solution)/shard_map/ppermute | solution.py:299
  34.7 2.4 %collective-permute-start.12 = (bf16[64,1024]{1,0:T(8,128)(2,1)}, bf16[64,1024]{1,0:T(8,128)(2,1)}, u32[]{:S(2)}, u32[]{:S(2)}) collective-permute-start(bf16[64,1024]{1,0:T(8,128)(2,1)} %get-tuple-element.71), channel_id=1, source_target_pairs={{0,2},{1,3},{2,0},{3,1},{4,6},{5,7},{6,4},{7,5},{8,10},{9,11},{10,... | collective-permute-start | bytes 393224 | tf_op jit(solution)/shard_map/ppermute | solution.py:299
  37.1 1.2 %collective-permute-start.13 = (bf16[64,1024]{1,0:T(8,128)(2,1)S(1)}, bf16[64,1024]{1,0:T(8,128)(2,1)}, u32[]{:S(2)}, u32[]{:S(2)}) collective-permute-start(bf16[64,1024]{1,0:T(8,128)(2,1)S(1)} %get-tuple-element.72), channel_id=1, source_target_pairs={{0,3},{1,0},{2,1},{3,2},{4,7},{5,4},{6,5},{7,6},{8,11},{9,8},{10,9... | collective-permute-start | bytes 393224 | tf_op jit(solution)/shard_map/ppermute | solution.py:299
  38.3 5.4 %shard_map.77.inner_taps_ref = f32[216,1152]{1,0:T(8,128)S(1)} custom-call(s32[1]{0:T(128)} %bitcast.var_ref, bf16[4,64,1280]{2,1,0:T(8,128)(2,1)S(1)} %all-to-all-done.inner_ref, bf16[10,64,256]{2,1,0:T(8,128)(2,1)S(1)} %copy-done, bf16[10,64,256]{2,1,0:T(8,128)(2,1)S(1)} %collective-permute-done.4.rest_1_.rest_5_, ...), custom_call_target="tpu_custom_call" | custom-call | flops 3019898880 | bytes 4194304 | tf_op jit(solution)/shard_map/pallas_call | solution.py:225
  43.7 1.1 %shard_map.78.rest_0_ = bf16[64,1024]{1,0:T(8,128)(2,1)S(1)} custom-call(s32[2]{0:T(128)S(1)} %pad_add_fusion.at_ref, s32[64]{0:T(128)S(1)} %get-tuple-element.61.lo_ref, s32[64]{0:T(128)S(1)} %get-tuple-element.62.hi_ref, s32[3,64,128]{2,1,0:T(8,128)S(1)} %reshape.29.u_ref, f32[3,64,128]{2,1,0:T(8,128)S(1)} %reshape.30.wt_ref, ...), custom_call_target="tpu_custom_call" | custom-call | flops 1073741824 | bytes 1048576 | tf_op jit(solution)/shard_map/pallas_call | solution.py:119
  44.9 6.2 %shard_map.79 = bf16[512,128]{1,0:T(8,128)(2,1)S(1)} custom-call(s32[1]{0:T(128)} %bitcast.var_ref, f32[216,1152]{1,0:T(8,128)S(1)} %shard_map.77.inner_taps_ref, bf16[4,64,1280]{2,1,0:T(8,128)(2,1)S(1)} %all-to-all-done.inner_ref, bf16[64,1024]{1,0:T(8,128)(2,1)S(1)} %shard_map.78.rest_0_, bf16[64,1024]{1,0:T(8,128)(2,1)} %collective-permute-done.11.rest_1_, ...), custom_call_target="tpu_custom_call" | custom-call | flops 3019898880 | bytes 4194304 | tf_op jit(solution)/shard_map/pallas_call | solution.py:241
  51.1 20.1 %all_to_all.10 = bf16[256,2,128]{2,1,0:T(2,128)(2,1)} all-to-all(bf16[256,2,128]{2,1,0:T(2,128)(2,1)S(1)} %bitcast.9), channel_id=1, replica_groups=mesh['tile'=64,'var'=4] {'var','tile'}, dimensions={0} | all-to-all | bytes 262144 | tf_op jit(solution)/shard_map/all_to_all | solution.py:351
  71.2 1.8 %shard_map.80 = f32[6,64,128]{2,1,0:T(8,128)} custom-call(bf16[512,128]{1,0:T(8,128)(2,1)} %bitcast.10), custom_call_target="tpu_custom_call" | custom-call | tf_op jit(solution)/shard_map/pallas_call | solution.py:267
  (27 shorter events, 0.5 us)
Async XLA Ops:
  0.0 6.4 %copy-start.1 = (bf16[64,4096]{1,0:T(8,128)(2,1)S(1)}, bf16[64,4096]{1,0:T(8,128)(2,1)}, u32[]{:S(2)}) copy-start(bf16[64,4096]{1,0:T(8,128)(2,1)} %lat_ref.4) | copy-start | bytes 1572868
  0.0 15.0 %copy-start.2 = (s32[3,64,128]{2,1,0:T(8,128)S(1)}, s32[3,64,128]{2,1,0:T(8,128)}, u32[]{:S(2)}) copy-start(s32[3,64,128]{2,1,0:T(8,128)} %param.8) | copy-start | bytes 294916
  2.0 25.6 %collective-permute-start.6 = (bf16[10,64,256]{2,1,0:T(8,128)(2,1)}, bf16[10,64,256]{2,1,0:T(8,128)(2,1)S(1)}, u32[]{:S(2)}, u32[]{:S(2)}) collective-permute-start(bf16[10,64,256]{2,1,0:T(8,128)(2,1)} %shard_map.76.rest_0_.rest_4_), channel_id=1, source_target_pairs={{0,3},{1,0},{2,1},{3,2},{4,7},{5,4},{6,5},{7,6},{8,11},{9,8},{10,9... | collective-permute-start | bytes 983048 | tf_op jit(solution)/shard_map/ppermute | solution.py:299
  5.3 22.3 %collective-permute-start.5 = (bf16[10,64,256]{2,1,0:T(8,128)(2,1)}, bf16[10,64,256]{2,1,0:T(8,128)(2,1)S(1)}, u32[]{:S(2)}, u32[]{:S(2)}) collective-permute-start(bf16[10,64,256]{2,1,0:T(8,128)(2,1)} %shard_map.76.rest_0_.rest_4_), channel_id=1, source_target_pairs={{0,2},{1,3},{2,0},{3,1},{4,6},{5,7},{6,4},{7,5},{8,10},{9,11},{10,... | collective-permute-start | bytes 983048 | tf_op jit(solution)/shard_map/ppermute | solution.py:299
  5.8 21.7 %collective-permute-start.4 = (bf16[10,64,256]{2,1,0:T(8,128)(2,1)}, bf16[10,64,256]{2,1,0:T(8,128)(2,1)S(1)}, u32[]{:S(2)}, u32[]{:S(2)}) collective-permute-start(bf16[10,64,256]{2,1,0:T(8,128)(2,1)} %shard_map.76.rest_0_.rest_4_), channel_id=1, source_target_pairs={{0,1},{1,2},{2,3},{3,0},{4,5},{5,6},{6,7},{7,4},{8,9},{9,10},{10,1... | collective-permute-start | bytes 983048 | tf_op jit(solution)/shard_map/ppermute | solution.py:299
  6.5 10.4 %collective-permute-start.1 = (bf16[64,64]{1,0:T(8,128)(2,1)S(1)}, bf16[64,64]{1,0:T(8,128)(2,1)S(1)}, u32[]{:S(2)}, u32[]{:S(2)}) collective-permute-start(bf16[64,64]{1,0:T(8,128)(2,1)S(1)} %get-tuple-element.75), channel_id=1, source_target_pairs={{0,252},{4,8},{8,4},{12,16},{16,12},{20,24},{24,20},{28,32},{32,28... | collective-permute-start | bytes 24584 | tf_op jit(solution)/shard_map/ppermute | solution.py:330
  9.6 7.3 %collective-permute-start = (bf16[64,64]{1,0:T(8,128)(2,1)S(1)}, bf16[64,64]{1,0:T(8,128)(2,1)S(1)}, u32[]{:S(2)}, u32[]{:S(2)}) collective-permute-start(bf16[64,64]{1,0:T(8,128)(2,1)S(1)} %get-tuple-element.76), channel_id=1, source_target_pairs={{0,4},{4,0},{8,12},{12,8},{16,20},{20,16},{24,28},{28,24},{32,36},... | collective-permute-start | bytes 24584 | tf_op jit(solution)/shard_map/ppermute | solution.py:329
  15.8 0.9 %copy-start.3 = (f32[3,64,128]{2,1,0:T(8,128)S(1)}, f32[3,64,128]{2,1,0:T(8,128)}, u32[]{:S(2)}) copy-start(f32[3,64,128]{2,1,0:T(8,128)} %param.9) | copy-start | bytes 294916
  17.8 3.5 %collective-permute-start.2 = (bf16[64,128]{1,0:T(8,128)(2,1)S(1)}, bf16[64,128]{1,0:T(8,128)(2,1)S(1)}, u32[]{:S(2)}, u32[]{:S(2)}) collective-permute-start(bf16[64,128]{1,0:T(8,128)(2,1)S(1)} %get-tuple-element.39), channel_id=1, source_target_pairs={{0,4},{4,0},{8,12},{12,8},{16,20},{20,16},{24,28},{28,24},{32,36},... | collective-permute-start | bytes 49160 | tf_op jit(solution)/shard_map/ppermute | solution.py:337
  17.9 3.5 %collective-permute-start.3 = (bf16[64,128]{1,0:T(8,128)(2,1)S(1)}, bf16[64,128]{1,0:T(8,128)(2,1)S(1)}, u32[]{:S(2)}, u32[]{:S(2)}) collective-permute-start(bf16[64,128]{1,0:T(8,128)(2,1)S(1)} %get-tuple-element.40), channel_id=1, source_target_pairs={{0,252},{4,8},{8,4},{12,16},{16,12},{20,24},{24,20},{28,32},{32,28... | collective-permute-start | bytes 49160 | tf_op jit(solution)/shard_map/ppermute | solution.py:338
  21.5 16.8 %all-to-all-start = ((bf16[4,64,1280]{2,1,0:T(8,128)(2,1)}), bf16[4,64,1280]{2,1,0:T(8,128)(2,1)S(1)}, u32[]{:S(2)}, u32[]{:S(2)}) async-start(bf16[4,64,1280]{2,1,0:T(8,128)(2,1)} %shard_map.74), calls=%async_computation | async-start | bytes 1310720 | tf_op jit(solution)/shard_map/all_to_all | solution.py:342
  25.0 2.6 %copy-start = (bf16[10,64,256]{2,1,0:T(8,128)(2,1)S(1)}, bf16[10,64,256]{2,1,0:T(8,128)(2,1)}, u32[]{:S(2)}) copy-start(bf16[10,64,256]{2,1,0:T(8,128)(2,1)} %shard_map.76.rest_0_.rest_4_) | copy-start | bytes 983044
  27.6 7.1 %collective-permute-start.7 = (bf16[10,64,256]{2,1,0:T(8,128)(2,1)S(1)}, bf16[10,64,256]{2,1,0:T(8,128)(2,1)S(1)}, u32[]{:S(2)}, u32[]{:S(2)}) collective-permute-start(bf16[10,64,256]{2,1,0:T(8,128)(2,1)S(1)} %copy-done), channel_id=1, source_target_pairs={{0,4},{4,0},{8,12},{12,8},{16,20},{20,16},{24,28},{28,24},{32,36},... | collective-permute-start | bytes 983048 | tf_op jit(solution)/shard_map/ppermute | solution.py:317
  32.2 4.9 %collective-permute-start.8 = (bf16[10,64,256]{2,1,0:T(8,128)(2,1)S(1)}, bf16[10,64,256]{2,1,0:T(8,128)(2,1)S(1)}, u32[]{:S(2)}, u32[]{:S(2)}) collective-permute-start(bf16[10,64,256]{2,1,0:T(8,128)(2,1)S(1)} %collective-permute-done.4.rest_1_.rest_5_), channel_id=1, source_target_pairs={{0,4},{4,0},{8,12},{12,8},{16,20},{20,16},{24,28},{28,24},{32,36},... | collective-permute-start | bytes 983048 | tf_op jit(solution)/shard_map/ppermute | solution.py:317
  32.5 5.8 %collective-permute-start.9 = (bf16[10,64,256]{2,1,0:T(8,128)(2,1)S(1)}, bf16[10,64,256]{2,1,0:T(8,128)(2,1)}, u32[]{:S(2)}, u32[]{:S(2)}) collective-permute-start(bf16[10,64,256]{2,1,0:T(8,128)(2,1)S(1)} %collective-permute-done.5.rest_2_.rest_6_), channel_id=1, source_target_pairs={{0,4},{4,0},{8,12},{12,8},{16,20},{20,16},{24,28},{28,24},{32,36},... | collective-permute-start | bytes 983048 | tf_op jit(solution)/shard_map/ppermute | solution.py:317
  32.7 5.6 %collective-permute-start.10 = (bf16[10,64,256]{2,1,0:T(8,128)(2,1)S(1)}, bf16[10,64,256]{2,1,0:T(8,128)(2,1)}, u32[]{:S(2)}, u32[]{:S(2)}) collective-permute-start(bf16[10,64,256]{2,1,0:T(8,128)(2,1)S(1)} %collective-permute-done.6.rest_3_.rest_7_), channel_id=1, source_target_pairs={{0,4},{4,0},{8,12},{12,8},{16,20},{20,16},{24,28},{28,24},{32,36},... | collective-permute-start | bytes 983048 | tf_op jit(solution)/shard_map/ppermute | solution.py:317
  33.0 11.9 %collective-permute-start.11 = (bf16[64,1024]{1,0:T(8,128)(2,1)}, bf16[64,1024]{1,0:T(8,128)(2,1)}, u32[]{:S(2)}, u32[]{:S(2)}) collective-permute-start(bf16[64,1024]{1,0:T(8,128)(2,1)} %get-tuple-element.70), channel_id=1, source_target_pairs={{0,1},{1,2},{2,3},{3,0},{4,5},{5,6},{6,7},{7,4},{8,9},{9,10},{10,1... | collective-permute-start | bytes 393224 | tf_op jit(solution)/shard_map/ppermute | solution.py:299
  34.7 10.2 %collective-permute-start.12 = (bf16[64,1024]{1,0:T(8,128)(2,1)}, bf16[64,1024]{1,0:T(8,128)(2,1)}, u32[]{:S(2)}, u32[]{:S(2)}) collective-permute-start(bf16[64,1024]{1,0:T(8,128)(2,1)} %get-tuple-element.71), channel_id=1, source_target_pairs={{0,2},{1,3},{2,0},{3,1},{4,6},{5,7},{6,4},{7,5},{8,10},{9,11},{10,... | collective-permute-start | bytes 393224 | tf_op jit(solution)/shard_map/ppermute | solution.py:299
  37.1 7.8 %collective-permute-start.13 = (bf16[64,1024]{1,0:T(8,128)(2,1)S(1)}, bf16[64,1024]{1,0:T(8,128)(2,1)}, u32[]{:S(2)}, u32[]{:S(2)}) collective-permute-start(bf16[64,1024]{1,0:T(8,128)(2,1)S(1)} %get-tuple-element.72), channel_id=1, source_target_pairs={{0,3},{1,0},{2,1},{3,2},{4,7},{5,4},{6,5},{7,6},{8,11},{9,8},{10,9... | collective-permute-start | bytes 393224 | tf_op jit(solution)/shard_map/ppermute | solution.py:299

commit v5 on v4

--- a/solution.py
+++ b/solution.py
@@ -274,10 +274,10 @@
 
 
 def pack_kernel(core_ref, bias2_ref, first_ref, second_ref, bias1_ref, out_ref):
-    half = first_ref.shape[1] // 2
+    half = first_ref.shape[1]
     bf = out_ref.dtype
     at = core_ref[0]
-    out_ref[:9] = first_ref[:, pl.ds(pl.multiple_of(at * half, half), half), :]
+    out_ref[:9] = first_ref[...]
     lane = lax.broadcasted_iota(jnp.int32, (1, 2 * half), 1) % half
     bias2 = jnp.zeros((1, 2 * half), jnp.float32)
     for k in range(bias2_ref.shape[0]):
@@ -301,13 +301,21 @@
 
 def gathered_weights(conv1_weight, conv1_bias, conv2_weight, conv2_bias):
     smem = pl.BlockSpec(memory_space=pltpu.SMEM)
-    vmem = pl.BlockSpec(memory_space=pltpu.VMEM)
     taps, channels, inputs = conv1_weight.shape
     mine = pl.pallas_call(
         pack_kernel,
         out_shape=jax.ShapeDtypeStruct((taps + 1, channels // 2, inputs), conv1_weight.dtype),
-        in_specs=[smem] * 2 + [vmem] * 3,
-        out_specs=vmem,
+        grid_spec=pltpu.PrefetchScalarGridSpec(
+            num_scalar_prefetch=1,
+            grid=(1,),
+            in_specs=[
+                smem,
+                pl.BlockSpec((taps, channels // 2, inputs), lambda i, core: (0, core[0], 0)),
+                pl.BlockSpec(conv2_weight.shape, lambda i, core: (0, 0, 0)),
+                pl.BlockSpec((1, channels), lambda i, core: (0, 0)),
+            ],
+            out_specs=pl.BlockSpec((taps + 1, channels // 2, inputs), lambda i, core: (0, 0, 0)),
+        ),
     )((lax.axis_index("tile") % 2).reshape(1), conv2_bias, conv1_weight, conv2_weight, conv1_bias.reshape(1, channels))
     return over_var([mine] * 4)
 

time: 73.3 us -> 73.2 us (level)
  no operation moved by 1% of the time
where the time goes in v5:
time: 73.2 us; the launch traced here: 72.9 us
  starting transfers between devices  27.3 us (37%)
  Pallas kernels  23.2 us (32%)
  blocking collectives  20.1 us (27%)
  local copies, waits for them, and re-layouts  1.51 us (2%)
    all_to_all x1, blocking collectives, body(): lax.all_to_all(fields.reshape(256, 2, 128), ('var', 'tile'), split_axis=0...  20.1 us
    ppermute x6, starting transfers between devices, over_var(): lax.ppermute(parts[d], 'var', [(i, (i + d) % count) for i in range(count)])  9.75 us
    pallas_call x4, Pallas kernels, decode(): pl.pallas_call(functools.partial(decode_kernel, part), out_shape=shapes,...  7.94 us
    pallas_call x1, Pallas kernels, convolve_outer(): pl.pallas_call(outer_kernel, out_shape=jax.ShapeDtypeStruct((512, 128), i...  6.16 us
    pallas_call x1, Pallas kernels, convolve_inner(): pl.pallas_call(inner_kernel, out_shape=jax.ShapeDtypeStruct((216, cells -...  5.41 us
    ppermute x4, starting transfers between devices, exchanged_weights(): lax.ppermute(b, 'tile', [(i, i ^ 1) for i in range(tiles)])  5.4 us
    ppermute x1, starting transfers between devices, body(): near_halo = lax.ppermute(jnp.where(core == 0, tail, head), 'tile', near)  5.38 us
    all_to_all x1, starting transfers between devices, body(): lax.all_to_all(inner, 'var', split_axis=0, concat_axis=0, tiled=True)  3.48 us
  transfers between devices with their start and end apart: 15, of which 1 were waited for; matrix products, arithmetic and copies ran while one was open for 2% of the time, Pallas kernels for 18%

profile of v5, /device:TPU:1, one launch (start us, length us, event | category | flops | bytes accessed | tf_op | source)
XLA Modules:
  0.0 72.9 jit_solution(12246572996511941223)
XLA Ops:
  0.0 1.9 %shard_map.76.rest_0_.rest_4_ = bf16[10,64,256]{2,1,0:T(8,128)(2,1)} custom-call(s32[1]{0:T(128)} %bitcast.1.core_ref, f32[6]{0:T(128)} %bias2_ref.1, bf16[9,128,256]{2,1,0:T(8,128)(2,1)} %first_ref.1, bf16[9,24,128]{2,1,0:T(8,128)(2,1)} %second_ref.1, f32[1,128]{1,0:T(1,128)} %bitcast.12), custom_call_target="tpu_custom_call" | custom-call | tf_op jit(solution)/shard_map/pallas_call | solution.py:305
  1.9 3.3 %collective-permute-start.6 = (bf16[10,64,256]{2,1,0:T(8,128)(2,1)}, bf16[10,64,256]{2,1,0:T(8,128)(2,1)S(1)}, u32[]{:S(2)}, u32[]{:S(2)}) collective-permute-start(bf16[10,64,256]{2,1,0:T(8,128)(2,1)} %shard_map.76.rest_0_.rest_4_), channel_id=1, source_target_pairs={{0,3},{1,0},{2,1},{3,2},{4,7},{5,4},{6,5},{7,6},{8,11},{9,8},{10,9... | collective-permute-start | bytes 983048 | tf_op jit(solution)/shard_map/ppermute | solution.py:299
  5.2 0.5 collective-permute-start.5
  5.7 0.6 collective-permute-start.4
  6.4 3.1 %collective-permute-start.1 = (bf16[64,64]{1,0:T(8,128)(2,1)S(1)}, bf16[64,64]{1,0:T(8,128)(2,1)S(1)}, u32[]{:S(2)}, u32[]{:S(2)}) collective-permute-start(bf16[64,64]{1,0:T(8,128)(2,1)S(1)} %get-tuple-element.75), channel_id=1, source_target_pairs={{0,252},{4,8},{8,4},{12,16},{16,12},{20,24},{24,20},{28,32},{32,28... | collective-permute-start | bytes 24584 | tf_op jit(solution)/shard_map/ppermute | solution.py:338
  9.4 5.4 %collective-permute-start = (bf16[64,64]{1,0:T(8,128)(2,1)S(1)}, bf16[64,64]{1,0:T(8,128)(2,1)S(1)}, u32[]{:S(2)}, u32[]{:S(2)}) collective-permute-start(bf16[64,64]{1,0:T(8,128)(2,1)S(1)} %get-tuple-element.76), channel_id=1, source_target_pairs={{0,4},{4,0},{8,12},{12,8},{16,20},{20,16},{24,28},{28,24},{32,36},... | collective-permute-start | bytes 24584 | tf_op jit(solution)/shard_map/ppermute | solution.py:337
  14.9 0.1 reduce_max.14
  15.0 0.1 reduce_min.14
  15.2 0.1 reduce_max.18
  15.3 0.1 reduce_min.18
  15.5 0.1 copy.11
  15.7 0.8 %copy-done.3 = f32[3,64,128]{2,1,0:T(8,128)S(1)} copy-done((f32[3,64,128]{2,1,0:T(8,128)S(1)}, f32[3,64,128]{2,1,0:T(8,128)}, u32[]{:S(2)}) %copy-start.3) | copy-done | bytes 98328
  16.5 0.1 copy.12
  16.8 0.9 %shard_map.73 = (bf16[64,128]{1,0:T(8,128)(2,1)S(1)}, bf16[64,128]{1,0:T(8,128)(2,1)S(1)}) custom-call(s32[2]{0:T(128)S(1)} %pad_add_fusion.at_ref, s32[64]{0:T(128)S(1)} %get-tuple-element.61.lo_ref, s32[64]{0:T(128)S(1)} %get-tuple-element.62.hi_ref, s32[3,64,128]{2,1,0:T(8,128)S(1)} %reshape.29.u_ref, f32[3,64,128]{2,1,0:T(8,128)S(1)} %reshape.30.wt_ref, ...), custom_call_target="tpu_custom_call" | custom-call | flops 268435456 | bytes 1048576 | tf_op jit(solution)/shard_map/pallas_call | solution.py:119
  17.7 0.1 collective-permute-start.2
  17.8 0.1 collective-permute-start.3
  17.9 3.3 %shard_map.74 = bf16[4,64,1280]{2,1,0:T(8,128)(2,1)} custom-call(s32[2]{0:T(128)S(1)} %pad_add_fusion.at_ref, s32[64]{0:T(128)S(1)} %get-tuple-element.61.lo_ref, s32[64]{0:T(128)S(1)} %get-tuple-element.62.hi_ref, s32[3,64,128]{2,1,0:T(8,128)S(1)} %reshape.29.u_ref, f32[3,64,128]{2,1,0:T(8,128)S(1)} %reshape.30.wt_ref, bf16[64,4096]{1,0:T(8,128)(2,1)S(1)} %copy-done.1, ...), custom_call_target="tpu_custom_call" | custom-call | flops 4294967296 | bytes 1048576 | tf_op jit(solution)/shard_map/pallas_call | solution.py:119
  21.3 0.1 collective-permute-done.3.rest_1_
  21.4 3.5 %all-to-all-start = ((bf16[4,64,1280]{2,1,0:T(8,128)(2,1)}), bf16[4,64,1280]{2,1,0:T(8,128)(2,1)S(1)}, u32[]{:S(2)}, u32[]{:S(2)}) async-start(bf16[4,64,1280]{2,1,0:T(8,128)(2,1)} %shard_map.74), calls=%async_computation | async-start | bytes 1310720 | tf_op jit(solution)/shard_map/all_to_all | solution.py:350
  24.9 2.6 %shard_map.75 = (bf16[64,1024]{1,0:T(8,128)(2,1)}, bf16[64,1024]{1,0:T(8,128)(2,1)}, bf16[64,1024]{1,0:T(8,128)(2,1)S(1)}) custom-call(s32[2]{0:T(128)S(1)} %pad_add_fusion.at_ref, s32[64]{0:T(128)S(1)} %get-tuple-element.61.lo_ref, s32[64]{0:T(128)S(1)} %get-tuple-element.62.hi_ref, s32[3,64,128]{2,1,0:T(8,128)S(1)} %reshape.29.u_ref, ...), custom_call_target="tpu_custom_call" | custom-call | flops 3221225472 | bytes 1048576 | tf_op jit(solution)/shard_map/pallas_call | solution.py:119
  27.4 4.6 %collective-permute-start.7 = (bf16[10,64,256]{2,1,0:T(8,128)(2,1)S(1)}, bf16[10,64,256]{2,1,0:T(8,128)(2,1)S(1)}, u32[]{:S(2)}, u32[]{:S(2)}) collective-permute-start(bf16[10,64,256]{2,1,0:T(8,128)(2,1)S(1)} %copy-done), channel_id=1, source_target_pairs={{0,4},{4,0},{8,12},{12,8},{16,20},{20,16},{24,28},{28,24},{32,36},... | collective-permute-start | bytes 983048 | tf_op jit(solution)/shard_map/ppermute | solution.py:325
  32.1 0.3 collective-permute-start.8
  32.3 0.2 collective-permute-start.9
  32.6 0.3 collective-permute-start.10
  32.8 1.7 %collective-permute-start.11 = (bf16[64,1024]{1,0:T(8,128)(2,1)}, bf16[64,1024]{1,0:T(8,128)(2,1)}, u32[]{:S(2)}, u32[]{:S(2)}) collective-permute-start(bf16[64,1024]{1,0:T(8,128)(2,1)} %get-tuple-element.70), channel_id=1, source_target_pairs={{0,1},{1,2},{2,3},{3,0},{4,5},{5,6},{6,7},{7,4},{8,9},{9,10},{10,1... | collective-permute-start | bytes 393224 | tf_op jit(solution)/shard_map/ppermute | solution.py:299
  34.6 2.4 %collective-permute-start.12 = (bf16[64,1024]{1,0:T(8,128)(2,1)}, bf16[64,1024]{1,0:T(8,128)(2,1)}, u32[]{:S(2)}, u32[]{:S(2)}) collective-permute-start(bf16[64,1024]{1,0:T(8,128)(2,1)} %get-tuple-element.71), channel_id=1, source_target_pairs={{0,2},{1,3},{2,0},{3,1},{4,6},{5,7},{6,4},{7,5},{8,10},{9,11},{10,... | collective-permute-start | bytes 393224 | tf_op jit(solution)/shard_map/ppermute | solution.py:299
  37.0 1.2 %collective-permute-start.13 = (bf16[64,1024]{1,0:T(8,128)(2,1)S(1)}, bf16[64,1024]{1,0:T(8,128)(2,1)}, u32[]{:S(2)}, u32[]{:S(2)}) collective-permute-start(bf16[64,1024]{1,0:T(8,128)(2,1)S(1)} %get-tuple-element.72), channel_id=1, source_target_pairs={{0,3},{1,0},{2,1},{3,2},{4,7},{5,4},{6,5},{7,6},{8,11},{9,8},{10,9... | collective-permute-start | bytes 393224 | tf_op jit(solution)/shard_map/ppermute | solution.py:299
  38.2 5.4 %shard_map.77.inner_taps_ref = f32[216,1152]{1,0:T(8,128)S(1)} custom-call(s32[1]{0:T(128)} %bitcast.var_ref, bf16[4,64,1280]{2,1,0:T(8,128)(2,1)S(1)} %all-to-all-done.inner_ref, bf16[10,64,256]{2,1,0:T(8,128)(2,1)S(1)} %copy-done, bf16[10,64,256]{2,1,0:T(8,128)(2,1)S(1)} %collective-permute-done.4.rest_1_.rest_5_, ...), custom_call_target="tpu_custom_call" | custom-call | flops 3019898880 | bytes 4194304 | tf_op jit(solution)/shard_map/pallas_call | solution.py:225
  43.6 1.1 %shard_map.78.rest_0_ = bf16[64,1024]{1,0:T(8,128)(2,1)S(1)} custom-call(s32[2]{0:T(128)S(1)} %pad_add_fusion.at_ref, s32[64]{0:T(128)S(1)} %get-tuple-element.61.lo_ref, s32[64]{0:T(128)S(1)} %get-tuple-element.62.hi_ref, s32[3,64,128]{2,1,0:T(8,128)S(1)} %reshape.29.u_ref, f32[3,64,128]{2,1,0:T(8,128)S(1)} %reshape.30.wt_ref, ...), custom_call_target="tpu_custom_call" | custom-call | flops 1073741824 | bytes 1048576 | tf_op jit(solution)/shard_map/pallas_call | solution.py:119
  44.8 6.2 %shard_map.79 = bf16[512,128]{1,0:T(8,128)(2,1)S(1)} custom-call(s32[1]{0:T(128)} %bitcast.var_ref, f32[216,1152]{1,0:T(8,128)S(1)} %shard_map.77.inner_taps_ref, bf16[4,64,1280]{2,1,0:T(8,128)(2,1)S(1)} %all-to-all-done.inner_ref, bf16[64,1024]{1,0:T(8,128)(2,1)S(1)} %shard_map.78.rest_0_, bf16[64,1024]{1,0:T(8,128)(2,1)} %collective-permute-done.11.rest_1_, ...), custom_call_target="tpu_custom_call" | custom-call | flops 3019898880 | bytes 4194304 | tf_op jit(solution)/shard_map/pallas_call | solution.py:241
  50.9 20.1 %all_to_all.10 = bf16[256,2,128]{2,1,0:T(2,128)(2,1)} all-to-all(bf16[256,2,128]{2,1,0:T(2,128)(2,1)S(1)} %bitcast.9), channel_id=1, replica_groups=mesh['tile'=64,'var'=4] {'var','tile'}, dimensions={0} | all-to-all | bytes 262144 | tf_op jit(solution)/shard_map/all_to_all | solution.py:359
  71.1 1.8 %shard_map.80 = f32[6,64,128]{2,1,0:T(8,128)} custom-call(bf16[512,128]{1,0:T(8,128)(2,1)} %bitcast.10), custom_call_target="tpu_custom_call" | custom-call | tf_op jit(solution)/shard_map/pallas_call | solution.py:267
  (27 shorter events, 0.5 us)
Async XLA Ops:
  0.0 6.3 %copy-start.1 = (bf16[64,4096]{1,0:T(8,128)(2,1)S(1)}, bf16[64,4096]{1,0:T(8,128)(2,1)}, u32[]{:S(2)}) copy-start(bf16[64,4096]{1,0:T(8,128)(2,1)} %lat_ref.4) | copy-start | bytes 1572868
  0.0 14.8 %copy-start.2 = (s32[3,64,128]{2,1,0:T(8,128)S(1)}, s32[3,64,128]{2,1,0:T(8,128)}, u32[]{:S(2)}) copy-start(s32[3,64,128]{2,1,0:T(8,128)} %param.8) | copy-start | bytes 294916
  1.9 25.6 %collective-permute-start.6 = (bf16[10,64,256]{2,1,0:T(8,128)(2,1)}, bf16[10,64,256]{2,1,0:T(8,128)(2,1)S(1)}, u32[]{:S(2)}, u32[]{:S(2)}) collective-permute-start(bf16[10,64,256]{2,1,0:T(8,128)(2,1)} %shard_map.76.rest_0_.rest_4_), channel_id=1, source_target_pairs={{0,3},{1,0},{2,1},{3,2},{4,7},{5,4},{6,5},{7,6},{8,11},{9,8},{10,9... | collective-permute-start | bytes 983048 | tf_op jit(solution)/shard_map/ppermute | solution.py:299
  5.2 22.3 %collective-permute-start.5 = (bf16[10,64,256]{2,1,0:T(8,128)(2,1)}, bf16[10,64,256]{2,1,0:T(8,128)(2,1)S(1)}, u32[]{:S(2)}, u32[]{:S(2)}) collective-permute-start(bf16[10,64,256]{2,1,0:T(8,128)(2,1)} %shard_map.76.rest_0_.rest_4_), channel_id=1, source_target_pairs={{0,2},{1,3},{2,0},{3,1},{4,6},{5,7},{6,4},{7,5},{8,10},{9,11},{10,... | collective-permute-start | bytes 983048 | tf_op jit(solution)/shard_map/ppermute | solution.py:299
  5.7 21.7 %collective-permute-start.4 = (bf16[10,64,256]{2,1,0:T(8,128)(2,1)}, bf16[10,64,256]{2,1,0:T(8,128)(2,1)S(1)}, u32[]{:S(2)}, u32[]{:S(2)}) collective-permute-start(bf16[10,64,256]{2,1,0:T(8,128)(2,1)} %shard_map.76.rest_0_.rest_4_), channel_id=1, source_target_pairs={{0,1},{1,2},{2,3},{3,0},{4,5},{5,6},{6,7},{7,4},{8,9},{9,10},{10,1... | collective-permute-start | bytes 983048 | tf_op jit(solution)/shard_map/ppermute | solution.py:299
  6.4 10.4 %collective-permute-start.1 = (bf16[64,64]{1,0:T(8,128)(2,1)S(1)}, bf16[64,64]{1,0:T(8,128)(2,1)S(1)}, u32[]{:S(2)}, u32[]{:S(2)}) collective-permute-start(bf16[64,64]{1,0:T(8,128)(2,1)S(1)} %get-tuple-element.75), channel_id=1, source_target_pairs={{0,252},{4,8},{8,4},{12,16},{16,12},{20,24},{24,20},{28,32},{32,28... | collective-permute-start | bytes 24584 | tf_op jit(solution)/shard_map/ppermute | solution.py:338
  9.4 7.3 %collective-permute-start = (bf16[64,64]{1,0:T(8,128)(2,1)S(1)}, bf16[64,64]{1,0:T(8,128)(2,1)S(1)}, u32[]{:S(2)}, u32[]{:S(2)}) collective-permute-start(bf16[64,64]{1,0:T(8,128)(2,1)S(1)} %get-tuple-element.76), channel_id=1, source_target_pairs={{0,4},{4,0},{8,12},{12,8},{16,20},{20,16},{24,28},{28,24},{32,36},... | collective-permute-start | bytes 24584 | tf_op jit(solution)/shard_map/ppermute | solution.py:337
  15.6 0.9 %copy-start.3 = (f32[3,64,128]{2,1,0:T(8,128)S(1)}, f32[3,64,128]{2,1,0:T(8,128)}, u32[]{:S(2)}) copy-start(f32[3,64,128]{2,1,0:T(8,128)} %param.9) | copy-start | bytes 294916
  17.7 3.5 %collective-permute-start.2 = (bf16[64,128]{1,0:T(8,128)(2,1)S(1)}, bf16[64,128]{1,0:T(8,128)(2,1)S(1)}, u32[]{:S(2)}, u32[]{:S(2)}) collective-permute-start(bf16[64,128]{1,0:T(8,128)(2,1)S(1)} %get-tuple-element.39), channel_id=1, source_target_pairs={{0,4},{4,0},{8,12},{12,8},{16,20},{20,16},{24,28},{28,24},{32,36},... | collective-permute-start | bytes 49160 | tf_op jit(solution)/shard_map/ppermute | solution.py:345
  17.8 3.5 %collective-permute-start.3 = (bf16[64,128]{1,0:T(8,128)(2,1)S(1)}, bf16[64,128]{1,0:T(8,128)(2,1)S(1)}, u32[]{:S(2)}, u32[]{:S(2)}) collective-permute-start(bf16[64,128]{1,0:T(8,128)(2,1)S(1)} %get-tuple-element.40), channel_id=1, source_target_pairs={{0,252},{4,8},{8,4},{12,16},{16,12},{20,24},{24,20},{28,32},{32,28... | collective-permute-start | bytes 49160 | tf_op jit(solution)/shard_map/ppermute | solution.py:346
  21.4 16.8 %all-to-all-start = ((bf16[4,64,1280]{2,1,0:T(8,128)(2,1)}), bf16[4,64,1280]{2,1,0:T(8,128)(2,1)S(1)}, u32[]{:S(2)}, u32[]{:S(2)}) async-start(bf16[4,64,1280]{2,1,0:T(8,128)(2,1)} %shard_map.74), calls=%async_computation | async-start | bytes 1310720 | tf_op jit(solution)/shard_map/all_to_all | solution.py:350
  24.9 2.6 %copy-start = (bf16[10,64,256]{2,1,0:T(8,128)(2,1)S(1)}, bf16[10,64,256]{2,1,0:T(8,128)(2,1)}, u32[]{:S(2)}) copy-start(bf16[10,64,256]{2,1,0:T(8,128)(2,1)} %shard_map.76.rest_0_.rest_4_) | copy-start | bytes 983044
  27.4 7.1 %collective-permute-start.7 = (bf16[10,64,256]{2,1,0:T(8,128)(2,1)S(1)}, bf16[10,64,256]{2,1,0:T(8,128)(2,1)S(1)}, u32[]{:S(2)}, u32[]{:S(2)}) collective-permute-start(bf16[10,64,256]{2,1,0:T(8,128)(2,1)S(1)} %copy-done), channel_id=1, source_target_pairs={{0,4},{4,0},{8,12},{12,8},{16,20},{20,16},{24,28},{28,24},{32,36},... | collective-permute-start | bytes 983048 | tf_op jit(solution)/shard_map/ppermute | solution.py:325
  32.1 4.9 %collective-permute-start.8 = (bf16[10,64,256]{2,1,0:T(8,128)(2,1)S(1)}, bf16[10,64,256]{2,1,0:T(8,128)(2,1)S(1)}, u32[]{:S(2)}, u32[]{:S(2)}) collective-permute-start(bf16[10,64,256]{2,1,0:T(8,128)(2,1)S(1)} %collective-permute-done.4.rest_1_.rest_5_), channel_id=1, source_target_pairs={{0,4},{4,0},{8,12},{12,8},{16,20},{20,16},{24,28},{28,24},{32,36},... | collective-permute-start | bytes 983048 | tf_op jit(solution)/shard_map/ppermute | solution.py:325
  32.3 5.8 %collective-permute-start.9 = (bf16[10,64,256]{2,1,0:T(8,128)(2,1)S(1)}, bf16[10,64,256]{2,1,0:T(8,128)(2,1)}, u32[]{:S(2)}, u32[]{:S(2)}) collective-permute-start(bf16[10,64,256]{2,1,0:T(8,128)(2,1)S(1)} %collective-permute-done.5.rest_2_.rest_6_), channel_id=1, source_target_pairs={{0,4},{4,0},{8,12},{12,8},{16,20},{20,16},{24,28},{28,24},{32,36},... | collective-permute-start | bytes 983048 | tf_op jit(solution)/shard_map/ppermute | solution.py:325
  32.6 5.6 %collective-permute-start.10 = (bf16[10,64,256]{2,1,0:T(8,128)(2,1)S(1)}, bf16[10,64,256]{2,1,0:T(8,128)(2,1)}, u32[]{:S(2)}, u32[]{:S(2)}) collective-permute-start(bf16[10,64,256]{2,1,0:T(8,128)(2,1)S(1)} %collective-permute-done.6.rest_3_.rest_7_), channel_id=1, source_target_pairs={{0,4},{4,0},{8,12},{12,8},{16,20},{20,16},{24,28},{28,24},{32,36},... | collective-permute-start | bytes 983048 | tf_op jit(solution)/shard_map/ppermute | solution.py:325
  32.8 11.9 %collective-permute-start.11 = (bf16[64,1024]{1,0:T(8,128)(2,1)}, bf16[64,1024]{1,0:T(8,128)(2,1)}, u32[]{:S(2)}, u32[]{:S(2)}) collective-permute-start(bf16[64,1024]{1,0:T(8,128)(2,1)} %get-tuple-element.70), channel_id=1, source_target_pairs={{0,1},{1,2},{2,3},{3,0},{4,5},{5,6},{6,7},{7,4},{8,9},{9,10},{10,1... | collective-permute-start | bytes 393224 | tf_op jit(solution)/shard_map/ppermute | solution.py:299
  34.6 10.2 %collective-permute-start.12 = (bf16[64,1024]{1,0:T(8,128)(2,1)}, bf16[64,1024]{1,0:T(8,128)(2,1)}, u32[]{:S(2)}, u32[]{:S(2)}) collective-permute-start(bf16[64,1024]{1,0:T(8,128)(2,1)} %get-tuple-element.71), channel_id=1, source_target_pairs={{0,2},{1,3},{2,0},{3,1},{4,6},{5,7},{6,4},{7,5},{8,10},{9,11},{10,... | collective-permute-start | bytes 393224 | tf_op jit(solution)/shard_map/ppermute | solution.py:299
  37.0 7.8 %collective-permute-start.13 = (bf16[64,1024]{1,0:T(8,128)(2,1)S(1)}, bf16[64,1024]{1,0:T(8,128)(2,1)}, u32[]{:S(2)}, u32[]{:S(2)}) collective-permute-start(bf16[64,1024]{1,0:T(8,128)(2,1)S(1)} %get-tuple-element.72), channel_id=1, source_target_pairs={{0,3},{1,0},{2,1},{3,2},{4,7},{5,4},{6,5},{7,6},{8,11},{9,8},{10,9... | collective-permute-start | bytes 393224 | tf_op jit(solution)/shard_map/ppermute | solution.py:299
